TPU v7x, 128 devices: a whole 4x4x4 slice. The times are simulated.
128 devices in a mesh: gx: 4 (over y), gy: 4 (over x), gz: 8 (over z, core).
Axes of the slice: x: 4, y: 4, z: 4, core: 2. Of those that a mesh axis runs over, the one named last changes fastest.
Arguments:
- right_side: float32 [128, 128, 1024], P('gx', 'gy', 'gz'), may hold values from -30 to 30
- screening: float32 [128, 128, 1024], P('gx', 'gy', 'gz'), may hold values from 0.002 to 0.05
- coarse_inverse: float32 [512, 512], P(('gx', 'gy', 'gz')), may hold values from -1 to 1
Outputs:
- solution_field: float32 [128, 128, 1024], P('gx', 'gy', 'gz')
- residual_norms: float32 [2], replicated
All inputs are finite; a program needn't handle non-finite values.
Results may differ from a plain program's by a relative error of at most 0.00011.
Values sent between devices are 32-bit elements; how exact they have to be, the bound alone decides.
No kernel may reach another device: no remote copies, remote signals or barrier semaphores. Data moves between devices by JAX's collectives and lax.ppermute only.
A program may use at most 192 MiB of HBM per device.

v0:
```python
import jax
import jax.numpy as jnp
from jax import lax
from jax.sharding import PartitionSpec as P

LEVELS = 5
CYCLES = 2


def with_halo(shard, sides, width):
    for axis, dim in sides:
        count, length = (lax.axis_size(axis), shard.shape[dim])
        up = [(i, (i + 1) % count) for i in range(count)]
        down = [(j, i) for i, j in up]
        last = lax.slice_in_dim(shard, length - width, length, axis=dim)
        initial = lax.slice_in_dim(shard, 0, width, axis=dim)
        before = lax.ppermute(last, axis, up)
        after = lax.ppermute(initial, axis, down)
        shard = jnp.concatenate([before, shard, after], axis=dim)
    return shard


def face_sum(padded):
    summed = padded[2:, 1:-1, 1:-1] + padded[:-2, 1:-1, 1:-1]
    summed = summed + padded[1:-1, 2:, 1:-1] + padded[1:-1, :-2, 1:-1]
    return summed + padded[1:-1, 1:-1, 2:] + padded[1:-1, 1:-1, :-2]


def parity_mask(grid_shape):
    index_x = lax.broadcasted_iota(jnp.int32, grid_shape, 0)
    index_y = lax.broadcasted_iota(jnp.int32, grid_shape, 1)
    index_z = lax.broadcasted_iota(jnp.int32, grid_shape, 2)
    return (index_x + index_y + index_z) % 2 == 0


def coarsen(values):
    size_x, size_y, size_z = values.shape
    return 0.5 * values.reshape(size_x // 2, 2, size_y // 2, 2, size_z // 2, 2).sum(axis=(1, 3, 5))


def refine(values):
    size_x, size_y, size_z = values.shape
    spread_out = jnp.broadcast_to(
        values[:, None, :, None, :, None], (size_x, 2, size_y, 2, size_z, 2)
    )
    return spread_out.reshape(2 * size_x, 2 * size_y, 2 * size_z)


def colour_half(values, source, screen, chosen):
    padded = with_halo(values, (("gx", 0), ("gy", 1), ("gz", 2)), 1)
    return jnp.where(chosen, (source + face_sum(padded)) / (6.0 + screen), values)


def remainder_of(values, source, screen):
    padded = with_halo(values, (("gx", 0), ("gy", 1), ("gz", 2)), 1)
    return source - ((6.0 + screen) * values - face_sum(padded))


def smooth(values, source, screen, red_mask):
    values = colour_half(values, source, screen, red_mask)
    values = colour_half(values, source, screen, jnp.logical_not(red_mask))
    return values


def local(right_side, screening, coarse_inverse):
    screens = [screening]
    for level in range(LEVELS):
        screens.append(coarsen(screens[-1]))
    red_masks = [parity_mask(screen_level.shape) for screen_level in screens[:LEVELS]]
    top = LEVELS
    solution_field = jnp.zeros_like(right_side)
    cell_count = right_side.size * lax.axis_size("gx") * lax.axis_size("gy") * lax.axis_size("gz")
    norm_list = []
    for cycle_index in range(CYCLES):
        sources = [right_side]
        smoothed = []
        packs = []
        for level in range(top):
            source = sources[level]
            rim_pack = None
            packs.append(rim_pack)
            values = solution_field if level == 0 else jnp.zeros_like(source)
            values = smooth(values, source, screens[level], red_masks[level])
            smoothed.append(values)
            sources.append(coarsen(remainder_of(values, source, screens[level])))
        coarse_shape = screens[LEVELS].shape
        flat_coarse = sources[LEVELS].reshape(-1)
        gathered = lax.all_gather(flat_coarse, ("gx", "gy", "gz"), axis=0, tiled=True)
        answer = jnp.dot(coarse_inverse, gathered, precision=lax.Precision.HIGHEST)
        correction = answer.reshape(coarse_shape)
        for level in reversed(range(top)):
            values = smoothed[level] + refine(correction)
            correction = smooth(values, sources[level], screens[level], red_masks[level])
        solution_field = correction
        remainder = remainder_of(solution_field, right_side, screening)
        squares = lax.psum(jnp.sum(remainder * remainder), ("gx", "gy", "gz"))
        norm_list.append(jnp.sqrt(squares / cell_count))
    return (solution_field, jnp.stack(norm_list))


def solution(mesh):
    return jax.shard_map(
        local,
        mesh=mesh,
        in_specs=(P("gx", "gy", "gz"), P("gx", "gy", "gz"), P(("gx", "gy", "gz"), None)),
        out_specs=(P("gx", "gy", "gz"), P()),
        check_vma=False,
    )
```

profile of v0, /device:TPU:1, one launch (start us, length us, event | category | flops | bytes accessed | tf_op | source)
XLA Modules:
  0.0 1209.1 jit_solution(17897688028009338943)
XLA Ops:
  39.0 35.6 %reshape.102 = f32[16,2,16,2,64,2]{5,4,3,2,1,0:T(8,128)} reshape(f32[32,32,128]{2,1,0:T(8,128)} %param.4) | data formatting | bytes 1048576 | tf_op jit(solution)/shard_map/reshape | solution.py:38
  74.6 12.2 %reduce_sum.159 = f32[16,16,64]{2,1,0:T(8,128)S(1)} reduce(f32[16,2,16,2,64,2]{5,4,3,2,1,0:T(8,128)} %reshape.102, f32[]{:T(128)} %constant.36.clone.1), dimensions={1,3,5}, to_apply=%region_1.0 | reduce | flops 114688 | bytes 589828 | tf_op jit(solution)/shard_map/reduce_sum | solution.py:38
  113.3 35.6 %reshape.101 = f32[16,2,16,2,64,2]{5,4,3,2,1,0:T(8,128)} reshape(f32[32,32,128]{2,1,0:T(8,128)} %fusion.73) | data formatting | bytes 1048576 | tf_op jit(solution)/shard_map/reshape | solution.py:38
  148.9 12.2 %reduce_sum.158 = f32[16,16,64]{2,1,0:T(8,128)S(1)} reduce(f32[16,2,16,2,64,2]{5,4,3,2,1,0:T(8,128)} %reshape.101, f32[]{:T(128)} %constant.36.clone.1), dimensions={1,3,5}, to_apply=%region_0.0 | reduce | flops 114688 | bytes 589828 | tf_op jit(solution)/shard_map/reduce_sum | solution.py:38
  250.0 6.6 collective-permute-start.52
  325.2 67.5 %all-reduce.10 = f32[512]{0:T(512)S(1)} all-reduce(f32[512]{0:T(512)S(1)} %multiply_dynamic-update-slice_fusion.1), channel_id=1, replica_groups=mesh['gx'=4,'gy'=4,'gz'=8] {'gx','gy','gz'}, use_global_device_ids=true, to_apply=%add.10 | all-reduce | flops 512 | bytes 4096
  475.9 6.4 collective-permute-start.124
  498.8 6.4 collective-permute-start.130
  515.1 7.3 collective-permute-start.136
  523.7 11.4 broadcast_in_dim.37
  535.1 24.0 %reshape.109 = f32[32,32,128]{2,1,0:T(8,128)S(1)} reshape(f32[16,2,16,2,64,2]{5,4,3,2,1,0:T(8,128)} %broadcast_in_dim.37) | data formatting | bytes 1048576 | tf_op jit(solution)/shard_map/reshape | solution.py:46
  571.4 8.3 collective-permute-start.142
  661.7 35.6 %reshape.110 = f32[16,2,16,2,64,2]{5,4,3,2,1,0:T(8,128)} reshape(f32[32,32,128]{2,1,0:T(8,128)} %fusion.37) | data formatting | bytes 1048576 | tf_op jit(solution)/shard_map/reshape | solution.py:38
  697.3 12.2 %reduce_sum.169 = f32[16,16,64]{2,1,0:T(8,128)S(1)} reduce(f32[16,2,16,2,64,2]{5,4,3,2,1,0:T(8,128)} %reshape.110, f32[]{:T(128)} %constant.36.clone.1), dimensions={1,3,5}, to_apply=%region_10.11 | reduce | flops 114688 | bytes 589828 | tf_op jit(solution)/shard_map/reduce_sum | solution.py:38
  733.9 6.7 collective-permute-start.178
  758.0 7.8 collective-permute-start.184
  775.9 7.0 collective-permute-start.190
  845.0 67.5 %all-reduce.11 = f32[512]{0:T(512)S(1)} all-reduce(f32[512]{0:T(512)S(1)} %multiply_dynamic-update-slice_fusion), channel_id=1, replica_groups=mesh['gx'=4,'gy'=4,'gz'=8] {'gx','gy','gz'}, use_global_device_ids=true, to_apply=%add.11 | all-reduce | flops 512 | bytes 4096
  1018.6 6.4 collective-permute-start.256
  1035.1 7.3 collective-permute-start.262
  1043.7 11.4 broadcast_in_dim.83
  1055.1 24.0 %reshape.117 = f32[32,32,128]{2,1,0:T(8,128)S(1)} reshape(f32[16,2,16,2,64,2]{5,4,3,2,1,0:T(8,128)} %broadcast_in_dim.83) | data formatting | bytes 1048576 | tf_op jit(solution)/shard_map/reshape | solution.py:46
  1091.0 8.3 collective-permute-start.268
  1139.1 67.7 %all-reduce.12 = (f32[]{:T(128)}, f32[]{:T(128)}) all-reduce(f32[]{:T(128)} %fusion.14, f32[]{:T(128)} %get-tuple-element.4), channel_id=1, replica_groups=mesh['gx'=4,'gy'=4,'gz'=8] {'gx','gy','gz'}, use_global_device_ids=true, to_apply=%region_19.20 | all-reduce | flops 2 | bytes 16 | tf_op jit(solution)/shard_map/psum | solution.py:96
  (937 shorter events, 708.8 us)
Async XLA Ops:
  34.7 52.1 %collective-permute-start.11 = (f32[34,34,1]{1,2,0:T(1,128)S(1)}, f32[34,34,1]{1,2,0:T(1,128)S(1)}, u32[]{:S(2)}, u32[]{:S(2)}) collective-permute-start(f32[34,34,1]{1,2,0:T(1,128)S(1)} %copy.11), channel_id=1, source_target_pairs={{0,1},{1,2},{2,3},{3,4},{4,5},{5,6},{6,7},{7,0},{8,9},{9,10},{10,1... | collective-permute-start | bytes 13880 | tf_op jit(solution)/shard_map/ppermute | solution.py:17
  37.5 49.8 %collective-permute-start.10 = (f32[34,34,1]{1,2,0:T(1,128)S(1)}, f32[34,34,1]{1,2,0:T(1,128)S(1)}, u32[]{:S(2)}, u32[]{:S(2)}) collective-permute-start(f32[34,34,1]{1,2,0:T(1,128)S(1)} %copy.9), channel_id=1, source_target_pairs={{1,0},{2,1},{3,2},{4,3},{5,4},{6,5},{7,6},{0,7},{9,8},{10,9},{11,1... | collective-permute-start | bytes 13880 | tf_op jit(solution)/shard_map/ppermute | solution.py:18
  37.5 54.4 %collective-permute-start.18 = (f32[1,16,64]{2,1,0:T(8,128)S(1)}, f32[1,16,64]{2,1,0:T(8,128)S(1)}, u32[]{:S(2)}, u32[]{:S(2)}) collective-permute-start(f32[1,16,64]{2,1,0:T(8,128)S(1)} %broadcast.143), channel_id=1, source_target_pairs={{32,0},{64,32},{96,64},{0,96},{33,1},{65,33},{97,65},{1,97},{34,2}... | collective-permute-start | bytes 12296 | tf_op jit(solution)/shard_map/ppermute | solution.py:18
  37.6 54.3 %collective-permute-start.19 = (f32[1,16,64]{2,1,0:T(8,128)S(1)}, f32[1,16,64]{2,1,0:T(8,128)S(1)}, u32[]{:S(2)}, u32[]{:S(2)}) collective-permute-start(f32[1,16,64]{2,1,0:T(8,128)S(1)} %broadcast.143), channel_id=1, source_target_pairs={{0,32},{32,64},{64,96},{96,0},{1,33},{33,65},{65,97},{97,1},{2,34}... | collective-permute-start | bytes 12296 | tf_op jit(solution)/shard_map/ppermute | solution.py:17
  101.0 9.5 collective-permute-start.17
  107.5 53.6 %collective-permute-start.23 = (f32[18,18,1]{2,1,0:T(8,128)}, f32[18,18,1]{2,1,0:T(8,128)S(1)}, u32[]{:S(2)}, u32[]{:S(2)}) collective-permute-start(f32[18,18,1]{2,1,0:T(8,128)} %get-tuple-element.95), channel_id=1, source_target_pairs={{0,1},{1,2},{2,3},{3,4},{4,5},{5,6},{6,7},{7,0},{8,9},{9,10},{10,1... | collective-permute-start | bytes 3896 | tf_op jit(solution)/shard_map/ppermute | solution.py:17
  108.4 52.7 %collective-permute-start.22 = (f32[18,18,1]{2,1,0:T(8,128)}, f32[18,18,1]{2,1,0:T(8,128)}, u32[]{:S(2)}, u32[]{:S(2)}) collective-permute-start(f32[18,18,1]{2,1,0:T(8,128)} %get-tuple-element.94), channel_id=1, source_target_pairs={{1,0},{2,1},{3,2},{4,3},{5,4},{6,5},{7,6},{0,7},{9,8},{10,9},{11,1... | collective-permute-start | bytes 3896 | tf_op jit(solution)/shard_map/ppermute | solution.py:18
  169.6 19.7 %collective-permute-start.36 = (f32[1,8,32]{2,1,0:T(8,128)S(1)}, f32[1,8,32]{2,1,0:T(8,128)S(1)}, u32[]{:S(2)}, u32[]{:S(2)}) collective-permute-start(f32[1,8,32]{2,1,0:T(8,128)S(1)} %broadcast.148), channel_id=1, source_target_pairs={{32,0},{64,32},{96,64},{0,96},{33,1},{65,33},{97,65},{1,97},{34,2}... | collective-permute-start | bytes 3080 | tf_op jit(solution)/shard_map/ppermute | solution.py:18
  169.6 19.8 %collective-permute-start.37 = (f32[1,8,32]{2,1,0:T(8,128)S(1)}, f32[1,8,32]{2,1,0:T(8,128)S(1)}, u32[]{:S(2)}, u32[]{:S(2)}) collective-permute-start(f32[1,8,32]{2,1,0:T(8,128)S(1)} %broadcast.148), channel_id=1, source_target_pairs={{0,32},{32,64},{64,96},{96,0},{1,33},{33,65},{65,97},{97,1},{2,34}... | collective-permute-start | bytes 3080 | tf_op jit(solution)/shard_map/ppermute | solution.py:17
  171.1 70.7 %collective-permute-start.54 = (f32[1,4,16]{2,1,0:T(4,128)S(1)}, f32[1,4,16]{2,1,0:T(4,128)S(1)}, u32[]{:S(2)}, u32[]{:S(2)}) collective-permute-start(f32[1,4,16]{2,1,0:T(4,128)S(1)} %broadcast.153), channel_id=1, source_target_pairs={{32,0},{64,32},{96,64},{0,96},{33,1},{65,33},{97,65},{1,97},{34,2}... | collective-permute-start | bytes 776 | tf_op jit(solution)/shard_map/ppermute | solution.py:18
  172.5 13.9 %collective-permute-start.29 = (f32[18,18,1]{2,1,0:T(8,128)S(1)}, f32[18,18,1]{2,1,0:T(8,128)S(1)}, u32[]{:S(2)}, u32[]{:S(2)}) collective-permute-start(f32[18,18,1]{2,1,0:T(8,128)S(1)} %get-tuple-element.93), channel_id=1, source_target_pairs={{0,1},{1,2},{2,3},{3,4},{4,5},{5,6},{6,7},{7,0},{8,9},{9,10},{10,1... | collective-permute-start | bytes 3896 | tf_op jit(solution)/shard_map/ppermute | solution.py:17
  174.7 12.2 %collective-permute-start.28 = (f32[18,18,1]{2,1,0:T(8,128)S(1)}, f32[18,18,1]{2,1,0:T(8,128)S(1)}, u32[]{:S(2)}, u32[]{:S(2)}) collective-permute-start(f32[18,18,1]{2,1,0:T(8,128)S(1)} %get-tuple-element.92), channel_id=1, source_target_pairs={{1,0},{2,1},{3,2},{4,3},{5,4},{6,5},{7,6},{0,7},{9,8},{10,9},{11,1... | collective-permute-start | bytes 3896 | tf_op jit(solution)/shard_map/ppermute | solution.py:18
  186.3 55.4 %collective-permute-start.55 = (f32[1,4,16]{2,1,0:T(4,128)S(1)}, f32[1,4,16]{2,1,0:T(4,128)S(1)}, u32[]{:S(2)}, u32[]{:S(2)}) collective-permute-start(f32[1,4,16]{2,1,0:T(4,128)S(1)} %broadcast.153), channel_id=1, source_target_pairs={{0,32},{32,64},{64,96},{96,0},{1,33},{33,65},{65,97},{97,1},{2,34}... | collective-permute-start | bytes 776 | tf_op jit(solution)/shard_map/ppermute | solution.py:17
  186.9 79.1 %collective-permute-start.72 = (f32[1,2,8]{2,1,0:T(2,128)S(1)}, f32[1,2,8]{2,1,0:T(2,128)S(1)}, u32[]{:S(2)}, u32[]{:S(2)}) collective-permute-start(f32[1,2,8]{2,1,0:T(2,128)S(1)} %broadcast.158), channel_id=1, source_target_pairs={{32,0},{64,32},{96,64},{0,96},{33,1},{65,33},{97,65},{1,97},{34,2}... | collective-permute-start | bytes 200 | tf_op jit(solution)/shard_map/ppermute | solution.py:18
  209.1 14.1 %collective-permute-start.41 = (f32[10,10,1]{2,1,0:T(8,128)S(1)}, f32[10,10,1]{2,1,0:T(8,128)S(1)}, u32[]{:S(2)}, u32[]{:S(2)}) collective-permute-start(f32[10,10,1]{2,1,0:T(8,128)S(1)} %get-tuple-element.147), channel_id=1, source_target_pairs={{0,1},{1,2},{2,3},{3,4},{4,5},{5,6},{6,7},{7,0},{8,9},{9,10},{10,1... | collective-permute-start | bytes 1208 | tf_op jit(solution)/shard_map/ppermute | solution.py:17
  209.3 14.0 %collective-permute-start.40 = (f32[10,10,1]{2,1,0:T(8,128)S(1)}, f32[10,10,1]{2,1,0:T(8,128)S(1)}, u32[]{:S(2)}, u32[]{:S(2)}) collective-permute-start(f32[10,10,1]{2,1,0:T(8,128)S(1)} %get-tuple-element.146), channel_id=1, source_target_pairs={{1,0},{2,1},{3,2},{4,3},{5,4},{6,5},{7,6},{0,7},{9,8},{10,9},{11,1... | collective-permute-start | bytes 1208 | tf_op jit(solution)/shard_map/ppermute | solution.py:18
  238.9 27.2 %collective-permute-start.73 = (f32[1,2,8]{2,1,0:T(2,128)S(1)}, f32[1,2,8]{2,1,0:T(2,128)S(1)}, u32[]{:S(2)}, u32[]{:S(2)}) collective-permute-start(f32[1,2,8]{2,1,0:T(2,128)S(1)} %broadcast.158), channel_id=1, source_target_pairs={{0,32},{32,64},{64,96},{96,0},{1,33},{33,65},{65,97},{97,1},{2,34}... | collective-permute-start | bytes 200 | tf_op jit(solution)/shard_map/ppermute | solution.py:17
  250.0 11.7 collective-permute-start.52
  271.3 9.0 collective-permute-start.74
  284.5 12.8 %collective-permute-start.77 = (f32[4,4,1]{2,1,0:T(4,128)S(1)}, f32[4,4,1]{2,1,0:T(4,128)S(1)}, u32[]{:S(2)}, u32[]{:S(2)}) collective-permute-start(f32[4,4,1]{2,1,0:T(4,128)S(1)} %get-tuple-element.247), channel_id=1, source_target_pairs={{0,1},{1,2},{2,3},{3,4},{4,5},{5,6},{6,7},{7,0},{8,9},{9,10},{10,1... | collective-permute-start | bytes 200 | tf_op jit(solution)/shard_map/ppermute | solution.py:17
  571.0 9.0 collective-permute-start.143
  571.4 9.1 collective-permute-start.142
  1090.7 9.0 collective-permute-start.269
  1091.0 9.1 collective-permute-start.268
  (272 other events, 2121.4 us)
where the time goes:
time: 1220 us; the launch traced here: 1210 us
  starting transfers between devices  422 us (35%)
  waiting for transfers between devices  256 us (21%)
  local copies, waits for them, and re-layouts  249 us (20%)
  blocking collectives  203 us (17%)
  other arithmetic  75.6 us (6%)
    ppermute x141, starting transfers between devices, with_halo(): after = lax.ppermute(initial, axis, down)  266 us
    ppermute x141, waiting for transfers between devices, with_halo(): before = lax.ppermute(last, axis, up)  156 us
    ppermute x141, starting transfers between devices, with_halo(): before = lax.ppermute(last, axis, up)  155 us
    unnamed x2, blocking collectives  135 us
    reshape x9, local copies, waits for them, and re-layouts, coarsen(): values.reshape(size_x // 2, 2, size_y // 2, 2, size_z // 2, 2)  119 us
    ppermute x141, waiting for transfers between devices, with_halo(): after = lax.ppermute(initial, axis, down)  99.6 us
    psum x1, blocking collectives, local(): squares = lax.psum(jnp.sum(remainder * remainder), ('gx', 'gy', 'gz'))  67.7 us
    reshape x8, local copies, waits for them, and re-layouts, refine(): return spread_out.reshape(2 * size_x, 2 * size_y, 2 * size_z)  58.4 us
  transfers between devices with their start and end apart: 282, of which 249 were waited for; matrix products, arithmetic and copies ran while one was open for 11% of the time, Pallas kernels for 0%

commit v1 on v0

v1 whole, which is shorter than its diff:
```python
import functools

import jax
import jax.numpy as jnp
from jax import lax
from jax.experimental import pallas as pl
from jax.experimental.pallas import tpu as pltpu
from jax.sharding import PartitionSpec as P

AXES = ("gx", "gy", "gz")
F32 = jnp.float32
LANES = 128
OWN = 32
H0 = 8
X0, Y0 = 48, 48
H1 = 14
X1, Y1 = 44, 48
H2 = 6
X2, Y2 = 20, 24
GROUP0 = 8
GROUP1 = 4
CELLS = 16777216.0


def iota(shape, dim):
    return lax.broadcasted_iota(jnp.int32, shape, dim)


def roll(value, shift, axis):
    return pltpu.roll(value, shift % value.shape[axis], axis)


def pick(value, index):
    return jnp.take_along_axis(value, index, axis=1, mode="promise_in_bounds")


def loop(start, stop, body, unroll=2):
    def step(index, carry):
        body(index)
        return carry

    lax.fori_loop(start, stop, step, 0, unroll=unroll)


def call(body, outs, *operands, scratch=()):
    specs = [
        pl.BlockSpec(memory_space=pltpu.SMEM if operand.dtype == jnp.int32 else pltpu.VMEM)
        for operand in operands
    ]
    return pl.pallas_call(
        body,
        out_shape=[jax.ShapeDtypeStruct(shape, F32) for shape in outs],
        in_specs=specs,
        out_specs=[pl.BlockSpec(memory_space=pltpu.VMEM)] * len(outs),
        scratch_shapes=[pltpu.VMEM(shape, F32) for shape in scratch],
        compiler_params=pltpu.CompilerParams(vmem_limit_bytes=56 * 1024 * 1024),
    )(*operands)


def beside(values, plane):
    mid = values[plane]
    total = values[plane + 1] + values[plane - 1]
    return mid, total + roll(mid, 1, 0) + roll(mid, -1, 0)


def sum_natural(values, plane):
    mid, total = beside(values, plane)
    return total + roll(mid, 1, 1) + roll(mid, -1, 1)


def sum_half(values, plane, onto_red):
    mid, total = beside(values, plane)
    odd = (iota(mid.shape, 0) + plane) % 2 == 1
    high = odd if onto_red else jnp.logical_not(odd)
    return total + mid + jnp.where(high, roll(mid, -1, 1), roll(mid, 1, 1))


def is_red(shape, plane):
    return (iota(shape, 0) + iota(shape, 1) + plane) % 2 == 0


def plane0(own, low, high, below, above, field, plane):
    if plane < H0:
        mid = low[field * H0 + plane]
    elif plane < H0 + 32:
        mid = own[plane - H0]
    else:
        mid = high[field * H0 + plane - H0 - 32]
    return jnp.concatenate([below[field * X0 + plane], mid, above[field * X0 + plane]], axis=0)


def pack_z0(f, s, low, high, below, above, to_high, to_low):
    lane = iota((Y0, LANES), 1)
    for group in range(-(-X0 // GROUP0)):
        up = jnp.zeros((Y0, LANES), F32)
        down = jnp.zeros((Y0, LANES), F32)
        for k in range(min(GROUP0, X0 - group * GROUP0)):
            plane = group * GROUP0 + k
            for field, own in enumerate((f, s)):
                value = plane0(own, low, high, below, above, field, plane)
                at = 16 * k + 8 * field
                here = jnp.logical_and(lane >= at, lane < at + 8)
                up = jnp.where(here, roll(value, at - 120, 1), up)
                down = jnp.where(here, roll(value, at, 1), down)
        to_high[group] = up
        to_low[group] = down


def down0(f, s, low, high, below, above, from_low, from_high, fr, fb, ir, ib, vb, fs1, red, sums):
    shape = (Y0, LANES)
    k_at = iota(shape, 1) - OWN
    for plane in range(X0):
        group, k = divmod(plane, GROUP0)
        odd = (iota(shape, 0) + plane) % 2
        for field, own in enumerate((f, s)):
            value = plane0(own, low, high, below, above, field, plane)
            at = 16 * k + 8 * field
            for colour in (0, 1):
                z = 2 * k_at + (odd if colour == 0 else 1 - odd)
                inner = pick(value, jnp.clip(z, 0, 127))
                left = pick(from_low[group], jnp.clip(z + 8 + at, 0, 127))
                right = pick(from_high[group], jnp.clip(z - 128 + at, 0, 127))
                result = jnp.where(k_at < 0, left, jnp.where(k_at > 63, right, inner))
                if field == 0:
                    (fr, fb)[colour][plane] = result
                else:
                    (ir, ib)[colour][plane] = result
    lane = iota((16, LANES), 1)

    def screen1(i):
        plane = 2 * i + H0
        sums[0] = ir[plane] + ib[plane] + ir[plane + 1] + ib[plane + 1]
        total = sums[0, pl.ds(8, 16, stride=2), :] + sums[0, pl.ds(9, 16, stride=2), :]
        fs1[i] = roll(0.5 * total, 64 - OWN, 1)

    loop(0, 16, screen1)

    def invert(p):
        ir[p] = 1.0 / (6.0 + ir[p])
        ib[p] = 1.0 / (6.0 + ib[p])
        red[p] = fr[p] * ir[p]

    loop(0, X0, invert)

    def black(p):
        vb[p] = (fb[p] + sum_half(red, p, False)) * ib[p]

    loop(1, X0 - 1, black)
    vb[0] = jnp.zeros(shape, F32)
    vb[X0 - 1] = jnp.zeros(shape, F32)

    def restrict(i):
        plane = 2 * i + H0
        sums[0] = sum_half(vb, plane, True) + sum_half(vb, plane + 1, True)
        total = sums[0, pl.ds(8, 16, stride=2), :] + sums[0, pl.ds(9, 16, stride=2), :]
        fs1[i] = jnp.where(lane < 64, roll(0.5 * total, -OWN, 1), fs1[i])

    loop(0, 16, restrict)


def pack_z1(own, below, above, to_high, to_low):
    lane = iota((Y1, LANES), 1)
    for group in range(X1 // GROUP1):
        up = jnp.zeros((Y1, LANES), F32)
        down = jnp.zeros((Y1, LANES), F32)
        for k in range(GROUP1):
            plane = group * GROUP1 + k
            value = jnp.concatenate([below[plane], own[plane], above[plane]], axis=0)
            for field in (0, 1):
                at = 28 * k + 14 * field
                here = jnp.logical_and(lane >= at, lane < at + 14)
                up = jnp.where(here, roll(value, at - 64 * field - 50, 1), up)
                down = jnp.where(here, roll(value, at - 64 * field, 1), down)
        to_high[group] = up
        to_low[group] = down


def unpack1(own, below, above, from_low, from_high, field, plane):
    lane = iota((Y1, LANES), 1)
    group, k = divmod(plane, GROUP1)
    at = 28 * k + 14 * field
    value = jnp.concatenate([below[plane], own[plane], above[plane]], axis=0)
    value = roll(value, OWN - 64 * field, 1)
    left = roll(from_low[group], OWN - 14 - at, 1)
    right = roll(from_high[group], OWN + 64 - at, 1)
    return jnp.where(lane < OWN, left, jnp.where(lane < OWN + 64, value, right))


def pair_index(rows):
    return jnp.clip(2 * iota((rows, LANES), 1) - OWN, 0, 127)


def spread_index(rows):
    return (iota((rows, LANES), 1) - OWN) // 2 + OWN


def sweep_zero(source, inverse, values, count, shape):
    def red(p):
        values[p] = jnp.where(is_red(shape, p), source[p] * inverse[p], 0.0)

    def black(p):
        fresh = (source[p] + sum_natural(values, p)) * inverse[p]
        values[p] = jnp.where(is_red(shape, p), values[p], fresh)

    loop(0, count, red)
    loop(1, count - 1, black)


def down12(f1, i1, v1, f2, i2, v2, sums):
    sweep_zero(f1, i1, v1, X1, (Y1, LANES))
    f2[0] = jnp.zeros((Y2, LANES), F32)
    f2[X2 - 1] = jnp.zeros((Y2, LANES), F32)

    def restrict(i):
        plane = 2 * i + 2
        total = jnp.zeros((Y1, LANES), F32)
        for p in (plane, plane + 1):
            total += jnp.where(is_red((Y1, LANES), p), sum_natural(v1, p), 0.0)
        f2[i] = coarse12(total, sums)

    loop(0, X2, restrict)
    sweep_zero(f2, i2, v2, X2, (Y2, LANES))


def coarse12(total, sums):
    sums[0] = total
    pairs = sums[0, pl.ds(0, Y2, stride=2), :] + sums[0, pl.ds(1, Y2, stride=2), :]
    pairs = pairs + roll(pairs, -1, 1)
    return 0.5 * pick(pairs, pair_index(Y2))


def coarse23(total, sums, x3):
    sums[0, 0:Y2, :] = total
    pairs = sums[0, pl.ds(8, 8, stride=2), :] + sums[0, pl.ds(9, 8, stride=2), :]
    pairs = pairs + roll(pairs, -1, 1)
    lane = iota((8, LANES), 1)
    spread = pick(pairs, OWN + 2 * (lane % 16))
    here = lane // 16 == (x3 % 2) * 4 + iota((8, LANES), 0)
    here = jnp.logical_and(here, iota((8, LANES), 0) < 4)
    return 0.5 * jnp.sum(jnp.where(here, spread, 0.0), axis=0, keepdims=True)


def source3(v2, sums):
    rows = []
    for x3 in range(4):
        plane = 2 * x3 + H2
        total = jnp.zeros((Y2, LANES), F32)
        for p in (plane, plane + 1):
            total += jnp.where(is_red((Y2, LANES), p), sum_natural(v2, p), 0.0)
        rows.append(coarse23(total, sums, x3))
    return [rows[0] + rows[1], rows[2] + rows[3]]


def down12_first(own, below, above, from_low, from_high, f1, i1, v1, f2, i2, v2, message, sums):
    for plane in range(X1):
        f1[plane] = unpack1(own, below, above, from_low, from_high, 0, plane)
        i1[plane] = unpack1(own, below, above, from_low, from_high, 1, plane)

    def screen2(i):
        i2[i] = coarse12(i1[2 * i + 2] + i1[2 * i + 3], sums)

    loop(0, X2, screen2)
    rows = []
    for x3 in range(4):
        plane = 2 * x3 + H2
        rows.append(coarse23(i2[plane] + i2[plane + 1], sums, x3))

    def invert1(p):
        i1[p] = 1.0 / (6.0 + i1[p])

    def invert2(p):
        i2[p] = 1.0 / (6.0 + i2[p])

    loop(0, X1, invert1)
    loop(0, X2, invert2)
    down12(f1, i1, v1, f2, i2, v2, sums)
    tile = jnp.concatenate(source3(v2, sums) + [rows[0] + rows[1], rows[2] + rows[3]], axis=0)
    tile = jnp.concatenate([tile, tile], axis=0)
    for i in range(64):
        message[8 * i : 8 * i + 8, :] = tile


def down12_next(own, below, above, from_low, from_high, i1, i2, f1, v1, f2, v2, message, sums):
    for plane in range(X1):
        f1[plane] = unpack1(own, below, above, from_low, from_high, 0, plane)
    down12(f1, i1, v1, f2, i2, v2, sums)
    tile = jnp.concatenate(source3(v2, sums) * 4, axis=0)
    for i in range(32):
        message[8 * i : 8 * i + 8, :] = tile


def unpack3(message, rows, first, into):
    sub, lane = iota((8, LANES), 0), iota((8, LANES), 1)
    for gx in range(4):
        for gy in range(4):
            for half in range(2):
                start = (gx * 4 + gy) * 8 * rows + first + half
                value = message[pl.ds(start, 8, stride=rows), :]
                for k in (1, 2, 4):
                    sub_high = (sub // k) % 2 == 1
                    lane_high = (lane // (16 * k)) % 2 == 1
                    from_below = roll(roll(value, -k, 0), 16 * k, 1)
                    from_above = roll(roll(value, k, 0), -16 * k, 1)
                    value = jnp.where(
                        sub_high == lane_high, value, jnp.where(sub_high, from_above, from_below)
                    )
                for x in range(2):
                    into[gx * 4 + 2 * half + x, gy * 4 : gy * 4 + 4, :] = value[4 * x : 4 * x + 4, :]


def turn(value, shift, axis):
    if axis == 0:
        return jnp.concatenate([value[-shift:], value[:-shift]], axis=0)
    return roll(value, shift, axis)


def sum_whole(value):
    total = turn(value, 1, 0) + turn(value, -1, 0)
    total = total + turn(value, 1, 1) + turn(value, -1, 1)
    return total + turn(value, 1, 2) + turn(value, -1, 2)


def red_whole(shape):
    return (iota(shape, 0) + iota(shape, 1) + iota(shape, 2)) % 2 == 0


def pick3(value, index):
    flat = value.reshape(-1, LANES)
    return pick(flat, jnp.broadcast_to(index, flat.shape)).reshape(value.shape)


def coarse34(value, wide):
    wide[...] = value.reshape(8, 2, 16, LANES).sum(axis=1)
    pairs = wide[:, pl.ds(0, 8, stride=2), :] + wide[:, pl.ds(1, 8, stride=2), :]
    pairs = pairs + roll(pairs, -1, 2)
    return 0.5 * pick3(pairs, 2 * (iota((1, LANES), 1) % 64))


def coarse_solve(f3, i3, i4, inverse, e3, wide):
    red3, red4 = red_whole((16, 16, LANES)), red_whole((8, 8, LANES))
    v3 = jnp.where(red3, f3 * i3, 0.0)
    v3 = jnp.where(red3, v3, (f3 + sum_whole(v3)) * i3)
    f4 = coarse34(jnp.where(red3, sum_whole(v3), 0.0), wide)
    v4 = jnp.where(red4, f4 * i4, 0.0)
    v4 = jnp.where(red4, v4, (f4 + sum_whole(v4)) * i4)
    r4 = jnp.where(red4, sum_whole(v4), 0.0).reshape(4, 2, 8, LANES).sum(axis=1)
    sub, lane = iota((8, LANES), 0), iota((8, LANES), 1)
    rows = []
    for x5 in range(4):
        pairs = r4[x5] + roll(r4[x5], -1, 1)
        spread = jnp.where(sub // 2 == lane // 32, pick(pairs, 2 * (lane % 32)), 0.0)
        rows.append(0.5 * jnp.sum(spread, axis=0, keepdims=True))
    vector = jnp.broadcast_to(jnp.concatenate(rows, axis=1), (8, 512))
    answer = lax.dot_general(
        vector,
        inverse[...],
        (((1,), (1,)), ((), ())),
        precision=lax.Precision.HIGHEST,
        preferred_element_type=F32,
    )
    planes = []
    for x5 in range(4):
        part = pick(answer[:, 128 * x5 : 128 * x5 + 128], (sub // 2) * 32 + (lane % 64) // 2)
        planes += [part[None], part[None]]
    w4 = v4 + jnp.concatenate(planes, axis=0)
    w4 = jnp.where(red4, (f4 + sum_whole(w4)) * i4, w4)
    e4 = jnp.where(red4, w4, (f4 + sum_whole(w4)) * i4)
    e4 = pick3(e4, iota((1, LANES), 1) // 2)
    wide[:, pl.ds(0, 8, stride=2), :] = e4
    wide[:, pl.ds(1, 8, stride=2), :] = e4
    spread = jnp.broadcast_to(wide[...][:, None], (8, 2, 16, LANES)).reshape(16, 16, LANES)
    w3 = v3 + spread
    w3 = jnp.where(red3, (f3 + sum_whole(w3)) * i3, w3)
    e3[...] = jnp.where(red3, w3, (f3 + sum_whole(w3)) * i3)


def sweep_up(source, inverse, values, first, last, shape):
    def red(p):
        fresh = (source[p] + sum_natural(values, p)) * inverse[p]
        values[p] = jnp.where(is_red(shape, p), fresh, values[p])

    def black(p):
        fresh = (source[p] + sum_natural(values, p)) * inverse[p]
        values[p] = jnp.where(is_red(shape, p), values[p], fresh)

    loop(first, last + 1, red)
    loop(first + 1, last, black)


def up21(place, e3, f2, i2, v2, f1, i1, v1, e2, e1, tall):
    shift_y = lax.rem(20 - 4 * place[1], 16)
    shift_z = lax.rem(160 - 16 * place[2], 128)

    def from3(i):
        value = e3[lax.rem(4 * place[0] + i + 13, 16)]
        value = pltpu.roll(pltpu.roll(value, shift_y, 0), shift_z, 1)
        value = pick(value, spread_index(16))[:12]
        tall[0, pl.ds(0, 12, stride=2), :] = value
        tall[0, pl.ds(1, 12, stride=2), :] = value
        value = tall[0, 0:Y2, :]
        e2[2 * i] = v2[2 * i] + value
        e2[2 * i + 1] = v2[2 * i + 1] + value

    loop(0, X2 // 2, from3, 1)
    sweep_up(f2, i2, e2, 1, X2 - 2, (Y2, LANES))

    def from2(i):
        value = pick(e2[i], spread_index(Y2))
        tall[0, pl.ds(0, Y2, stride=2), :] = value
        tall[0, pl.ds(1, Y2, stride=2), :] = value
        value = tall[0]
        e1[2 * i + 2] = v1[2 * i + 2] + value
        e1[2 * i + 3] = v1[2 * i + 3] + value

    loop(3, 17, from2, 1)
    sweep_up(f1, i1, e1, 9, 34, (Y1, LANES))


def add0(e1, b, w, tall):
    def from1(i):
        value = e1[i + 10, pl.ds(12, 24), :]
        tall[0, pl.ds(0, 24, stride=2), :] = value
        tall[0, pl.ds(1, 24, stride=2), :] = value
        value = tall[0]
        w[2 * i] = b[2 * i] + value
        w[2 * i + 1] = b[2 * i + 1] + value

    loop(0, X0 // 2, from1, 1)


def middle(
    message, place, inverse, f2, i2, v2, f1, i1, v1, fr, fb, ir, ib, vb,
    i3, i4, rnew, bnew, own1, norm,
    f3, e3, wide, tall, e2, e1, w, r,
):
    unpack3(message, 4, 0, f3)
    unpack3(message, 4, 2, e3)
    screen3 = e3[...]
    screen4 = coarse34(screen3, wide)
    i3[...] = 1.0 / (6.0 + screen3)
    i4[...] = 1.0 / (6.0 + screen4)
    coarse_solve(f3[...], i3[...], i4[...], inverse, e3, wide)
    up21(place, e3, f2, i2, v2, f1, i1, v1, e2, e1, tall)
    add0(e1, vb, w, tall)

    def red_up(p):
        r[p] = (fr[p] + sum_half(w, p, True)) * ir[p]

    loop(2, X0 - 2, red_up)

    def black_up(p):
        w[p] = (fb[p] + sum_half(r, p, False)) * ib[p]

    loop(3, X0 - 3, black_up)

    def red_down(p):
        rnew[p] = (fr[p] + sum_half(w, p, True)) * ir[p]

    loop(4, X0 - 4, red_down)

    def squares(p, total):
        part = (rnew[p] - r[p])[8:40] / ir[p, 8:40, :]
        return total + part * part

    total = lax.fori_loop(H0, H0 + 32, squares, jnp.zeros((32, LANES), F32), unroll=2)
    norm[...] = jnp.sum(total.reshape(4, 8, LANES), axis=0)

    def black_down(p):
        fresh = (fb[p] + sum_half(rnew, p, False)) * ib[p]
        bnew[p] = fresh
        r[p] = fresh - w[p]

    loop(5, X0 - 5, black_down)

    def restrict(i):
        plane = 2 * i + H0
        tall[0] = sum_half(r, plane, True) + sum_half(r, plane + 1, True)
        total = tall[0, pl.ds(8, 16, stride=2), :] + tall[0, pl.ds(9, 16, stride=2), :]
        own1[i] = roll(0.5 * total, -OWN, 1)

    loop(0, 16, restrict)


def final(
    message, place, inverse, f2, i2, v2, f1, i1, v1, fr, fb, ir, ib, b, i3, i4, norm,
    field, sums,
    f3, e3, wide, tall, e2, e1, w, r, last,
):
    unpack3(message, 2, 0, f3)
    coarse_solve(f3[...], i3[...], i4[...], inverse, e3, wide)
    up21(place, e3, f2, i2, v2, f1, i1, v1, e2, e1, tall)
    add0(e1, b, w, tall)

    def red_up(p):
        r[p] = (fr[p] + sum_half(w, p, True)) * ir[p]

    loop(6, X0 - 6, red_up)

    def black_up(p):
        fresh = (fb[p] + sum_half(r, p, False)) * ib[p]
        last[p] = fresh
        w[p] = fresh - w[p]

    loop(7, X0 - 7, black_up)

    def finish(p, total):
        part = sum_half(w, p, True)[8:40]
        lane = iota((32, LANES), 1)
        index = OWN + lane // 2
        reds = pick(r[p, 8:40, :], index)
        blacks = pick(last[p, 8:40, :], index)
        here = (iota((32, LANES), 0) + lane + p) % 2 == 0
        field[p - H0] = jnp.where(here, reds, blacks)
        return total + part * part

    total = lax.fori_loop(H0, H0 + 32, finish, jnp.zeros((32, LANES), F32), unroll=2)
    after = jnp.sum(total, axis=0, keepdims=True)
    before = jnp.sum(norm[...], axis=0, keepdims=True)
    low = iota((1, LANES), 1) < 64
    both = jnp.where(low, roll(before, -OWN, 1), roll(after, 64 - OWN, 1))
    for i in range(16):
        sums[8 * i : 8 * i + 8, :] = jnp.broadcast_to(both, (8, LANES))


def exchange(to_high, to_low, axis):
    count = lax.axis_size(axis)
    up = [(i, (i + 1) % count) for i in range(count)]
    down = [(j, i) for i, j in up]
    return lax.ppermute(to_high, axis, up), lax.ppermute(to_low, axis, down)


def exchange1(own):
    low, high = exchange(own[16 - H1 :], own[:H1], "gx")
    own = jnp.concatenate([low, own, high], axis=0)
    below, above = exchange(own, own, "gy")
    groups = X1 // GROUP1
    to_high, to_low = call(pack_z1, [(groups, Y1, LANES)] * 2, own, below, above)
    from_low, from_high = exchange(to_high, to_low, "gz")
    return own, below, above, from_low, from_high


def local(f, s, coarse_inverse):
    inverse = lax.all_gather(coarse_inverse, AXES, axis=0, tiled=True)
    place = jnp.stack([lax.axis_index(axis) for axis in AXES]).astype(jnp.int32)
    low, high = exchange(
        jnp.concatenate([f[32 - H0 :], s[32 - H0 :]], axis=0),
        jnp.concatenate([f[:H0], s[:H0]], axis=0),
        "gx",
    )

    def rows(cut):
        parts = [low[:H0], f, high[:H0], low[H0:], s, high[H0:]]
        return jnp.concatenate([part[:, cut] for part in parts], axis=0)

    below, above = exchange(rows(slice(24, 32)), rows(slice(0, 8)), "gy")
    groups = -(-X0 // GROUP0)
    pieces = (f, s, low, high, below, above)
    to_high, to_low = call(pack_z0, [(groups, Y0, LANES)] * 2, *pieces)
    from_low, from_high = exchange(to_high, to_low, "gz")
    level0, level1, level2 = (X0, Y0, LANES), (X1, Y1, LANES), (X2, Y2, LANES)
    line = (1, Y0, LANES)
    fr, fb, ir, ib, vb, own1 = call(
        down0, [level0] * 5 + [(16, 16, LANES)], *pieces, from_low, from_high, scratch=[level0, line]
    )
    f1, i1, v1, f2, i2, v2, message = call(
        down12_first,
        [level1] * 3 + [level2] * 3 + [(512, LANES)],
        *exchange1(own1),
        scratch=[line],
    )
    message = lax.all_to_all(message, AXES, 0, 0, tiled=True)
    whole = (16, 16, LANES)
    work = [whole, whole, (8, 16, LANES), line, level2, level1, level0, level0]
    i3, i4, rnew, bnew, own1, norm = call(
        middle,
        [whole, (8, 8, LANES), level0, level0, (16, 16, LANES), (8, LANES)],
        message, place, inverse, f2, i2, v2, f1, i1, v1, fr, fb, ir, ib, vb,
        scratch=work,
    )
    f1, v1, f2, v2, message = call(
        down12_next,
        [level1] * 2 + [level2] * 2 + [(256, LANES)],
        *exchange1(own1),
        i1,
        i2,
        scratch=[line],
    )
    message = lax.all_to_all(message, AXES, 0, 0, tiled=True)
    field, sums = call(
        final,
        [(32, 32, LANES), (128, LANES)],
        message, place, inverse, f2, i2, v2, f1, i1, v1, fr, fb, ir, ib, bnew, i3, i4, norm,
        scratch=work + [level0],
    )
    sums = lax.all_to_all(sums, AXES, 0, 0, tiled=True)
    squares = jnp.sum(sums.reshape(128, 2, 64), axis=(0, 2))
    return field, jnp.sqrt(squares / CELLS)


def solution(mesh):
    return jax.shard_map(
        local,
        mesh=mesh,
        in_specs=(P("gx", "gy", "gz"), P("gx", "gy", "gz"), P(("gx", "gy", "gz"), None)),
        out_specs=(P("gx", "gy", "gz"), P()),
        check_vma=False,
    )
```

time: 1220 us -> 254 us (0.21)
  starting transfers between devices: 422 us -> 32.1 us
  local copies, waits for them, and re-layouts: 249 us -> 12.9 us
  waiting for transfers between devices: 256 us -> 65.6 us
  blocking collectives: 203 us -> 30 us
  Pallas kernels: 0 us -> 97.1 us
  other arithmetic: 75.6 us -> 1.43 us
    ppermute x282 -> x18, starting transfers between devices: 422 us -> 26.2 us  [exchange(): return (lax.ppermute(to_high, axis, up), lax.ppermute(to_low, axis, down))]
    ppermute x282 -> x18, waiting for transfers between devices: 256 us -> 57.9 us  [exchange(): return (lax.ppermute(to_high, axis, up), lax.ppermute(to_low, axis, down))]
    reshape x17 -> x0, local copies, waits for them, and re-layouts: 178 us -> none  [the longest x9 119 us: coarsen(): values.reshape(size_x // 2, 2, size_y // 2, 2, size_z // 2, 2)]
    unnamed x2 -> x0, blocking collectives: 135 us -> none
    pallas_call x0 -> x8, Pallas kernels: none -> 97.1 us  [call(): pl.pallas_call(body, out_shape=[jax.ShapeDtypeStruct(shape, F32) for shap...]
    psum x1 -> x0, blocking collectives: 67.7 us -> none  [local(): squares = lax.psum(jnp.sum(remainder * remainder), ('gx', 'gy', 'gz'))]
    reduce_sum x18 -> x2, other arithmetic: 48 us -> 0.27 us  [local(): squares = jnp.sum(sums.reshape(128, 2, 64), axis=(0, 2))]
    all_to_all x0 -> x2, blocking collectives: none -> 30 us  [the longest x1 15.8 us: local(): message = lax.all_to_all(message, AXES, 0, 0, tiled=True)]
  transfers between devices with their start and end apart: 282 -> 20, of which waited for: 249 -> 16; matrix products, arithmetic and copies ran while one was open for 11% -> 2% of each run, Pallas kernels for 0% -> 15%
where the time goes in v1:
time: 254 us; the launch traced here: 253 us
  Pallas kernels  97.1 us (38%)
  waiting for transfers between devices  65.6 us (26%)
  starting transfers between devices  32.1 us (13%)
  blocking collectives  30 us (12%)
  between operations  14.3 us (6%)
  local copies, waits for them, and re-layouts  12.9 us (5%)
    pallas_call x8, Pallas kernels, call(): pl.pallas_call(body, out_shape=[jax.ShapeDtypeStruct(shape, F32) for shap...  97.1 us
    ppermute x18, waiting for transfers between devices, exchange(): return (lax.ppermute(to_high, axis, up), lax.ppermute(to_low, axis, down))  57.9 us
    ppermute x18, starting transfers between devices, exchange(): return (lax.ppermute(to_high, axis, up), lax.ppermute(to_low, axis, down))  26.2 us
    all_to_all x1, blocking collectives, local(): message = lax.all_to_all(message, AXES, 0, 0, tiled=True)  15.8 us
    all_to_all x1, blocking collectives, local(): sums = lax.all_to_all(sums, AXES, 0, 0, tiled=True)  14.2 us
    unnamed x48, local copies, waits for them, and re-layouts  9.59 us
    all_to_all x1, waiting for transfers between devices, local(): message = lax.all_to_all(message, AXES, 0, 0, tiled=True)  7.65 us
    all_to_all x1, starting transfers between devices, local(): message = lax.all_to_all(message, AXES, 0, 0, tiled=True)  5.89 us
  transfers between devices with their start and end apart: 20, of which 16 were waited for; matrix products, arithmetic and copies ran while one was open for 2% of the time, Pallas kernels for 15%

profile of v1, /device:TPU:1, one launch (start us, length us, event | category | flops | bytes accessed | tf_op | source)
XLA Modules:
  0.0 253.4 jit_solution(11717135871436585720)
XLA Ops:
  12.2 5.8 %collective-permute-done.low = f32[16,32,128]{2,1,0:T(8,128)S(1)} collective-permute-done((f32[16,32,128]{2,1,0:T(8,128)S(1)}, f32[16,32,128]{2,1,0:T(8,128)S(1)}, u32[]{:S(2)}, u32[]{:S(2)}) %collective-permute-start) | collective-permute-done | bytes 262176 | tf_op jit(solution)/shard_map/ppermute | solution.py:529
  20.6 6.9 %collective-permute-done.3.above = f32[96,8,128]{2,1,0:T(8,128)S(1)} collective-permute-done((f32[96,8,128]{2,1,0:T(8,128)S(1)}, f32[96,8,128]{2,1,0:T(8,128)S(1)}, u32[]{:S(2)}, u32[]{:S(2)}) %collective-permute-start.3) | collective-permute-done | bytes 393248 | tf_op jit(solution)/shard_map/ppermute | solution.py:529
  27.5 3.1 %collective-permute-done.2.below = f32[96,8,128]{2,1,0:T(8,128)S(1)} collective-permute-done((f32[96,8,128]{2,1,0:T(8,128)S(1)}, f32[96,8,128]{2,1,0:T(8,128)S(1)}, u32[]{:S(2)}, u32[]{:S(2)}) %collective-permute-start.2) | collective-permute-done | bytes 393248 | tf_op jit(solution)/shard_map/ppermute | solution.py:529
  31.3 3.5 %shard_map.50 = (f32[6,48,128]{2,1,0:T(8,128)}, f32[6,48,128]{2,1,0:T(8,128)}) custom-call(f32[32,32,128]{2,1,0:T(8,128)} %f.3, f32[32,32,128]{2,1,0:T(8,128)} %s.3, f32[16,32,128]{2,1,0:T(8,128)} %copy-done.4, f32[16,32,128]{2,1,0:T(8,128)} %copy-done.5, f32[96,8,128]{2,1,0:T(8,128)} %copy-done.7, f32[96,8,128]{2,1,0:T(8,128)} %copy-done.6), custom_call_target="tpu_custom_call" | custom-call | tf_op jit(solution)/shard_map/pallas_call | solution.py:50
  34.9 4.3 %collective-permute-start.4 = (f32[6,48,128]{2,1,0:T(8,128)}, f32[6,48,128]{2,1,0:T(8,128)S(1)}, u32[]{:S(2)}, u32[]{:S(2)}) collective-permute-start(f32[6,48,128]{2,1,0:T(8,128)} %get-tuple-element.33), channel_id=1, source_target_pairs={{0,1},{1,2},{2,3},{3,4},{4,5},{5,6},{6,7},{7,0},{8,9},{9,10},{10,1... | collective-permute-start | bytes 442376 | tf_op jit(solution)/shard_map/ppermute | solution.py:529
  44.8 18.7 %shard_map.51 = (f32[48,48,128]{2,1,0:T(8,128)}, f32[48,48,128]{2,1,0:T(8,128)}, f32[48,48,128]{2,1,0:T(8,128)}, f32[48,48,128]{2,1,0:T(8,128)}, f32[48,48,128]{2,1,0:T(8,128)}, /*index=5*/f32[16,16,128]{2,1,0:T(8,128)}) custom-call(f32[32,32,128]{2,1,0:T(8,128)} %f.3, f32[32,32,128]{2,1,0:T(8,128)} %s.3, f32[16,32,128]{2,1,0:T(8,128)} %copy-done.4, ...), custom_call_target="tpu_custom_call" | custom-call | tf_op jit(solution)/shard_map/pallas_call | solution.py:50
  67.3 3.2 %collective-permute-done.6 = f32[14,16,128]{2,1,0:T(8,128)S(1)} collective-permute-done((f32[14,16,128]{2,1,0:T(8,128)S(1)}, f32[14,16,128]{2,1,0:T(8,128)S(1)}, u32[]{:S(2)}, u32[]{:S(2)}) %collective-permute-start.6) | collective-permute-done | bytes 114720 | tf_op jit(solution)/shard_map/ppermute | solution.py:529
  73.0 9.3 %collective-permute-done.9.above = f32[44,16,128]{2,1,0:T(8,128)S(1)} collective-permute-done((f32[44,16,128]{2,1,0:T(8,128)S(1)}, f32[44,16,128]{2,1,0:T(8,128)S(1)}, u32[]{:S(2)}, u32[]{:S(2)}) %collective-permute-start.9) | collective-permute-done | bytes 360480 | tf_op jit(solution)/shard_map/ppermute | solution.py:529
  83.9 2.9 %shard_map.52 = (f32[11,48,128]{2,1,0:T(8,128)}, f32[11,48,128]{2,1,0:T(8,128)}) custom-call(f32[44,16,128]{2,1,0:T(8,128)} %copy-done.2, f32[44,16,128]{2,1,0:T(8,128)} %copy-done.10, f32[44,16,128]{2,1,0:T(8,128)} %copy-done.8), custom_call_target="tpu_custom_call" | custom-call | tf_op jit(solution)/shard_map/pallas_call | solution.py:50
  86.7 3.6 %collective-permute-start.10 = (f32[11,48,128]{2,1,0:T(8,128)}, f32[11,48,128]{2,1,0:T(8,128)S(1)}, u32[]{:S(2)}, u32[]{:S(2)}) collective-permute-start(f32[11,48,128]{2,1,0:T(8,128)} %get-tuple-element.36), channel_id=1, source_target_pairs={{0,1},{1,2},{2,3},{3,4},{4,5},{5,6},{6,7},{7,0},{8,9},{9,10},{10,1... | collective-permute-start | bytes 811016 | tf_op jit(solution)/shard_map/ppermute | solution.py:529
  90.3 3.7 %collective-permute-done.10.from_low = f32[11,48,128]{2,1,0:T(8,128)S(1)} collective-permute-done((f32[11,48,128]{2,1,0:T(8,128)}, f32[11,48,128]{2,1,0:T(8,128)S(1)}, u32[]{:S(2)}, u32[]{:S(2)}) %collective-permute-start.10) | collective-permute-done | bytes 270368 | tf_op jit(solution)/shard_map/ppermute | solution.py:529
  97.1 13.6 %shard_map.53 = (f32[44,48,128]{2,1,0:T(8,128)}, f32[44,48,128]{2,1,0:T(8,128)}, f32[44,48,128]{2,1,0:T(8,128)}, f32[20,24,128]{2,1,0:T(8,128)}, f32[20,24,128]{...) custom-call(f32[44,16,128]{2,1,0:T(8,128)} %copy-done.2, f32[44,16,128]{2,1,0:T(8,128)} %copy-done.10, ...), custom_call_target="tpu_custom_call" | custom-call | tf_op jit(solution)/shard_map/pallas_call | solution.py:50
  110.8 5.9 %all-to-all-start = ((f32[128,4,128]{2,1,0:T(4,128)}), f32[128,4,128]{2,1,0:T(4,128)S(1)}, u32[]{:S(2)}, u32[]{:S(2)}) async-start(f32[128,4,128]{2,1,0:T(4,128)} %bitcast.13), calls=%async_computation | async-start | bytes 524288 | tf_op jit(solution)/shard_map/all_to_all | solution.py:571
  119.9 7.7 %all-to-all-done = f32[128,4,128]{2,1,0:T(4,128)S(1)} async-done(((f32[128,4,128]{2,1,0:T(4,128)}), f32[128,4,128]{2,1,0:T(4,128)S(1)}, u32[]{:S(2)}, u32[]{:S(2)}) %all-to-all-start) | async-done | bytes 262176 | tf_op jit(solution)/shard_map/all_to_all | solution.py:571
  128.3 25.1 %shard_map.54 = (f32[16,16,128]{2,1,0:T(8,128)}, f32[8,8,128]{2,1,0:T(8,128)}, f32[48,48,128]{2,1,0:T(8,128)}, f32[48,48,128]{2,1,0:T(8,128)}, f32[16,16,128]{2,1,0:T(8,128)}, /*index=5*/f32[8,128]{1,0:T(8,128)}) custom-call(f32[512,128]{1,0:T(8,128)} %bitcast.11, s32[3]{0:T(128)} %pad_add_fusion.place, f32[512,512]{1,0:T(8,128)} %reshape.13.inverse, ...), custom_call_target="tpu_custom_call" | custom-call | tf_op jit(solution)/shard_map/pallas_call | solution.py:50
  161.9 6.2 %collective-permute-done.15.above = f32[44,16,128]{2,1,0:T(8,128)S(1)} collective-permute-done((f32[44,16,128]{2,1,0:T(8,128)S(1)}, f32[44,16,128]{2,1,0:T(8,128)S(1)}, u32[]{:S(2)}, u32[]{:S(2)}) %collective-permute-start.15) | collective-permute-done | bytes 360480 | tf_op jit(solution)/shard_map/ppermute | solution.py:529
  168.2 3.1 %collective-permute-done.14.below = f32[44,16,128]{2,1,0:T(8,128)S(1)} collective-permute-done((f32[44,16,128]{2,1,0:T(8,128)S(1)}, f32[44,16,128]{2,1,0:T(8,128)S(1)}, u32[]{:S(2)}, u32[]{:S(2)}) %collective-permute-start.14) | collective-permute-done | bytes 360480 | tf_op jit(solution)/shard_map/ppermute | solution.py:529
  172.0 2.8 %shard_map.55 = (f32[11,48,128]{2,1,0:T(8,128)}, f32[11,48,128]{2,1,0:T(8,128)}) custom-call(f32[44,16,128]{2,1,0:T(8,128)} %copy-done.3, f32[44,16,128]{2,1,0:T(8,128)} %copy-done.11, f32[44,16,128]{2,1,0:T(8,128)} %copy-done.9), custom_call_target="tpu_custom_call" | custom-call | tf_op jit(solution)/shard_map/pallas_call | solution.py:50
  174.9 3.4 %collective-permute-start.16 = (f32[11,48,128]{2,1,0:T(8,128)}, f32[11,48,128]{2,1,0:T(8,128)S(1)}, u32[]{:S(2)}, u32[]{:S(2)}) collective-permute-start(f32[11,48,128]{2,1,0:T(8,128)} %get-tuple-element.51), channel_id=1, source_target_pairs={{0,1},{1,2},{2,3},{3,4},{4,5},{5,6},{6,7},{7,0},{8,9},{9,10},{10,1... | collective-permute-start | bytes 811016 | tf_op jit(solution)/shard_map/ppermute | solution.py:529
  178.3 3.7 %collective-permute-done.16.from_low = f32[11,48,128]{2,1,0:T(8,128)S(1)} collective-permute-done((f32[11,48,128]{2,1,0:T(8,128)}, f32[11,48,128]{2,1,0:T(8,128)S(1)}, u32[]{:S(2)}, u32[]{:S(2)}) %collective-permute-start.16) | collective-permute-done | bytes 270368 | tf_op jit(solution)/shard_map/ppermute | solution.py:529
  185.2 10.7 %shard_map.56 = (f32[44,48,128]{2,1,0:T(8,128)}, f32[44,48,128]{2,1,0:T(8,128)}, f32[20,24,128]{2,1,0:T(8,128)}, f32[20,24,128]{2,1,0:T(8,128)}, f32[256,128]{1,0:T(8,128)}) custom-call(f32[44,16,128]{2,1,0:T(8,128)} %copy-done.3, f32[44,16,128]{2,1,0:T(8,128)} %copy-done.11, f32[44,16,128]{2,1,0:T(8,128)} %copy-done.9, f32[11,48,128]{2,1,0:T(8,128)} %copy-done.14, ...), custom_call_target="tpu_custom_call" | custom-call | tf_op jit(solution)/shard_map/pallas_call | solution.py:50
  195.9 15.8 %all_to_all.31 = f32[128,2,128]{2,1,0:T(2,128)} all-to-all(f32[128,2,128]{2,1,0:T(2,128)} %bitcast.14), channel_id=1, replica_groups=mesh['gx'=4,'gy'=4,'gz'=8] {'gx','gy','gz'}, dimensions={0} | all-to-all | bytes 262144 | tf_op jit(solution)/shard_map/all_to_all | solution.py:588
  211.7 19.7 %shard_map.57 = (f32[32,32,128]{2,1,0:T(8,128)}, f32[128,128]{1,0:T(8,128)}) custom-call(f32[256,128]{1,0:T(8,128)} %bitcast.12, s32[3]{0:T(128)} %pad_add_fusion.place, f32[512,512]{1,0:T(8,128)} %reshape.13.inverse, f32[20,24,128]{2,1,0:T(8,128)} %get-tuple-element.54.f2, f32[20,24,128]{2,1,0:T(8,128)} %get-tuple-element.40.i2, ...), custom_call_target="tpu_custom_call" | custom-call | tf_op jit(solution)/shard_map/pallas_call | solution.py:50
  231.5 14.2 %all_to_all.32 = f32[128,1,128]{2,1,0:T(1,128)S(1)} all-to-all(f32[128,1,128]{2,1,0:T(1,128)} %bitcast.15), channel_id=1, replica_groups=mesh['gx'=4,'gy'=4,'gz'=8] {'gx','gy','gz'}, dimensions={0} | all-to-all | bytes 131072 | tf_op jit(solution)/shard_map/all_to_all | solution.py:595
  (88 shorter events, 42.1 us)
Async XLA Ops:
  7.2 110.1 %all-gather.3.cloned.1.call-start = ((), (), s32[]{:S(2)}) async-start(), calls=%async_computation.3 | async-start | bytes 1056768 | tf_op jit(solution)/shard_map/all_gather | solution.py:543
  8.4 9.5 %collective-permute-start = (f32[16,32,128]{2,1,0:T(8,128)S(1)}, f32[16,32,128]{2,1,0:T(8,128)S(1)}, u32[]{:S(2)}, u32[]{:S(2)}) collective-permute-start(f32[16,32,128]{2,1,0:T(8,128)S(1)} %pad_maximum_fusion), channel_id=1, source_target_pairs={{0,32},{32,64},{64,96},{96,0},{1,33},{33,65},{65,97},{97,1},{2,34}... | collective-permute-start | bytes 786440 | tf_op jit(solution)/shard_map/ppermute | solution.py:529
  10.7 7.3 %collective-permute-start.1 = (f32[16,32,128]{2,1,0:T(8,128)S(1)}, f32[16,32,128]{2,1,0:T(8,128)S(1)}, u32[]{:S(2)}, u32[]{:S(2)}) collective-permute-start(f32[16,32,128]{2,1,0:T(8,128)S(1)} %pad_maximum_fusion.1), channel_id=1, source_target_pairs={{32,0},{64,32},{96,64},{0,96},{33,1},{65,33},{97,65},{1,97},{34,2}... | collective-permute-start | bytes 786440 | tf_op jit(solution)/shard_map/ppermute | solution.py:529
  18.0 12.6 %copy-start.4 = (f32[16,32,128]{2,1,0:T(8,128)}, f32[16,32,128]{2,1,0:T(8,128)S(1)}, u32[]{:S(2)}) copy-start(f32[16,32,128]{2,1,0:T(8,128)S(1)} %collective-permute-done.low) | copy-start | bytes 786436
  18.0 12.6 %copy-start.5 = (f32[16,32,128]{2,1,0:T(8,128)}, f32[16,32,128]{2,1,0:T(8,128)S(1)}, u32[]{:S(2)}) copy-start(f32[16,32,128]{2,1,0:T(8,128)S(1)} %collective-permute-done.1.high) | copy-start | bytes 786436
  18.1 9.3 %collective-permute-start.3 = (f32[96,8,128]{2,1,0:T(8,128)S(1)}, f32[96,8,128]{2,1,0:T(8,128)S(1)}, u32[]{:S(2)}, u32[]{:S(2)}) collective-permute-start(f32[96,8,128]{2,1,0:T(8,128)S(1)} %get-tuple-element.72), channel_id=1, source_target_pairs={{8,0},{16,8},{24,16},{0,24},{9,1},{17,9},{25,17},{1,25},{10,2},{18... | collective-permute-start | bytes 1179656 | tf_op jit(solution)/shard_map/ppermute | solution.py:529
  20.6 10.0 %collective-permute-start.2 = (f32[96,8,128]{2,1,0:T(8,128)S(1)}, f32[96,8,128]{2,1,0:T(8,128)S(1)}, u32[]{:S(2)}, u32[]{:S(2)}) collective-permute-start(f32[96,8,128]{2,1,0:T(8,128)S(1)} %get-tuple-element.73), channel_id=1, source_target_pairs={{0,8},{8,16},{16,24},{24,0},{1,9},{9,17},{17,25},{25,1},{2,10},{10... | collective-permute-start | bytes 1179656 | tf_op jit(solution)/shard_map/ppermute | solution.py:529
  34.9 6.7 %collective-permute-start.4 = (f32[6,48,128]{2,1,0:T(8,128)}, f32[6,48,128]{2,1,0:T(8,128)S(1)}, u32[]{:S(2)}, u32[]{:S(2)}) collective-permute-start(f32[6,48,128]{2,1,0:T(8,128)} %get-tuple-element.33), channel_id=1, source_target_pairs={{0,1},{1,2},{2,3},{3,4},{4,5},{5,6},{6,7},{7,0},{8,9},{9,10},{10,1... | collective-permute-start | bytes 442376 | tf_op jit(solution)/shard_map/ppermute | solution.py:529
  39.1 5.0 %collective-permute-start.5 = (f32[6,48,128]{2,1,0:T(8,128)}, f32[6,48,128]{2,1,0:T(8,128)S(1)}, u32[]{:S(2)}, u32[]{:S(2)}) collective-permute-start(f32[6,48,128]{2,1,0:T(8,128)} %get-tuple-element.34), channel_id=1, source_target_pairs={{1,0},{2,1},{3,2},{4,3},{5,4},{6,5},{7,6},{0,7},{9,8},{10,9},{11,1... | collective-permute-start | bytes 442376 | tf_op jit(solution)/shard_map/ppermute | solution.py:529
  64.5 6.0 %collective-permute-start.6 = (f32[14,16,128]{2,1,0:T(8,128)S(1)}, f32[14,16,128]{2,1,0:T(8,128)S(1)}, u32[]{:S(2)}, u32[]{:S(2)}) collective-permute-start(f32[14,16,128]{2,1,0:T(8,128)S(1)} %get-tuple-element.83), channel_id=1, source_target_pairs={{0,32},{32,64},{64,96},{96,0},{1,33},{33,65},{65,97},{97,1},{2,34}... | collective-permute-start | bytes 344072 | tf_op jit(solution)/shard_map/ppermute | solution.py:529
  65.7 5.8 %collective-permute-start.7 = (f32[14,16,128]{2,1,0:T(8,128)S(1)}, f32[14,16,128]{2,1,0:T(8,128)S(1)}, u32[]{:S(2)}, u32[]{:S(2)}) collective-permute-start(f32[14,16,128]{2,1,0:T(8,128)S(1)} %get-tuple-element.82), channel_id=1, source_target_pairs={{32,0},{64,32},{96,64},{0,96},{33,1},{65,33},{97,65},{1,97},{34,2}... | collective-permute-start | bytes 344072 | tf_op jit(solution)/shard_map/ppermute | solution.py:529
  71.5 11.6 %copy-start.2 = (f32[44,16,128]{2,1,0:T(8,128)}, f32[44,16,128]{2,1,0:T(8,128)S(1)}, u32[]{:S(2)}) copy-start(f32[44,16,128]{2,1,0:T(8,128)S(1)} %constant_dynamic-update-slice_fusion.8.own) | copy-start | bytes 1081348
  71.5 10.8 %collective-permute-start.9 = (f32[44,16,128]{2,1,0:T(8,128)S(1)}, f32[44,16,128]{2,1,0:T(8,128)S(1)}, u32[]{:S(2)}, u32[]{:S(2)}) collective-permute-start(f32[44,16,128]{2,1,0:T(8,128)S(1)} %constant_dynamic-update-slice_fusion.8.own), channel_id=1, source_target_pairs={{8,0},{16,8},{24,16},{0,24},{9,1},{17,9},{25,17},{1,25},{10,2},{18... | collective-permute-start | bytes 1081352 | tf_op jit(solution)/shard_map/ppermute | solution.py:529
  71.8 11.3 %collective-permute-start.8 = (f32[44,16,128]{2,1,0:T(8,128)S(1)}, f32[44,16,128]{2,1,0:T(8,128)S(1)}, u32[]{:S(2)}, u32[]{:S(2)}) collective-permute-start(f32[44,16,128]{2,1,0:T(8,128)S(1)} %constant_dynamic-update-slice_fusion.8.own), channel_id=1, source_target_pairs={{0,8},{8,16},{16,24},{24,0},{1,9},{9,17},{17,25},{25,1},{2,10},{10... | collective-permute-start | bytes 1081352 | tf_op jit(solution)/shard_map/ppermute | solution.py:529
  86.7 7.3 %collective-permute-start.10 = (f32[11,48,128]{2,1,0:T(8,128)}, f32[11,48,128]{2,1,0:T(8,128)S(1)}, u32[]{:S(2)}, u32[]{:S(2)}) collective-permute-start(f32[11,48,128]{2,1,0:T(8,128)} %get-tuple-element.36), channel_id=1, source_target_pairs={{0,1},{1,2},{2,3},{3,4},{4,5},{5,6},{6,7},{7,0},{8,9},{9,10},{10,1... | collective-permute-start | bytes 811016 | tf_op jit(solution)/shard_map/ppermute | solution.py:529
  90.3 6.1 %collective-permute-start.11 = (f32[11,48,128]{2,1,0:T(8,128)}, f32[11,48,128]{2,1,0:T(8,128)S(1)}, u32[]{:S(2)}, u32[]{:S(2)}) collective-permute-start(f32[11,48,128]{2,1,0:T(8,128)} %get-tuple-element.37), channel_id=1, source_target_pairs={{1,0},{2,1},{3,2},{4,3},{5,4},{6,5},{7,6},{0,7},{9,8},{10,9},{11,1... | collective-permute-start | bytes 811016 | tf_op jit(solution)/shard_map/ppermute | solution.py:529
  110.8 16.8 %all-to-all-start = ((f32[128,4,128]{2,1,0:T(4,128)}), f32[128,4,128]{2,1,0:T(4,128)S(1)}, u32[]{:S(2)}, u32[]{:S(2)}) async-start(f32[128,4,128]{2,1,0:T(4,128)} %bitcast.13), calls=%async_computation | async-start | bytes 524288 | tf_op jit(solution)/shard_map/all_to_all | solution.py:571
  154.4 4.9 %collective-permute-start.12 = (f32[14,16,128]{2,1,0:T(8,128)S(1)}, f32[14,16,128]{2,1,0:T(8,128)S(1)}, u32[]{:S(2)}, u32[]{:S(2)}) collective-permute-start(f32[14,16,128]{2,1,0:T(8,128)S(1)} %get-tuple-element.81), channel_id=1, source_target_pairs={{0,32},{32,64},{64,96},{96,0},{1,33},{33,65},{65,97},{97,1},{2,34}... | collective-permute-start | bytes 344072 | tf_op jit(solution)/shard_map/ppermute | solution.py:529
  154.8 5.4 %collective-permute-start.13 = (f32[14,16,128]{2,1,0:T(8,128)S(1)}, f32[14,16,128]{2,1,0:T(8,128)S(1)}, u32[]{:S(2)}, u32[]{:S(2)}) collective-permute-start(f32[14,16,128]{2,1,0:T(8,128)S(1)} %get-tuple-element.80), channel_id=1, source_target_pairs={{32,0},{64,32},{96,64},{0,96},{33,1},{65,33},{97,65},{1,97},{34,2}... | collective-permute-start | bytes 344072 | tf_op jit(solution)/shard_map/ppermute | solution.py:529
  160.2 11.1 %copy-start.3 = (f32[44,16,128]{2,1,0:T(8,128)}, f32[44,16,128]{2,1,0:T(8,128)S(1)}, u32[]{:S(2)}) copy-start(f32[44,16,128]{2,1,0:T(8,128)S(1)} %constant_dynamic-update-slice_fusion.11.own) | copy-start | bytes 1081348
  160.2 7.9 %collective-permute-start.15 = (f32[44,16,128]{2,1,0:T(8,128)S(1)}, f32[44,16,128]{2,1,0:T(8,128)S(1)}, u32[]{:S(2)}, u32[]{:S(2)}) collective-permute-start(f32[44,16,128]{2,1,0:T(8,128)S(1)} %constant_dynamic-update-slice_fusion.11.own), channel_id=1, source_target_pairs={{8,0},{16,8},{24,16},{0,24},{9,1},{17,9},{25,17},{1,25},{10,2},{18... | collective-permute-start | bytes 1081352 | tf_op jit(solution)/shard_map/ppermute | solution.py:529
  161.9 9.4 %collective-permute-start.14 = (f32[44,16,128]{2,1,0:T(8,128)S(1)}, f32[44,16,128]{2,1,0:T(8,128)S(1)}, u32[]{:S(2)}, u32[]{:S(2)}) collective-permute-start(f32[44,16,128]{2,1,0:T(8,128)S(1)} %constant_dynamic-update-slice_fusion.11.own), channel_id=1, source_target_pairs={{0,8},{8,16},{16,24},{24,0},{1,9},{9,17},{17,25},{25,1},{2,10},{10... | collective-permute-start | bytes 1081352 | tf_op jit(solution)/shard_map/ppermute | solution.py:529
  174.9 7.1 %collective-permute-start.16 = (f32[11,48,128]{2,1,0:T(8,128)}, f32[11,48,128]{2,1,0:T(8,128)S(1)}, u32[]{:S(2)}, u32[]{:S(2)}) collective-permute-start(f32[11,48,128]{2,1,0:T(8,128)} %get-tuple-element.51), channel_id=1, source_target_pairs={{0,1},{1,2},{2,3},{3,4},{4,5},{5,6},{6,7},{7,0},{8,9},{9,10},{10,1... | collective-permute-start | bytes 811016 | tf_op jit(solution)/shard_map/ppermute | solution.py:529
  178.3 6.2 %collective-permute-start.17 = (f32[11,48,128]{2,1,0:T(8,128)}, f32[11,48,128]{2,1,0:T(8,128)S(1)}, u32[]{:S(2)}, u32[]{:S(2)}) collective-permute-start(f32[11,48,128]{2,1,0:T(8,128)} %get-tuple-element.52), channel_id=1, source_target_pairs={{1,0},{2,1},{3,2},{4,3},{5,4},{6,5},{7,6},{0,7},{9,8},{10,9},{11,1... | collective-permute-start | bytes 811016 | tf_op jit(solution)/shard_map/ppermute | solution.py:529
  (15 other events, 40.0 us)
Sparse Core Ops, SparseCore 0:
  20.7 67.9 all-gather.2

commit v2 on v1

v2 whole, which is shorter than its diff:
```python
import jax
import jax.numpy as jnp
import numpy as np
from jax import lax
from jax.experimental import pallas as pl
from jax.experimental.pallas import tpu as pltpu
from jax.sharding import PartitionSpec as P

AXES = ("gx", "gy", "gz")
F32 = jnp.float32
LANES = 128
OWN = 32
H0 = 8
X0, Y0 = 48, 48
H1 = 14
X1, Y1 = 44, 48
H2 = 6
X2, Y2 = 20, 24
GROUP0 = 8
GROUP1 = 4
CELLS = 16777216.0


def iota(shape, dim):
    return lax.broadcasted_iota(jnp.int32, shape, dim)


def roll(value, shift, axis):
    return pltpu.roll(value, shift % value.shape[axis], axis)


def pick(value, index):
    return jnp.take_along_axis(value, index, axis=1, mode="promise_in_bounds")


def loop(start, stop, body, unroll=2):
    def step(index, carry):
        body(index)
        return carry

    lax.fori_loop(start, stop, step, 0, unroll=unroll)


def call(body, outs, *operands, scratch=()):
    specs = [
        pl.BlockSpec(memory_space=pltpu.SMEM if operand.dtype == jnp.int32 else pltpu.VMEM)
        for operand in operands
    ]
    return pl.pallas_call(
        body,
        out_shape=[jax.ShapeDtypeStruct(shape, F32) for shape in outs],
        in_specs=specs,
        out_specs=[pl.BlockSpec(memory_space=pltpu.VMEM)] * len(outs),
        scratch_shapes=[pltpu.VMEM(shape, F32) for shape in scratch],
        compiler_params=pltpu.CompilerParams(vmem_limit_bytes=32 * 1024 * 1024),
    )(*operands)


def lower_matrices():
    matrices = np.zeros((GROUP0, 256, 256), np.float32)
    for k in range(GROUP0):
        for z in range(-8, 136):
            if 0 <= z < 128:
                row = z
            elif z < 0:
                row = 128 + (16 * k + z) % 128
            else:
                row = 128 + 16 * k + z - 128
            matrices[k, row, 128 * (z % 2) + OWN + z // 2] = 1.0
    return matrices


def upper_matrix():
    matrix = np.zeros((256, 128), np.float32)
    for z in range(128):
        matrix[128 * (z % 2) + OWN + z // 2, z] = 1.0
    return matrix


def halo_matrices1():
    matrices = np.zeros((GROUP1, 384, 256), np.float32)
    for k in range(GROUP1):
        for half in (0, 1):
            for z in range(-H1, 64 + H1):
                if 0 <= z < 64:
                    row = (OWN + 64 * half + z) % 128
                elif z < 0:
                    row = 128 + 64 * half + 14 * k + z + H1
                else:
                    row = 256 + 64 * half + 14 * k + z - 64
                matrices[k, row, 128 * half + OWN + z] = 1.0
    return matrices


def thirds(value):
    high = value.astype(jnp.bfloat16)
    rest = value - high.astype(F32)
    mid = rest.astype(jnp.bfloat16)
    return (rest - mid.astype(F32)).astype(jnp.bfloat16), mid, high


def move(pieces, matrix):
    total = None
    for parts in zip(*pieces):
        left = parts[0] if len(parts) == 1 else jnp.concatenate(parts, axis=1)
        term = jnp.dot(left, matrix, preferred_element_type=F32)
        total = term if total is None else total + term
    return total


def plane_pairs(first, last, body, unroll=4):
    def both(i):
        body(2 * i, 0)
        body(2 * i + 1, 1)

    loop(first // 2, last // 2, both, unroll)


def sum0(values, plane, parity, q, onto_red):
    mid, other = values[plane, q], values[plane, 1 - q]
    total = values[plane + 1, q] + values[plane - 1, q] + mid
    total = total + other + roll(other, 1 if q == 0 else -1, 0)
    high = ((parity + q) % 2 == 1) == onto_red
    return total + roll(mid, -1 if high else 1, 1)


def even_lanes(shape, parity):
    return (iota(shape, 1) + parity) % 2 == 0


def sum1(values, plane, parity, onto_red):
    mid = values[plane]
    total = values[plane + 1] + values[plane - 1] + mid
    total = total + roll(mid, 1, 1) + roll(mid, -1, 1)
    less, more = roll(mid, 1, 0), roll(mid, -1, 0)
    first, second = (less, more) if onto_red else (more, less)
    return total + jnp.where(even_lanes(mid.shape, parity), first, second)


def sum2(values, plane):
    mid = values[plane]
    total = values[plane + 1] + values[plane - 1]
    total = total + roll(mid, 1, 0) + roll(mid, -1, 0)
    return total + roll(mid, 1, 1) + roll(mid, -1, 1)


def is_red(shape, plane):
    return (iota(shape, 0) + iota(shape, 1) + plane) % 2 == 0


def pack_z0(f, s, low, high, below, above, split, message, rows):
    block = (iota((Y0, LANES), 1) + 8) % LANES // 16
    for group in range(2 * X0 // GROUP0):
        packed = jnp.zeros((Y0, LANES), F32)
        for k in range(GROUP0):
            item = group * GROUP0 + k
            field, plane = divmod(item, X0)
            own = (f, s)[field]
            slot = item % 16
            rows[slot, 0:8, :] = below[item]
            if plane < H0:
                rows[slot, 8:40, :] = low[field * H0 + plane]
            elif plane < H0 + 32:
                rows[slot, 8:40, :] = own[plane - H0]
            else:
                rows[slot, 8:40, :] = high[field * H0 + plane - H0 - 32]
            rows[slot, 40:48, :] = above[item]
            even = rows[slot, pl.ds(0, 24, stride=2), :]
            odd = rows[slot, pl.ds(1, 24, stride=2), :]
            value = jnp.concatenate([even, odd], axis=0)
            split[item] = value
            packed = jnp.where(block == k, roll(value, 16 * k, 1), packed)
        message[group] = packed


def down0(split, from_low, from_high, matrices, fr, fb, ir, ib, vb, own1, red, screen):
    lane = iota((Y0, LANES), 1)
    groups = 2 * X0 // GROUP0
    merged = [
        jnp.where(lane // 8 % 2 == 1, from_low[group], from_high[group]) for group in range(groups)
    ]
    merged = thirds(jnp.concatenate(merged, axis=0))
    for k in range(GROUP0):
        own = [split[group * GROUP0 + k] for group in range(groups)]
        result = move([thirds(jnp.concatenate(own, axis=0)), merged], matrices[k])
        for group in range(groups):
            field, plane = divmod(group * GROUP0 + k, X0)
            part = result[Y0 * group : Y0 * group + Y0]
            even, odd = part[:, :LANES], part[:, LANES:]
            if field == 1:
                screen[plane] = even[:24] + odd[:24] + even[24:] + odd[24:]
            for q in (0, 1):
                reds, blacks = (even, odd) if (k + q) % 2 == 0 else (odd, even)
                reds, blacks = reds[24 * q : 24 * q + 24], blacks[24 * q : 24 * q + 24]
                if field == 0:
                    fr[plane, q] = reds
                    fb[plane, q] = blacks
                else:
                    ir[plane, q] = 1.0 / (6.0 + reds)
                    ib[plane, q] = 1.0 / (6.0 + blacks)

    def first(p):
        red[p] = fr[p] * ir[p]

    loop(0, X0, first, 4)

    def black(p, parity):
        for q in (0, 1):
            vb[p, q] = (fb[p, q] + sum0(red, p, parity, q, False)) * ib[p, q]

    black(1, 1)
    plane_pairs(2, X0 - 2, black)
    black(X0 - 2, 0)

    def restrict(i):
        plane = 2 * i + H0
        source = 0.5 * below_sum(vb, plane)
        own = (iota((16, LANES), 1) + 128 - OWN) % LANES < 64
        screens = 0.5 * (screen[plane] + screen[plane + 1])[4:20]
        own1[i] = jnp.where(own, source[4:20], roll(screens, 64, 1))

    loop(0, 16, restrict)


def below_sum(values, plane):
    total = sum0(values, plane, 0, 0, True) + sum0(values, plane, 0, 1, True)
    total = total + sum0(values, plane + 1, 1, 0, True)
    return total + sum0(values, plane + 1, 1, 1, True)


def pack_z1(own, below, above, coloured, to_high, to_low):
    block = iota((24, LANES), 1) % 64 // 14
    for group in range(own.shape[0] // GROUP1):
        up = [jnp.zeros((24, LANES), F32)] * 2
        down = [jnp.zeros((24, LANES), F32)] * 2
        for k in range(GROUP1):
            item = group * GROUP1 + k
            even, odd = [
                jnp.concatenate([ref[item, pl.ds(q, 8, stride=2), :] for ref in (below, own, above)], axis=0)
                for q in (0, 1)
            ]
            here = even_lanes((24, LANES), item)
            for colour in (0, 1):
                first, second = (even, odd) if colour == 0 else (odd, even)
                value = jnp.where(here, first, second)
                coloured[item, colour] = value
                up[colour] = jnp.where(block == k, roll(value, 14 * k - 82, 1), up[colour])
                down[colour] = jnp.where(block == k, roll(value, 14 * k - 32, 1), down[colour])
        for colour in (0, 1):
            to_high[group, colour] = up[colour]
            to_low[group, colour] = down[colour]


def unpack1(coloured, from_low, from_high, matrices, store):
    items = coloured.shape[0]
    rows = items // GROUP1 * 48
    halos = [thirds(ref[...].reshape(rows, LANES)) for ref in (from_low, from_high)]
    for k in range(GROUP1):
        own = [coloured[item, colour] for item in range(k, items, GROUP1) for colour in (0, 1)]
        result = move([thirds(jnp.concatenate(own, axis=0)), *halos], matrices[k])
        for at in range(items // GROUP1 * 2):
            part = result[24 * at : 24 * at + 24]
            store(at // 2 * GROUP1 + k, at % 2, (part[:, :LANES], part[:, LANES:]))


def pair_index(rows):
    return jnp.clip(2 * iota((rows, LANES), 1) - OWN, 0, 127)


def spread_index(rows):
    return (iota((rows, LANES), 1) - OWN) // 2 + OWN


def coarse12(total):
    pairs = total + roll(total, -1, 1)
    return 0.5 * pick(pairs, pair_index(Y2))


def down12(f1, i1, b1, f2, i2, v2, red):
    def first(p):
        red[p] = f1[p, 0] * i1[p, 0]

    loop(0, X1, first, 4)

    def black(p, parity):
        b1[p] = (f1[p, 1] + sum1(red, p, parity, False)) * i1[p, 1]

    black(1, 1)
    plane_pairs(2, X1 - 2, black)
    black(X1 - 2, 0)

    def restrict(i):
        plane = 2 * i + 2
        f2[i] = coarse12(sum1(b1, plane, 0, True) + sum1(b1, plane + 1, 1, True))

    loop(0, X2, restrict, 4)

    def red2(p):
        v2[p] = jnp.where(is_red((Y2, LANES), p), f2[p] * i2[p], 0.0)

    def black2(p):
        fresh = (f2[p] + sum2(v2, p)) * i2[p]
        v2[p] = jnp.where(is_red((Y2, LANES), p), v2[p], fresh)

    loop(0, X2, red2, 4)
    loop(1, X2 - 1, black2, 3)


def coarse23(total, sums, x3):
    sums[x3] = total
    pairs = sums[x3, pl.ds(8, 8, stride=2), :] + sums[x3, pl.ds(9, 8, stride=2), :]
    pairs = pairs + roll(pairs, -1, 1)
    lane = iota((8, LANES), 1)
    spread = pick(pairs, OWN + 2 * (lane % 16))
    here = lane // 16 == (x3 % 2) * 4 + iota((8, LANES), 0)
    here = jnp.logical_and(here, iota((8, LANES), 0) < 4)
    return 0.5 * jnp.sum(jnp.where(here, spread, 0.0), axis=0, keepdims=True)


def source3(v2, sums):
    rows = []
    for x3 in range(4):
        plane = 2 * x3 + H2
        total = jnp.zeros((Y2, LANES), F32)
        for p in (plane, plane + 1):
            total += jnp.where(is_red((Y2, LANES), p), sum2(v2, p), 0.0)
        rows.append(coarse23(total, sums, x3))
    return [rows[0] + rows[1], rows[2] + rows[3]]


def down12_first(coloured, from_low, from_high, matrices, f1, i1, b1, f2, i2, v2, message, red, sums):
    def store(plane, colour, halves):
        f1[plane, colour], i1[plane, colour] = halves

    unpack1(coloured, from_low, from_high, matrices, store)

    def screen2(i):
        plane = 2 * i + 2
        total = i1[plane, 0] + i1[plane, 1] + i1[plane + 1, 0] + i1[plane + 1, 1]
        i2[i] = coarse12(total)

    loop(0, X2, screen2, 4)
    rows = []
    for x3 in range(4):
        plane = 2 * x3 + H2
        rows.append(coarse23(i2[plane] + i2[plane + 1], sums, x3))

    def invert1(p):
        i1[p] = 1.0 / (6.0 + i1[p])

    def invert2(p):
        i2[p] = 1.0 / (6.0 + i2[p])

    loop(0, X1, invert1, 4)
    loop(0, X2, invert2, 4)
    down12(f1, i1, b1, f2, i2, v2, red)
    tile = jnp.concatenate(source3(v2, sums) + [rows[0] + rows[1], rows[2] + rows[3]], axis=0)
    tile = jnp.concatenate([tile, tile], axis=0)
    for i in range(64):
        message[8 * i : 8 * i + 8, :] = tile


def down12_next(coloured, from_low, from_high, matrices, i1, i2, f1, b1, f2, v2, message, red, sums):
    def store(item, colour, halves):
        block, i = divmod(item, 8)
        for half in (0, 1):
            plane = H1 + 16 * (block - 1) + 8 * half + i
            if 0 <= plane < X1:
                f1[plane, colour] = halves[half]

    unpack1(coloured, from_low, from_high, matrices, store)
    down12(f1, i1, b1, f2, i2, v2, red)
    tile = jnp.concatenate(source3(v2, sums) * 4, axis=0)
    for i in range(32):
        message[8 * i : 8 * i + 8, :] = tile


def unpack3(message, rows, first, into):
    sub, lane = iota((8, LANES), 0), iota((8, LANES), 1)
    for gx in range(4):
        for gy in range(4):
            for half in range(2):
                start = (gx * 4 + gy) * 8 * rows + first + half
                value = message[pl.ds(start, 8, stride=rows), :]
                for k in (1, 2, 4):
                    sub_high = (sub // k) % 2 == 1
                    lane_high = (lane // (16 * k)) % 2 == 1
                    from_below = roll(roll(value, -k, 0), 16 * k, 1)
                    from_above = roll(roll(value, k, 0), -16 * k, 1)
                    value = jnp.where(
                        sub_high == lane_high, value, jnp.where(sub_high, from_above, from_below)
                    )
                for x in range(2):
                    into[gx * 4 + 2 * half + x, gy * 4 : gy * 4 + 4, :] = value[4 * x : 4 * x + 4, :]


def turn(value, shift, axis):
    if axis == 0:
        return jnp.concatenate([value[-shift:], value[:-shift]], axis=0)
    return roll(value, shift, axis)


def sum_whole(value):
    total = turn(value, 1, 0) + turn(value, -1, 0)
    total = total + turn(value, 1, 1) + turn(value, -1, 1)
    return total + turn(value, 1, 2) + turn(value, -1, 2)


def red_whole(shape):
    return (iota(shape, 0) + iota(shape, 1) + iota(shape, 2)) % 2 == 0


def pick3(value, index):
    flat = value.reshape(-1, LANES)
    return pick(flat, jnp.broadcast_to(index, flat.shape)).reshape(value.shape)


def coarse34(value, wide):
    wide[...] = value.reshape(8, 2, 16, LANES).sum(axis=1)
    pairs = wide[:, pl.ds(0, 8, stride=2), :] + wide[:, pl.ds(1, 8, stride=2), :]
    pairs = pairs + roll(pairs, -1, 2)
    return 0.5 * pick3(pairs, 2 * (iota((1, LANES), 1) % 64))


def coarse_solve(f3, i3, i4, inverse, e3, wide):
    red3, red4 = red_whole((16, 16, LANES)), red_whole((8, 8, LANES))
    v3 = jnp.where(red3, f3 * i3, 0.0)
    v3 = jnp.where(red3, v3, (f3 + sum_whole(v3)) * i3)
    f4 = coarse34(jnp.where(red3, sum_whole(v3), 0.0), wide)
    v4 = jnp.where(red4, f4 * i4, 0.0)
    v4 = jnp.where(red4, v4, (f4 + sum_whole(v4)) * i4)
    r4 = jnp.where(red4, sum_whole(v4), 0.0).reshape(4, 2, 8, LANES).sum(axis=1)
    sub, lane = iota((8, LANES), 0), iota((8, LANES), 1)
    rows = []
    for x5 in range(4):
        pairs = r4[x5] + roll(r4[x5], -1, 1)
        spread = jnp.where(sub // 2 == lane // 32, pick(pairs, 2 * (lane % 32)), 0.0)
        rows.append(0.5 * jnp.sum(spread, axis=0, keepdims=True))
    vector = jnp.broadcast_to(jnp.concatenate(rows, axis=1), (8, 512))
    answer = lax.dot_general(
        vector,
        inverse[...],
        (((1,), (1,)), ((), ())),
        precision=lax.Precision.HIGHEST,
        preferred_element_type=F32,
    )
    planes = []
    for x5 in range(4):
        part = pick(answer[:, 128 * x5 : 128 * x5 + 128], (sub // 2) * 32 + (lane % 64) // 2)
        planes += [part[None], part[None]]
    w4 = v4 + jnp.concatenate(planes, axis=0)
    w4 = jnp.where(red4, (f4 + sum_whole(w4)) * i4, w4)
    e4 = jnp.where(red4, w4, (f4 + sum_whole(w4)) * i4)
    e4 = pick3(e4, iota((1, LANES), 1) // 2)
    wide[:, pl.ds(0, 8, stride=2), :] = e4
    wide[:, pl.ds(1, 8, stride=2), :] = e4
    spread = jnp.broadcast_to(wide[...][:, None], (8, 2, 16, LANES)).reshape(16, 16, LANES)
    w3 = v3 + spread
    w3 = jnp.where(red3, (f3 + sum_whole(w3)) * i3, w3)
    e3[...] = jnp.where(red3, w3, (f3 + sum_whole(w3)) * i3)


def up21(place, e3, f2, i2, v2, f1, i1, b1, e2, er, eb, tall):
    shift_y = lax.rem(20 - 4 * place[1], 16)
    shift_z = lax.rem(160 - 16 * place[2], 128)

    def from3(i):
        value = e3[lax.rem(4 * place[0] + i + 13, 16)]
        value = pltpu.roll(pltpu.roll(value, shift_y, 0), shift_z, 1)
        value = pick(value, spread_index(16))[:12]
        tall[i, pl.ds(0, 12, stride=2), :] = value
        tall[i, pl.ds(1, 12, stride=2), :] = value
        value = tall[i]
        e2[2 * i] = v2[2 * i] + value
        e2[2 * i + 1] = v2[2 * i + 1] + value

    loop(0, X2 // 2, from3, 5)

    def red2(p):
        fresh = (f2[p] + sum2(e2, p)) * i2[p]
        e2[p] = jnp.where(is_red((Y2, LANES), p), fresh, e2[p])

    def black2(p):
        fresh = (f2[p] + sum2(e2, p)) * i2[p]
        e2[p] = jnp.where(is_red((Y2, LANES), p), e2[p], fresh)

    loop(1, X2 - 1, red2, 3)
    loop(2, X2 - 2, black2, 4)

    def from2(i):
        value = pick(e2[i], spread_index(Y2))
        eb[2 * i + 2] = b1[2 * i + 2] + value
        eb[2 * i + 3] = b1[2 * i + 3] + value

    loop(3, 17, from2, 7)

    def red1(p, parity):
        er[p] = (f1[p, 0] + sum1(eb, p, parity, True)) * i1[p, 0]

    def black1(p, parity):
        eb[p] = (f1[p, 1] + sum1(er, p, parity, False)) * i1[p, 1]

    plane_pairs(8, 36, red1)
    plane_pairs(10, 34, black1)


def add0(er, eb, b, w, tall):
    def from1(i):
        reds, blacks = er[i + 10, 6:18], eb[i + 10, 6:18]
        here = (iota((12, LANES), 1) + i) % 2 == 0
        tall[i, pl.ds(0, 12, stride=2), :] = jnp.where(here, reds, blacks)
        tall[i, pl.ds(1, 12, stride=2), :] = jnp.where(here, blacks, reds)
        value = tall[i]
        for p in (2 * i, 2 * i + 1):
            for q in (0, 1):
                w[p, q] = b[p, q] + value

    loop(0, X0 // 2, from1, 4)


def own_sum(total):
    row, lane = iota((24, LANES), 0), iota((24, LANES), 1)
    own = jnp.logical_and((row + 20) % 24 < 16, (lane + 128 - OWN) % LANES < 64)
    return jnp.sum(jnp.where(own, total, 0.0), axis=0, keepdims=True)


def sum_over(body):
    def step(i, total):
        return total + body(2 * i, 0) + body(2 * i + 1, 1)

    return lax.fori_loop(H0 // 2, H0 // 2 + 16, step, jnp.zeros((24, LANES), F32), unroll=2)


def middle(
    message, place, inverse, f2, i2, v2, f1, i1, b1, fr, fb, ir, ib, vb,
    i3, i4, bnew, own1, norm,
    f3, e3, wide, tall, e2, er, eb, w, r, rnew,
):
    unpack3(message, 4, 0, f3)
    unpack3(message, 4, 2, e3)
    screen3 = e3[...]
    screen4 = coarse34(screen3, wide)
    i3[...] = 1.0 / (6.0 + screen3)
    i4[...] = 1.0 / (6.0 + screen4)
    coarse_solve(f3[...], i3[...], i4[...], inverse, e3, wide)
    up21(place, e3, f2, i2, v2, f1, i1, b1, e2, er, eb, tall)
    add0(er, eb, vb, w, tall)

    def red_up(p, parity):
        for q in (0, 1):
            r[p, q] = (fr[p, q] + sum0(w, p, parity, q, True)) * ir[p, q]

    plane_pairs(2, X0 - 2, red_up)

    def black_up(p, parity):
        for q in (0, 1):
            w[p, q] = (fb[p, q] + sum0(r, p, parity, q, False)) * ib[p, q]

    black_up(3, 1)
    plane_pairs(4, X0 - 4, black_up)
    black_up(X0 - 4, 0)

    def red_down(p, parity):
        for q in (0, 1):
            rnew[p, q] = (fr[p, q] + sum0(w, p, parity, q, True)) * ir[p, q]

    plane_pairs(4, X0 - 4, red_down)

    def squares(p, parity):
        total = jnp.zeros((24, LANES), F32)
        for q in (0, 1):
            part = (rnew[p, q] - r[p, q]) / ir[p, q]
            total = total + part * part
        return total

    norm[...] = jnp.broadcast_to(own_sum(sum_over(squares)), (8, LANES))

    def black_down(p, parity):
        for q in (0, 1):
            fresh = (fb[p, q] + sum0(rnew, p, parity, q, False)) * ib[p, q]
            bnew[p, q] = fresh
            r[p, q] = fresh - w[p, q]

    black_down(5, 1)
    plane_pairs(6, X0 - 6, black_down)
    black_down(X0 - 6, 0)

    def restrict(i):
        low = 0.5 * below_sum(r, 2 * i + H0)[4:20]
        high = 0.5 * below_sum(r, 2 * i + H0 + 16)[4:20]
        own = (iota((16, LANES), 1) + 128 - OWN) % LANES < 64
        own1[i] = jnp.where(own, low, roll(high, 64, 1))

    loop(0, 8, restrict)


def final(
    message, place, inverse, f2, i2, v2, f1, i1, b1, fr, fb, ir, ib, b, i3, i4, norm, matrix,
    field, sums,
    f3, e3, wide, tall, e2, er, eb, w, r, last,
):
    unpack3(message, 2, 0, f3)
    coarse_solve(f3[...], i3[...], i4[...], inverse, e3, wide)
    up21(place, e3, f2, i2, v2, f1, i1, b1, e2, er, eb, tall)
    add0(er, eb, b, w, tall)

    def red_up(p, parity):
        for q in (0, 1):
            r[p, q] = (fr[p, q] + sum0(w, p, parity, q, True)) * ir[p, q]

    plane_pairs(6, X0 - 6, red_up)

    def black_up(p, parity):
        for q in (0, 1):
            fresh = (fb[p, q] + sum0(r, p, parity, q, False)) * ib[p, q]
            last[p, q] = fresh
            w[p, q] = fresh - w[p, q]

    black_up(7, 1)
    plane_pairs(8, X0 - 8, black_up)
    black_up(X0 - 8, 0)

    def squares(p, parity):
        total = jnp.zeros((24, LANES), F32)
        for q in (0, 1):
            part = sum0(w, p, parity, q, True)
            total = total + part * part
        return total

    after = own_sum(sum_over(squares))

    def finish(i):
        parts = []
        for x in (0, 1):
            for q in (0, 1):
                order = (r, last) if x == q else (last, r)
                parts.append(jnp.concatenate([ref[2 * i + x, q] for ref in order], axis=1))
        result = move([thirds(jnp.concatenate(parts, axis=0))], matrix[...])
        for at in range(4):
            rows = result[24 * at + 4 : 24 * at + 20]
            field[2 * i + at // 2 - H0, pl.ds(at % 2, 16, stride=2), :] = rows

    loop(H0 // 2, H0 // 2 + 16, finish)
    before = norm[0:1, :]
    low = iota((1, LANES), 1) < 64
    both = jnp.where(low, roll(before, -OWN, 1), roll(after, 64 - OWN, 1))
    for i in range(16):
        sums[8 * i : 8 * i + 8, :] = jnp.broadcast_to(both, (8, LANES))


def exchange(to_high, to_low, axis):
    count = lax.axis_size(axis)
    up = [(i, (i + 1) % count) for i in range(count)]
    down = [(j, i) for i, j in up]
    return lax.ppermute(to_high, axis, up), lax.ppermute(to_low, axis, down)


def exchange1(own, low, high):
    from_low, from_high = exchange(high, low, "gx")
    own = jnp.concatenate([from_low, own, from_high], axis=0)
    below, above = exchange(own, own, "gy")
    items = own.shape[0]
    message = (items // GROUP1, 2, 24, LANES)
    coloured, to_high, to_low = call(
        pack_z1, [(items, 2, 24, LANES), message, message], own, below, above
    )
    return coloured, *exchange(to_high, to_low, "gz")


def local(f, s, coarse_inverse):
    inverse = lax.all_gather(coarse_inverse, AXES, axis=0, tiled=True)
    place = jnp.stack([lax.axis_index(axis) for axis in AXES]).astype(jnp.int32)
    low, high = exchange(
        jnp.concatenate([f[32 - H0 :], s[32 - H0 :]], axis=0),
        jnp.concatenate([f[:H0], s[:H0]], axis=0),
        "gx",
    )

    def rows(cut):
        parts = [low[:H0], f, high[:H0], low[H0:], s, high[H0:]]
        return jnp.concatenate([part[:, cut] for part in parts], axis=0)

    below, above = exchange(rows(slice(24, 32)), rows(slice(0, 8)), "gy")
    groups = 2 * X0 // GROUP0
    line0, line1, line2 = (Y0, LANES), (24, LANES), (Y2, LANES)
    split, message = call(
        pack_z0,
        [(2 * X0, *line0), (groups, *line0)],
        *(f, s, low, high, below, above),
        scratch=[(16, *line0)],
    )
    level0, level1, level2 = (X0, 2, *line1), (X1, *line1), (X2, *line2)
    both1 = (X1, 2, *line1)
    matrices1 = jnp.asarray(halo_matrices1(), jnp.bfloat16)
    fr, fb, ir, ib, vb, own1 = call(
        down0,
        [level0] * 5 + [(16, 16, LANES)],
        split,
        *exchange(message, message, "gz"),
        jnp.asarray(lower_matrices(), jnp.bfloat16),
        scratch=[level0, (X0, *line1)],
    )
    f1, i1, b1, f2, i2, v2, message = call(
        down12_first,
        [both1, both1, level1, level2, level2, level2, (512, LANES)],
        *exchange1(own1, own1[:H1], own1[16 - H1 :]),
        matrices1,
        scratch=[level1, (4, *line2)],
    )
    message = lax.all_to_all(message, AXES, 0, 0, tiled=True)
    whole = (16, 16, LANES)
    work = [whole, whole, (8, 16, LANES), (X0 // 2, *line1), level2, level1, level1]
    work += [level0, level0, level0]
    i3, i4, bnew, own1, norm = call(
        middle,
        [whole, (8, 8, LANES), level0, (8, 16, LANES), (8, LANES)],
        message, place, inverse, f2, i2, v2, f1, i1, b1, fr, fb, ir, ib, vb,
        scratch=work,
    )
    f1, b1, f2, v2, message = call(
        down12_next,
        [both1, level1, level2, level2, (256, LANES)],
        *exchange1(own1, own1, own1),
        matrices1,
        i1,
        i2,
        scratch=[level1, (4, *line2)],
    )
    message = lax.all_to_all(message, AXES, 0, 0, tiled=True)
    field, sums = call(
        final,
        [(32, 32, LANES), (128, LANES)],
        message, place, inverse, f2, i2, v2, f1, i1, b1, fr, fb, ir, ib, bnew, i3, i4, norm,
        jnp.asarray(upper_matrix(), jnp.bfloat16),
        scratch=work,
    )
    sums = lax.all_to_all(sums, AXES, 0, 0, tiled=True)
    squares = jnp.sum(sums.reshape(128, 2, 64), axis=(0, 2))
    return field, jnp.sqrt(squares / CELLS)


def solution(mesh):
    return jax.shard_map(
        local,
        mesh=mesh,
        in_specs=(P("gx", "gy", "gz"), P("gx", "gy", "gz"), P(("gx", "gy", "gz"), None)),
        out_specs=(P("gx", "gy", "gz"), P()),
        check_vma=False,
    )
```

time: 254 us -> 197 us (0.78)
  Pallas kernels: 97.1 us -> 38 us
  waiting for transfers between devices: 65.6 us -> 55.6 us
  local copies, waits for them, and re-layouts: 12.9 us -> 17.5 us
  starting transfers between devices: 32.1 us -> 36.3 us
  blocking collectives: 30 us -> 33.4 us
    pallas_call x8, Pallas kernels: 97.1 us -> 38 us  [call(): pl.pallas_call(body, out_shape=[jax.ShapeDtypeStruct(shape, F32) for shap...]
    ppermute x18, waiting for transfers between devices: 57.9 us -> 47.2 us  [exchange(): return (lax.ppermute(to_high, axis, up), lax.ppermute(to_low, axis, down))]
    unnamed x48 -> x62, local copies, waits for them, and re-layouts: 9.59 us -> 16.2 us
    all_to_all x1, starting transfers between devices: 5.89 us -> 9.9 us  [local(): message = lax.all_to_all(message, AXES, 0, 0, tiled=True)]
    all_to_all x1, blocking collectives: 15.8 us -> 19.8 us  [local(): message = lax.all_to_all(message, AXES, 0, 0, tiled=True)]
  transfers between devices with their start and end apart: 20 -> 20, of which waited for: 16 -> 13; matrix products, arithmetic and copies ran while one was open for 2% -> 1% of each run, Pallas kernels for 15% -> 6%
where the time goes in v2:
time: 197 us
  waiting for transfers between devices  55.6 us (28%)
  Pallas kernels  38 us (19%)
  starting transfers between devices  36.3 us (18%)
  blocking collectives  33.4 us (17%)
  local copies, waits for them, and re-layouts  17.5 us (9%)
  between operations  14.3 us (7%)
    ppermute x18, waiting for transfers between devices, exchange(): return (lax.ppermute(to_high, axis, up), lax.ppermute(to_low, axis, down))  47.2 us
    pallas_call x8, Pallas kernels, call(): pl.pallas_call(body, out_shape=[jax.ShapeDtypeStruct(shape, F32) for shap...  38 us
    ppermute x18, starting transfers between devices, exchange(): return (lax.ppermute(to_high, axis, up), lax.ppermute(to_low, axis, down))  26.4 us
    all_to_all x1, blocking collectives, local(): message = lax.all_to_all(message, AXES, 0, 0, tiled=True)  19.8 us
    unnamed x62, local copies, waits for them, and re-layouts  16.2 us
    all_to_all x1, blocking collectives, local(): sums = lax.all_to_all(sums, AXES, 0, 0, tiled=True)  13.6 us
    all_to_all x1, starting transfers between devices, local(): message = lax.all_to_all(message, AXES, 0, 0, tiled=True)  9.9 us
    all_to_all x1, waiting for transfers between devices, local(): message = lax.all_to_all(message, AXES, 0, 0, tiled=True)  8.39 us
  transfers between devices with their start and end apart: 20, of which 13 were waited for; matrix products, arithmetic and copies ran while one was open for 1% of the time, Pallas kernels for 6%

profile of v2, /device:TPU:1, one launch (start us, length us, event | category | flops | bytes accessed | tf_op | source)
XLA Modules:
  0.0 196.6 jit_solution(9185477223084219411)
XLA Ops:
  8.5 2.2 %collective-permute-start = (f32[16,32,128]{2,1,0:T(8,128)S(1)}, f32[16,32,128]{2,1,0:T(8,128)S(1)}, u32[]{:S(2)}, u32[]{:S(2)}) collective-permute-start(f32[16,32,128]{2,1,0:T(8,128)S(1)} %pad_maximum_fusion), channel_id=1, source_target_pairs={{0,32},{32,64},{64,96},{96,0},{1,33},{33,65},{65,97},{97,1},{2,34}... | collective-permute-start | bytes 786440 | tf_op jit(solution)/shard_map/ppermute | solution.py:655
  12.2 5.8 %collective-permute-done.low = f32[16,32,128]{2,1,0:T(8,128)S(1)} collective-permute-done((f32[16,32,128]{2,1,0:T(8,128)S(1)}, f32[16,32,128]{2,1,0:T(8,128)S(1)}, u32[]{:S(2)}, u32[]{:S(2)}) %collective-permute-start) | collective-permute-done | bytes 262176 | tf_op jit(solution)/shard_map/ppermute | solution.py:655
  20.9 7.7 %collective-permute-done.2.below = f32[96,8,128]{2,1,0:T(8,128)S(1)} collective-permute-done((f32[96,8,128]{2,1,0:T(8,128)S(1)}, f32[96,8,128]{2,1,0:T(8,128)S(1)}, u32[]{:S(2)}, u32[]{:S(2)}) %collective-permute-start.2) | collective-permute-done | bytes 393248 | tf_op jit(solution)/shard_map/ppermute | solution.py:655
  29.3 3.8 %collective-permute-start.4 = (f32[12,48,128]{2,1,0:T(8,128)S(1)}, f32[12,48,128]{2,1,0:T(8,128)S(1)}, u32[]{:S(2)}, u32[]{:S(2)}) collective-permute-start(f32[12,48,128]{2,1,0:T(8,128)S(1)} %get-tuple-element.36), channel_id=1, source_target_pairs={{0,1},{1,2},{2,3},{3,4},{4,5},{5,6},{6,7},{7,0},{8,9},{9,10},{10,1... | collective-permute-start | bytes 884744 | tf_op jit(solution)/shard_map/ppermute | solution.py:655
  33.1 3.7 %collective-permute-done.4.from_low = f32[12,48,128]{2,1,0:T(8,128)S(1)} collective-permute-done((f32[12,48,128]{2,1,0:T(8,128)S(1)}, f32[12,48,128]{2,1,0:T(8,128)S(1)}, u32[]{:S(2)}, u32[]{:S(2)}) %collective-permute-start.4) | collective-permute-done | bytes 294944 | tf_op jit(solution)/shard_map/ppermute | solution.py:655
  36.8 2.5 %collective-permute-done.5.from_high = f32[12,48,128]{2,1,0:T(8,128)S(1)} collective-permute-done((f32[12,48,128]{2,1,0:T(8,128)S(1)}, f32[12,48,128]{2,1,0:T(8,128)S(1)}, u32[]{:S(2)}, u32[]{:S(2)}) %collective-permute-start.5) | collective-permute-done | bytes 294944 | tf_op jit(solution)/shard_map/ppermute | solution.py:655
  39.2 3.9 %shard_map.78 = (f32[48,2,24,128]{3,2,1,0:T(8,128)S(1)}, f32[48,2,24,128]{3,2,1,0:T(8,128)S(1)}, f32[48,2,24,128]{3,2,1,0:T(8,128)S(1)}, f32[48,2,24,128]{3,2,1,...) custom-call(f32[96,48,128]{2,1,0:T(8,128)S(1)} %get-tuple-element.35.split, ...), custom_call_target="tpu_custom_call" | custom-call | tf_op jit(solution)/shard_map/pallas_call | solution.py:49
  48.0 3.4 %collective-permute-done.6 = f32[14,16,128]{2,1,0:T(8,128)S(1)} collective-permute-done((f32[14,16,128]{2,1,0:T(8,128)S(1)}, f32[14,16,128]{2,1,0:T(8,128)S(1)}, u32[]{:S(2)}, u32[]{:S(2)}) %collective-permute-start.6) | collective-permute-done | bytes 114720 | tf_op jit(solution)/shard_map/ppermute | solution.py:655
  54.7 8.4 %collective-permute-done.8.below = f32[44,16,128]{2,1,0:T(8,128)S(1)} collective-permute-done((f32[44,16,128]{2,1,0:T(8,128)S(1)}, f32[44,16,128]{2,1,0:T(8,128)S(1)}, u32[]{:S(2)}, u32[]{:S(2)}) %collective-permute-start.8) | collective-permute-done | bytes 360480 | tf_op jit(solution)/shard_map/ppermute | solution.py:655
  65.1 3.4 %collective-permute-done.10.from_low = f32[11,2,24,128]{3,2,1,0:T(8,128)S(1)} collective-permute-done((f32[11,2,24,128]{3,2,1,0:T(8,128)S(1)}, f32[11,2,24,128]{3,2,1,0:T(8,128)S(1)}, u32[]{:S(2)}, u32[]{:S(2)}) %collective-permute-start.10) | collective-permute-done | bytes 270368 | tf_op jit(solution)/shard_map/ppermute | solution.py:655
  68.5 2.8 %collective-permute-done.11.from_high = f32[11,2,24,128]{3,2,1,0:T(8,128)S(1)} collective-permute-done((f32[11,2,24,128]{3,2,1,0:T(8,128)S(1)}, f32[11,2,24,128]{3,2,1,0:T(8,128)S(1)}, u32[]{:S(2)}, u32[]{:S(2)}) %collective-permute-start.11) | collective-permute-done | bytes 270368 | tf_op jit(solution)/shard_map/ppermute | solution.py:655
  71.3 7.1 %shard_map.80 = (f32[44,2,24,128]{3,2,1,0:T(8,128)S(1)}, f32[44,2,24,128]{3,2,1,0:T(8,128)S(1)}, f32[44,24,128]{2,1,0:T(8,128)S(1)}, f32[20,24,128]{2,1,0:T(8,12...) custom-call(f32[44,2,24,128]{3,2,1,0:T(8,128)S(1)} %get-tuple-element.38.coloured, ...), custom_call_target="tpu_custom_call" | custom-call | tf_op jit(solution)/shard_map/pallas_call | solution.py:49
  80.9 9.9 %all-to-all-start = ((f32[128,4,128]{2,1,0:T(4,128)}), f32[128,4,128]{2,1,0:T(4,128)}, u32[]{:S(2)}, u32[]{:S(2)}) async-start(f32[128,4,128]{2,1,0:T(4,128)} %bitcast), calls=%async_computation | async-start | bytes 524288 | tf_op jit(solution)/shard_map/all_to_all | solution.py:710
  93.1 8.4 %all-to-all-done = f32[128,4,128]{2,1,0:T(4,128)} async-done(((f32[128,4,128]{2,1,0:T(4,128)}), f32[128,4,128]{2,1,0:T(4,128)}, u32[]{:S(2)}, u32[]{:S(2)}) %all-to-all-start) | async-done | bytes 262176 | tf_op jit(solution)/shard_map/all_to_all | solution.py:710
  111.3 10.4 %shard_map.81 = (f32[16,16,128]{2,1,0:T(8,128)S(1)}, f32[8,8,128]{2,1,0:T(8,128)S(1)}, f32[48,2,24,128]{3,2,1,0:T(8,128)S(1)}, f32[8,16,128]{2,1,0:T(8,128)S(1)}, f32[8,128]{1,0:T(8,128)S(1)}) custom-call(f32[512,128]{1,0:T(8,128)} %bitcast.1.message, s32[3]{0:T(128)S(1)} %copy-done.25, f32[512,512]{1,0:T(8,128)S(1)} %reshape.13.inverse, ...), custom_call_target="tpu_custom_call" | custom-call | tf_op jit(solution)/shard_map/pallas_call | solution.py:49
  122.0 2.5 %collective-permute-start.13 = (f32[8,16,128]{2,1,0:T(8,128)S(1)}, f32[8,16,128]{2,1,0:T(8,128)S(1)}, u32[]{:S(2)}, u32[]{:S(2)}) collective-permute-start(f32[8,16,128]{2,1,0:T(8,128)S(1)} %get-tuple-element.53), channel_id=1, source_target_pairs={{32,0},{64,32},{96,64},{0,96},{33,1},{65,33},{97,65},{1,97},{34,2}... | collective-permute-start | bytes 196616 | tf_op jit(solution)/shard_map/ppermute | solution.py:655
  126.4 2.5 %collective-permute-start.15 = (f32[24,16,128]{2,1,0:T(8,128)S(1)}, f32[24,16,128]{2,1,0:T(8,128)S(1)}, u32[]{:S(2)}, u32[]{:S(2)}) collective-permute-start(f32[24,16,128]{2,1,0:T(8,128)S(1)} %constant_dynamic-update-slice_fusion.11.own), channel_id=1, source_target_pairs={{8,0},{16,8},{24,16},{0,24},{9,1},{17,9},{25,17},{1,25},{10,2},{18... | collective-permute-start | bytes 589832 | tf_op jit(solution)/shard_map/ppermute | solution.py:655
  128.9 3.1 %collective-permute-done.14.below = f32[24,16,128]{2,1,0:T(8,128)S(1)} collective-permute-done((f32[24,16,128]{2,1,0:T(8,128)S(1)}, f32[24,16,128]{2,1,0:T(8,128)S(1)}, u32[]{:S(2)}, u32[]{:S(2)}) %collective-permute-start.14) | collective-permute-done | bytes 196640 | tf_op jit(solution)/shard_map/ppermute | solution.py:655
  132.3 3.3 %collective-permute-start.16 = (f32[6,2,24,128]{3,2,1,0:T(8,128)S(1)}, f32[6,2,24,128]{3,2,1,0:T(8,128)S(1)}, u32[]{:S(2)}, u32[]{:S(2)}) collective-permute-start(f32[6,2,24,128]{3,2,1,0:T(8,128)S(1)} %get-tuple-element.55), channel_id=1, source_target_pairs={{0,1},{1,2},{2,3},{3,4},{4,5},{5,6},{6,7},{7,0},{8,9},{9,10},{10,1... | collective-permute-start | bytes 442376 | tf_op jit(solution)/shard_map/ppermute | solution.py:655
  137.7 2.8 %collective-permute-done.17.from_high = f32[6,2,24,128]{3,2,1,0:T(8,128)S(1)} collective-permute-done((f32[6,2,24,128]{3,2,1,0:T(8,128)S(1)}, f32[6,2,24,128]{3,2,1,0:T(8,128)S(1)}, u32[]{:S(2)}, u32[]{:S(2)}) %collective-permute-start.17) | collective-permute-done | bytes 147488 | tf_op jit(solution)/shard_map/ppermute | solution.py:655
  140.5 4.3 %shard_map.83 = (f32[44,2,24,128]{3,2,1,0:T(8,128)S(1)}, f32[44,24,128]{2,1,0:T(8,128)S(1)}, f32[20,24,128]{2,1,0:T(8,128)S(1)}, f32[20,24,128]{2,1,0:T(8,128)S(1)}, f32[256,128]{1,0:T(8,128)S(1)}) custom-call(f32[24,2,24,128]{3,2,1,0:T(8,128)S(1)} %get-tuple-element.54.coloured, f32[6,2,24,128]{3,2,1,0:T(8,128)S(1)} %collective-permute-done.16.from_low, ...), custom_call_target="tpu_custom_call" | custom-call | tf_op jit(solution)/shard_map/pallas_call | solution.py:49
  144.8 19.8 %all_to_all.31 = f32[128,2,128]{2,1,0:T(2,128)S(1)} all-to-all(f32[128,2,128]{2,1,0:T(2,128)S(1)} %bitcast.12), channel_id=1, replica_groups=mesh['gx'=4,'gy'=4,'gz'=8] {'gx','gy','gz'}, dimensions={0} | all-to-all | bytes 262144 | tf_op jit(solution)/shard_map/all_to_all | solution.py:729
  164.6 10.6 %shard_map.84 = (f32[32,32,128]{2,1,0:T(8,128)}, f32[128,128]{1,0:T(8,128)S(1)}) custom-call(f32[256,128]{1,0:T(8,128)S(1)} %bitcast.11, s32[3]{0:T(128)S(1)} %copy-done.25, f32[512,512]{1,0:T(8,128)S(1)} %reshape.13.inverse, f32[20,24,128]{2,1,0:T(8,128)S(1)} %get-tuple-element.58.f2, f32[20,24,128]{2,1,0:T(8,128)S(1)} %get-tuple-element.43.i2, ...), custom_call_target="tpu_custom_call" | custom-call | tf_op jit(solution)/shard_map/pallas_call | solution.py:49
  175.2 13.6 %all_to_all.32 = f32[128,1,128]{2,1,0:T(1,128)S(1)} all-to-all(f32[128,1,128]{2,1,0:T(1,128)S(1)} %bitcast.13), channel_id=1, replica_groups=mesh['gx'=4,'gy'=4,'gz'=8] {'gx','gy','gz'}, dimensions={0} | all-to-all | bytes 131072 | tf_op jit(solution)/shard_map/all_to_all | solution.py:737
  (101 shorter events, 36.6 us)
Async XLA Ops:
  7.2 84.3 %all-gather.3.cloned.1.call-start = ((), (), s32[]{:S(2)}) async-start(), calls=%async_computation.3 | async-start | bytes 1056768 | tf_op jit(solution)/shard_map/all_gather | solution.py:671
  8.5 9.5 %collective-permute-start = (f32[16,32,128]{2,1,0:T(8,128)S(1)}, f32[16,32,128]{2,1,0:T(8,128)S(1)}, u32[]{:S(2)}, u32[]{:S(2)}) collective-permute-start(f32[16,32,128]{2,1,0:T(8,128)S(1)} %pad_maximum_fusion), channel_id=1, source_target_pairs={{0,32},{32,64},{64,96},{96,0},{1,33},{33,65},{65,97},{97,1},{2,34}... | collective-permute-start | bytes 786440 | tf_op jit(solution)/shard_map/ppermute | solution.py:655
  10.7 7.3 %collective-permute-start.1 = (f32[16,32,128]{2,1,0:T(8,128)S(1)}, f32[16,32,128]{2,1,0:T(8,128)S(1)}, u32[]{:S(2)}, u32[]{:S(2)}) collective-permute-start(f32[16,32,128]{2,1,0:T(8,128)S(1)} %pad_maximum_fusion.1), channel_id=1, source_target_pairs={{32,0},{64,32},{96,64},{0,96},{33,1},{65,33},{97,65},{1,97},{34,2}... | collective-permute-start | bytes 786440 | tf_op jit(solution)/shard_map/ppermute | solution.py:655
  18.1 10.5 %collective-permute-start.2 = (f32[96,8,128]{2,1,0:T(8,128)S(1)}, f32[96,8,128]{2,1,0:T(8,128)S(1)}, u32[]{:S(2)}, u32[]{:S(2)}) collective-permute-start(f32[96,8,128]{2,1,0:T(8,128)S(1)} %get-tuple-element.77), channel_id=1, source_target_pairs={{0,8},{8,16},{16,24},{24,0},{1,9},{9,17},{17,25},{25,1},{2,10},{10... | collective-permute-start | bytes 1179656 | tf_op jit(solution)/shard_map/ppermute | solution.py:655
  19.3 9.3 %collective-permute-start.3 = (f32[96,8,128]{2,1,0:T(8,128)S(1)}, f32[96,8,128]{2,1,0:T(8,128)S(1)}, u32[]{:S(2)}, u32[]{:S(2)}) collective-permute-start(f32[96,8,128]{2,1,0:T(8,128)S(1)} %get-tuple-element.76), channel_id=1, source_target_pairs={{8,0},{16,8},{24,16},{0,24},{9,1},{17,9},{25,17},{1,25},{10,2},{18... | collective-permute-start | bytes 1179656 | tf_op jit(solution)/shard_map/ppermute | solution.py:655
  29.3 7.5 %collective-permute-start.4 = (f32[12,48,128]{2,1,0:T(8,128)S(1)}, f32[12,48,128]{2,1,0:T(8,128)S(1)}, u32[]{:S(2)}, u32[]{:S(2)}) collective-permute-start(f32[12,48,128]{2,1,0:T(8,128)S(1)} %get-tuple-element.36), channel_id=1, source_target_pairs={{0,1},{1,2},{2,3},{3,4},{4,5},{5,6},{6,7},{7,0},{8,9},{9,10},{10,1... | collective-permute-start | bytes 884744 | tf_op jit(solution)/shard_map/ppermute | solution.py:655
  33.1 6.2 %collective-permute-start.5 = (f32[12,48,128]{2,1,0:T(8,128)S(1)}, f32[12,48,128]{2,1,0:T(8,128)S(1)}, u32[]{:S(2)}, u32[]{:S(2)}) collective-permute-start(f32[12,48,128]{2,1,0:T(8,128)S(1)} %get-tuple-element.36), channel_id=1, source_target_pairs={{1,0},{2,1},{3,2},{4,3},{5,4},{6,5},{7,6},{0,7},{9,8},{10,9},{11,1... | collective-permute-start | bytes 884744 | tf_op jit(solution)/shard_map/ppermute | solution.py:655
  45.3 26.0 %copy-start = (f32[48,2,24,128]{3,2,1,0:T(8,128)}, f32[48,2,24,128]{3,2,1,0:T(8,128)S(1)}, u32[]{:S(2)}) copy-start(f32[48,2,24,128]{3,2,1,0:T(8,128)S(1)} %get-tuple-element.49.fb) | copy-start | bytes 3538948
  45.3 33.1 %copy-start.6 = (f32[48,2,24,128]{3,2,1,0:T(8,128)}, f32[48,2,24,128]{3,2,1,0:T(8,128)S(1)}, u32[]{:S(2)}) copy-start(f32[48,2,24,128]{3,2,1,0:T(8,128)S(1)} %get-tuple-element.51.ib) | copy-start | bytes 3538948
  45.3 6.2 %collective-permute-start.6 = (f32[14,16,128]{2,1,0:T(8,128)S(1)}, f32[14,16,128]{2,1,0:T(8,128)S(1)}, u32[]{:S(2)}, u32[]{:S(2)}) collective-permute-start(f32[14,16,128]{2,1,0:T(8,128)S(1)} %get-tuple-element.85), channel_id=1, source_target_pairs={{0,32},{32,64},{64,96},{96,0},{1,33},{33,65},{65,97},{97,1},{2,34}... | collective-permute-start | bytes 344072 | tf_op jit(solution)/shard_map/ppermute | solution.py:655
  46.3 5.2 %collective-permute-start.7 = (f32[14,16,128]{2,1,0:T(8,128)S(1)}, f32[14,16,128]{2,1,0:T(8,128)S(1)}, u32[]{:S(2)}, u32[]{:S(2)}) collective-permute-start(f32[14,16,128]{2,1,0:T(8,128)S(1)} %get-tuple-element.84), channel_id=1, source_target_pairs={{32,0},{64,32},{96,64},{0,96},{33,1},{65,33},{97,65},{1,97},{34,2}... | collective-permute-start | bytes 344072 | tf_op jit(solution)/shard_map/ppermute | solution.py:655
  51.5 11.6 %collective-permute-start.8 = (f32[44,16,128]{2,1,0:T(8,128)S(1)}, f32[44,16,128]{2,1,0:T(8,128)S(1)}, u32[]{:S(2)}, u32[]{:S(2)}) collective-permute-start(f32[44,16,128]{2,1,0:T(8,128)S(1)} %constant_dynamic-update-slice_fusion.8.own), channel_id=1, source_target_pairs={{0,8},{8,16},{16,24},{24,0},{1,9},{9,17},{17,25},{25,1},{2,10},{10... | collective-permute-start | bytes 1081352 | tf_op jit(solution)/shard_map/ppermute | solution.py:655
  53.2 9.9 %collective-permute-start.9 = (f32[44,16,128]{2,1,0:T(8,128)S(1)}, f32[44,16,128]{2,1,0:T(8,128)S(1)}, u32[]{:S(2)}, u32[]{:S(2)}) collective-permute-start(f32[44,16,128]{2,1,0:T(8,128)S(1)} %constant_dynamic-update-slice_fusion.8.own), channel_id=1, source_target_pairs={{8,0},{16,8},{24,16},{0,24},{9,1},{17,9},{25,17},{1,25},{10,2},{18... | collective-permute-start | bytes 1081352 | tf_op jit(solution)/shard_map/ppermute | solution.py:655
  63.7 4.8 %collective-permute-start.10 = (f32[11,2,24,128]{3,2,1,0:T(8,128)S(1)}, f32[11,2,24,128]{3,2,1,0:T(8,128)S(1)}, u32[]{:S(2)}, u32[]{:S(2)}) collective-permute-start(f32[11,2,24,128]{3,2,1,0:T(8,128)S(1)} %get-tuple-element.39), channel_id=1, source_target_pairs={{0,1},{1,2},{2,3},{3,4},{4,5},{5,6},{6,7},{7,0},{8,9},{9,10},{10,1... | collective-permute-start | bytes 811016 | tf_op jit(solution)/shard_map/ppermute | solution.py:655
  65.1 6.2 %collective-permute-start.11 = (f32[11,2,24,128]{3,2,1,0:T(8,128)S(1)}, f32[11,2,24,128]{3,2,1,0:T(8,128)S(1)}, u32[]{:S(2)}, u32[]{:S(2)}) collective-permute-start(f32[11,2,24,128]{3,2,1,0:T(8,128)S(1)} %get-tuple-element.40), channel_id=1, source_target_pairs={{1,0},{2,1},{3,2},{4,3},{5,4},{6,5},{7,6},{0,7},{9,8},{10,9},{11,1... | collective-permute-start | bytes 811016 | tf_op jit(solution)/shard_map/ppermute | solution.py:655
  80.9 20.5 %all-to-all-start = ((f32[128,4,128]{2,1,0:T(4,128)}), f32[128,4,128]{2,1,0:T(4,128)}, u32[]{:S(2)}, u32[]{:S(2)}) async-start(f32[128,4,128]{2,1,0:T(4,128)} %bitcast), calls=%async_computation | async-start | bytes 524288 | tf_op jit(solution)/shard_map/all_to_all | solution.py:710
  111.3 29.1 %copy-start.10 = (bf16[4,384,256]{2,1,0:T(8,128)(2,1)S(1)}, bf16[4,384,256]{2,1,0:T(8,128)(2,1)}, u32[]{:S(2)}) copy-start(bf16[4,384,256]{2,1,0:T(8,128)(2,1)} %constant.23.clone.matrices) | copy-start | bytes 2359300
  121.7 4.4 %collective-permute-start.12 = (f32[8,16,128]{2,1,0:T(8,128)S(1)}, f32[8,16,128]{2,1,0:T(8,128)S(1)}, u32[]{:S(2)}, u32[]{:S(2)}) collective-permute-start(f32[8,16,128]{2,1,0:T(8,128)S(1)} %get-tuple-element.53), channel_id=1, source_target_pairs={{0,32},{32,64},{64,96},{96,0},{1,33},{33,65},{65,97},{97,1},{2,34}... | collective-permute-start | bytes 196616 | tf_op jit(solution)/shard_map/ppermute | solution.py:655
  122.0 4.1 %collective-permute-start.13 = (f32[8,16,128]{2,1,0:T(8,128)S(1)}, f32[8,16,128]{2,1,0:T(8,128)S(1)}, u32[]{:S(2)}, u32[]{:S(2)}) collective-permute-start(f32[8,16,128]{2,1,0:T(8,128)S(1)} %get-tuple-element.53), channel_id=1, source_target_pairs={{32,0},{64,32},{96,64},{0,96},{33,1},{65,33},{97,65},{1,97},{34,2}... | collective-permute-start | bytes 196616 | tf_op jit(solution)/shard_map/ppermute | solution.py:655
  126.1 5.8 %collective-permute-start.14 = (f32[24,16,128]{2,1,0:T(8,128)S(1)}, f32[24,16,128]{2,1,0:T(8,128)S(1)}, u32[]{:S(2)}, u32[]{:S(2)}) collective-permute-start(f32[24,16,128]{2,1,0:T(8,128)S(1)} %constant_dynamic-update-slice_fusion.11.own), channel_id=1, source_target_pairs={{0,8},{8,16},{16,24},{24,0},{1,9},{9,17},{17,25},{25,1},{2,10},{10... | collective-permute-start | bytes 589832 | tf_op jit(solution)/shard_map/ppermute | solution.py:655
  126.4 5.5 %collective-permute-start.15 = (f32[24,16,128]{2,1,0:T(8,128)S(1)}, f32[24,16,128]{2,1,0:T(8,128)S(1)}, u32[]{:S(2)}, u32[]{:S(2)}) collective-permute-start(f32[24,16,128]{2,1,0:T(8,128)S(1)} %constant_dynamic-update-slice_fusion.11.own), channel_id=1, source_target_pairs={{8,0},{16,8},{24,16},{0,24},{9,1},{17,9},{25,17},{1,25},{10,2},{18... | collective-permute-start | bytes 589832 | tf_op jit(solution)/shard_map/ppermute | solution.py:655
  131.9 32.7 %copy-start.8 = (f32[48,2,24,128]{3,2,1,0:T(8,128)S(1)}, f32[48,2,24,128]{3,2,1,0:T(8,128)}, u32[]{:S(2)}) copy-start(f32[48,2,24,128]{3,2,1,0:T(8,128)} %copy-done.6) | copy-start | bytes 3538948
  132.3 5.4 %collective-permute-start.16 = (f32[6,2,24,128]{3,2,1,0:T(8,128)S(1)}, f32[6,2,24,128]{3,2,1,0:T(8,128)S(1)}, u32[]{:S(2)}, u32[]{:S(2)}) collective-permute-start(f32[6,2,24,128]{3,2,1,0:T(8,128)S(1)} %get-tuple-element.55), channel_id=1, source_target_pairs={{0,1},{1,2},{2,3},{3,4},{4,5},{5,6},{6,7},{7,0},{8,9},{9,10},{10,1... | collective-permute-start | bytes 442376 | tf_op jit(solution)/shard_map/ppermute | solution.py:655
  135.6 4.9 %collective-permute-start.17 = (f32[6,2,24,128]{3,2,1,0:T(8,128)S(1)}, f32[6,2,24,128]{3,2,1,0:T(8,128)S(1)}, u32[]{:S(2)}, u32[]{:S(2)}) collective-permute-start(f32[6,2,24,128]{3,2,1,0:T(8,128)S(1)} %get-tuple-element.56), channel_id=1, source_target_pairs={{1,0},{2,1},{3,2},{4,3},{5,4},{6,5},{7,6},{0,7},{9,8},{10,9},{11,1... | collective-permute-start | bytes 442376 | tf_op jit(solution)/shard_map/ppermute | solution.py:655
  (22 other events, 162.3 us)
Sparse Core Ops, SparseCore 0:
  21.0 66.5 all-gather.2

commit v3 on v2

--- a/solution.py
+++ b/solution.py
@@ -41,19 +41,74 @@
     lax.fori_loop(start, stop, step, 0, unroll=unroll)
 
 
-def call(body, outs, *operands, scratch=()):
-    specs = [
-        pl.BlockSpec(memory_space=pltpu.SMEM if operand.dtype == jnp.int32 else pltpu.VMEM)
-        for operand in operands
-    ]
-    return pl.pallas_call(
-        body,
-        out_shape=[jax.ShapeDtypeStruct(shape, F32) for shape in outs],
-        in_specs=specs,
-        out_specs=[pl.BlockSpec(memory_space=pltpu.VMEM)] * len(outs),
-        scratch_shapes=[pltpu.VMEM(shape, F32) for shape in scratch],
+class Parked:
+    def __init__(self, shape, place, whole=None):
+        self.shape, self.place, self.whole = shape, place, whole
+
+    def of(self, whole):
+        return Parked(self.shape, self.place, whole)
+
+
+def call(body, outs, *operands, scratch=(), park=None):
+    inputs, input_at = [], []
+    for operand in operands:
+        array = operand.whole if isinstance(operand, Parked) else operand
+        at = next((k for k, other in enumerate(inputs) if other is array), len(inputs))
+        if at == len(inputs):
+            inputs.append(array)
+        input_at.append(at)
+    far = [isinstance(item, Parked) for item in (*operands, *outs)]
+    parked = [item for item in (*operands, *outs) if isinstance(item, Parked)]
+    near_outs = [shape for shape in outs if not isinstance(shape, Parked)]
+    far_arrays = [operand.whole for operand in operands if isinstance(operand, Parked)]
+
+    def kernel(*refs):
+        refs = list(refs)
+        ins = [refs.pop(0) for _ in inputs]
+        near = [refs.pop(0) for _ in near_outs]
+        store = refs.pop(0) if park else None
+        semaphores = refs.pop() if parked else None
+        work, nears = refs[: len(scratch)], refs[len(scratch) :]
+        ready, copies = [], {}
+        for at, item in enumerate((*operands, *outs)):
+            inward = at < len(operands)
+            if far[at]:
+                ref = nears.pop(0)
+                place = item.place(ins[input_at[at]] if inward else store)
+                ends = (place, ref) if inward else (ref, place)
+                copies[at] = pltpu.make_async_copy(*ends, semaphores.at[len(copies)])
+                if inward:
+                    copies[at].start()
+            else:
+                ref = ins[input_at[at]] if inward else near.pop(0)
+            ready.append(ref)
+        body(*ready, *work, copies)
+        for at in range(len(operands), len(far)):
+            if far[at]:
+                copies[at].wait()
+
+    def spec(array):
+        if any(array is other for other in far_arrays):
+            return pl.BlockSpec(memory_space=pl.ANY)
+        return pl.BlockSpec(memory_space=pltpu.SMEM if array.dtype == jnp.int32 else pltpu.VMEM)
+
+    shapes = near_outs + ([park] if park else [])
+    spaces = [pltpu.VMEM] * len(near_outs) + ([pl.ANY] if park else [])
+    work = [pltpu.VMEM(shape, F32) for shape in scratch]
+    work += [pltpu.VMEM(item.shape, F32) for item in parked]
+    if parked:
+        work.append(pltpu.SemaphoreType.DMA((len(parked),)))
+    results = pl.pallas_call(
+        kernel,
+        out_shape=[jax.ShapeDtypeStruct(shape, F32) for shape in shapes],
+        in_specs=[spec(array) for array in inputs],
+        out_specs=[pl.BlockSpec(memory_space=space) for space in spaces],
+        scratch_shapes=work,
         compiler_params=pltpu.CompilerParams(vmem_limit_bytes=32 * 1024 * 1024),
-    )(*operands)
+    )(*inputs)
+    results = list(results)
+    whole = results.pop() if park else None
+    return [out.of(whole) if isinstance(out, Parked) else results.pop(0) for out in outs]
 
 
 def lower_matrices():
@@ -148,7 +203,16 @@
     return (iota(shape, 0) + iota(shape, 1) + plane) % 2 == 0
 
 
-def pack_z0(f, s, low, high, below, above, split, message, rows):
+def pack_y0(f, s, low, high, to_high, to_low, _):
+    for field, own in enumerate((f, s)):
+        at, halo = field * X0, slice(field * H0, field * H0 + H0)
+        for cut, message in ((slice(24, 32), to_high), (slice(0, 8), to_low)):
+            message[at : at + H0] = low[halo, cut]
+            message[at + H0 : at + H0 + 32] = own[:, cut]
+            message[at + H0 + 32 : at + X0] = high[halo, cut]
+
+
+def pack_z0(f, s, low, high, below, above, split, message, rows, _):
     block = (iota((Y0, LANES), 1) + 8) % LANES // 16
     for group in range(2 * X0 // GROUP0):
         packed = jnp.zeros((Y0, LANES), F32)
@@ -173,7 +237,7 @@
         message[group] = packed
 
 
-def down0(split, from_low, from_high, matrices, fr, fb, ir, ib, vb, own1, red, screen):
+def down0(split, from_low, from_high, matrices, fr, fb, ir, ib, vb, own1, red, screen, copies):
     lane = iota((Y0, LANES), 1)
     groups = 2 * X0 // GROUP0
     merged = [
@@ -199,6 +263,9 @@
                     ir[plane, q] = 1.0 / (6.0 + reds)
                     ib[plane, q] = 1.0 / (6.0 + blacks)
 
+    for at in range(4, 8):
+        copies[at].start()
+
     def first(p):
         red[p] = fr[p] * ir[p]
 
@@ -211,6 +278,7 @@
     black(1, 1)
     plane_pairs(2, X0 - 2, black)
     black(X0 - 2, 0)
+    copies[8].start()
 
     def restrict(i):
         plane = 2 * i + H0
@@ -228,7 +296,7 @@
     return total + sum0(values, plane + 1, 1, 1, True)
 
 
-def pack_z1(own, below, above, coloured, to_high, to_low):
+def pack_z1(own, below, above, coloured, to_high, to_low, _):
     block = iota((24, LANES), 1) % 64 // 14
     for group in range(own.shape[0] // GROUP1):
         up = [jnp.zeros((24, LANES), F32)] * 2
@@ -328,7 +396,7 @@
     return [rows[0] + rows[1], rows[2] + rows[3]]
 
 
-def down12_first(coloured, from_low, from_high, matrices, f1, i1, b1, f2, i2, v2, message, red, sums):
+def down12_first(coloured, from_low, from_high, matrices, f1, i1, b1, f2, i2, v2, message, red, sums, copies):
     def store(plane, colour, halves):
         f1[plane, colour], i1[plane, colour] = halves
 
@@ -353,14 +421,18 @@
 
     loop(0, X1, invert1, 4)
     loop(0, X2, invert2, 4)
+    for at in (4, 5, 8):
+        copies[at].start()
     down12(f1, i1, b1, f2, i2, v2, red)
-    tile = jnp.concatenate(source3(v2, sums) + [rows[0] + rows[1], rows[2] + rows[3]], axis=0)
-    tile = jnp.concatenate([tile, tile], axis=0)
+    for at in (6, 7, 9):
+        copies[at].start()
+    tile = source3(v2, sums) + [rows[0] + rows[1], rows[2] + rows[3]]
+    tile = jnp.concatenate(tile + tile, axis=0)
     for i in range(64):
         message[8 * i : 8 * i + 8, :] = tile
 
 
-def down12_next(coloured, from_low, from_high, matrices, i1, i2, f1, b1, f2, v2, message, red, sums):
+def down12_next(coloured, from_low, from_high, matrices, i1, i2, f1, b1, f2, v2, message, red, sums, copies):
     def store(item, colour, halves):
         block, i = divmod(item, 8)
         for half in (0, 1):
@@ -369,6 +441,8 @@
                 f1[plane, colour] = halves[half]
 
     unpack1(coloured, from_low, from_high, matrices, store)
+    for at in (4, 5):
+        copies[at].wait()
     down12(f1, i1, b1, f2, i2, v2, red)
     tile = jnp.concatenate(source3(v2, sums) * 4, axis=0)
     for i in range(32):
@@ -422,7 +496,7 @@
     return 0.5 * pick3(pairs, 2 * (iota((1, LANES), 1) % 64))
 
 
-def coarse_solve(f3, i3, i4, inverse, e3, wide):
+def coarse_solve(f3, i3, i4, place, inverse, e3, wide):
     red3, red4 = red_whole((16, 16, LANES)), red_whole((8, 8, LANES))
     v3 = jnp.where(red3, f3 * i3, 0.0)
     v3 = jnp.where(red3, v3, (f3 + sum_whole(v3)) * i3)
@@ -439,14 +513,19 @@
     vector = jnp.broadcast_to(jnp.concatenate(rows, axis=1), (8, 512))
     answer = lax.dot_general(
         vector,
-        inverse[...],
+        jnp.concatenate([ref[...] for ref in inverse] + [jnp.zeros((64, 512), F32)], axis=0),
         (((1,), (1,)), ((), ())),
         precision=lax.Precision.HIGHEST,
         preferred_element_type=F32,
     )
     planes = []
     for x5 in range(4):
-        part = pick(answer[:, 128 * x5 : 128 * x5 + 128], (sub // 2) * 32 + (lane % 64) // 2)
+        z5 = lane % 64 // 2
+        index = (place[1] + 4 - sub // 2) % 4 * 16 + (place[0] + 4 - x5) % 4 * 4 + z5 % 4
+        apart = (z5 // 4 + 8 - place[2]) % 8
+        same = pick(answer[:, :LANES], index + jnp.where(apart == 7, 64, 0))
+        part = jnp.where(apart == 1, pick(answer[:, LANES:], index), same)
+        part = jnp.where(jnp.logical_or(apart <= 1, apart == 7), part, 0.0)
         planes += [part[None], part[None]]
     w4 = v4 + jnp.concatenate(planes, axis=0)
     w4 = jnp.where(red4, (f4 + sum_whole(w4)) * i4, w4)
@@ -532,9 +611,9 @@
 
 
 def middle(
-    message, place, inverse, f2, i2, v2, f1, i1, b1, fr, fb, ir, ib, vb,
+    message, place, near, before, after, f2, i2, v2, f1, i1, b1, fr, fb, ir, ib, vb,
     i3, i4, bnew, own1, norm,
-    f3, e3, wide, tall, e2, er, eb, w, r, rnew,
+    f3, e3, wide, tall, e2, er, eb, w, r, rnew, copies,
 ):
     unpack3(message, 4, 0, f3)
     unpack3(message, 4, 2, e3)
@@ -542,8 +621,12 @@
     screen4 = coarse34(screen3, wide)
     i3[...] = 1.0 / (6.0 + screen3)
     i4[...] = 1.0 / (6.0 + screen4)
-    coarse_solve(f3[...], i3[...], i4[...], inverse, e3, wide)
+    coarse_solve(f3[...], i3[...], i4[...], place, (near, before, after), e3, wide)
+    for at in range(5, 11):
+        copies[at].wait()
     up21(place, e3, f2, i2, v2, f1, i1, b1, e2, er, eb, tall)
+    for at in range(11, 16):
+        copies[at].wait()
     add0(er, eb, vb, w, tall)
 
     def red_up(p, parity):
@@ -595,13 +678,18 @@
 
 
 def final(
-    message, place, inverse, f2, i2, v2, f1, i1, b1, fr, fb, ir, ib, b, i3, i4, norm, matrix,
+    message, place, near, before, after, f2, i2, v2, f1, i1, b1, fr, fb, ir, ib, b, i3, i4,
+    norm, matrix,
     field, sums,
-    f3, e3, wide, tall, e2, er, eb, w, r, last,
+    f3, e3, wide, tall, e2, er, eb, w, r, last, copies,
 ):
     unpack3(message, 2, 0, f3)
-    coarse_solve(f3[...], i3[...], i4[...], inverse, e3, wide)
+    coarse_solve(f3[...], i3[...], i4[...], place, (near, before, after), e3, wide)
+    for at in (6, 9):
+        copies[at].wait()
     up21(place, e3, f2, i2, v2, f1, i1, b1, e2, er, eb, tall)
+    for at in range(11, 15):
+        copies[at].wait()
     add0(er, eb, b, w, tall)
 
     def red_up(p, parity):
@@ -627,7 +715,7 @@
             total = total + part * part
         return total
 
-    after = own_sum(sum_over(squares))
+    squared = own_sum(sum_over(squares))
 
     def finish(i):
         parts = []
@@ -641,9 +729,8 @@
             field[2 * i + at // 2 - H0, pl.ds(at % 2, 16, stride=2), :] = rows
 
     loop(H0 // 2, H0 // 2 + 16, finish)
-    before = norm[0:1, :]
     low = iota((1, LANES), 1) < 64
-    both = jnp.where(low, roll(before, -OWN, 1), roll(after, 64 - OWN, 1))
+    both = jnp.where(low, roll(norm[0:1, :], -OWN, 1), roll(squared, 64 - OWN, 1))
     for i in range(16):
         sums[8 * i : 8 * i + 8, :] = jnp.broadcast_to(both, (8, LANES))
 
@@ -655,32 +742,44 @@
     return lax.ppermute(to_high, axis, up), lax.ppermute(to_low, axis, down)
 
 
-def exchange1(own, low, high):
+def from_all(own, axis):
+    count = lax.axis_size(axis)
+    shifts = [[(i, (i + k) % count) for i in range(count)] for k in range(1, count)]
+    return [lax.ppermute(own, axis, shift) for shift in shifts]
+
+
+def together(first, second):
+    both = lax.optimization_barrier((*first, *second))
+    return both[: len(first)], both[len(first) :]
+
+
+def exchange1(own, low, high, beside=()):
     from_low, from_high = exchange(high, low, "gx")
     own = jnp.concatenate([from_low, own, from_high], axis=0)
     below, above = exchange(own, own, "gy")
+    if beside:
+        (below, above), beside = together((below, above), exchange(*beside, "gz"))
     items = own.shape[0]
     message = (items // GROUP1, 2, 24, LANES)
     coloured, to_high, to_low = call(
         pack_z1, [(items, 2, 24, LANES), message, message], own, below, above
     )
-    return coloured, *exchange(to_high, to_low, "gz")
+    return (coloured, *exchange(to_high, to_low, "gz")), beside
 
 
 def local(f, s, coarse_inverse):
-    inverse = lax.all_gather(coarse_inverse, AXES, axis=0, tiled=True)
     place = jnp.stack([lax.axis_index(axis) for axis in AXES]).astype(jnp.int32)
     low, high = exchange(
         jnp.concatenate([f[32 - H0 :], s[32 - H0 :]], axis=0),
         jnp.concatenate([f[:H0], s[:H0]], axis=0),
         "gx",
     )
-
-    def rows(cut):
-        parts = [low[:H0], f, high[:H0], low[H0:], s, high[H0:]]
-        return jnp.concatenate([part[:, cut] for part in parts], axis=0)
-
-    below, above = exchange(rows(slice(24, 32)), rows(slice(0, 8)), "gy")
+    (low, high), others = together((low, high), from_all(coarse_inverse, "gx"))
+    inverse = jnp.concatenate([coarse_inverse, *others], axis=0)
+    messages = call(pack_y0, [(2 * X0, 8, LANES)] * 2, f, s, low, high)
+    below, above = exchange(*messages, "gy")
+    (below, above), others = together((below, above), from_all(inverse, "gy"))
+    inverse = jnp.concatenate([inverse, *others], axis=0)
     groups = 2 * X0 // GROUP0
     line0, line1, line2 = (Y0, LANES), (24, LANES), (Y2, LANES)
     split, message = call(
@@ -694,18 +793,30 @@
     matrices1 = jnp.asarray(halo_matrices1(), jnp.bfloat16)
     fr, fb, ir, ib, vb, own1 = call(
         down0,
-        [level0] * 5 + [(16, 16, LANES)],
+        [Parked(level0, lambda ref, k=k: ref.at[k]) for k in range(5)] + [(16, 16, LANES)],
         split,
         *exchange(message, message, "gz"),
         jnp.asarray(lower_matrices(), jnp.bfloat16),
         scratch=[level0, (X0, *line1)],
-    )
+        park=(56, *level0),
+    )
+    level1_parts, others = exchange1(own1, own1[:H1], own1[16 - H1 :], (inverse, inverse))
+    inverse = (inverse, *others)
     f1, i1, b1, f2, i2, v2, message = call(
         down12_first,
-        [both1, both1, level1, level2, level2, level2, (512, LANES)],
-        *exchange1(own1, own1[:H1], own1[16 - H1 :]),
+        [
+            Parked(both1, lambda ref: ref.at[0]),
+            Parked(both1, lambda ref: ref.at[1]),
+            Parked(level1, lambda ref: ref.at[2, :, 0]),
+            Parked(level2, lambda ref: ref.at[2, 0:X2, 1]),
+            Parked(level2, lambda ref: ref.at[3, 0:X2, 0]),
+            Parked(level2, lambda ref: ref.at[3, 0:X2, 1]),
+            (512, LANES),
+        ],
+        *level1_parts,
         matrices1,
         scratch=[level1, (4, *line2)],
+        park=(60, *both1),
     )
     message = lax.all_to_all(message, AXES, 0, 0, tiled=True)
     whole = (16, 16, LANES)
@@ -714,13 +825,13 @@
     i3, i4, bnew, own1, norm = call(
         middle,
         [whole, (8, 8, LANES), level0, (8, 16, LANES), (8, LANES)],
-        message, place, inverse, f2, i2, v2, f1, i1, b1, fr, fb, ir, ib, vb,
+        message, place, *inverse, f2, i2, v2, f1, i1, b1, fr, fb, ir, ib, vb,
         scratch=work,
     )
     f1, b1, f2, v2, message = call(
         down12_next,
         [both1, level1, level2, level2, (256, LANES)],
-        *exchange1(own1, own1, own1),
+        *exchange1(own1, own1, own1)[0],
         matrices1,
         i1,
         i2,
@@ -730,7 +841,7 @@
     field, sums = call(
         final,
         [(32, 32, LANES), (128, LANES)],
-        message, place, inverse, f2, i2, v2, f1, i1, b1, fr, fb, ir, ib, bnew, i3, i4, norm,
+        message, place, *inverse, f2, i2, v2, f1, i1, b1, fr, fb, ir, ib, bnew, i3, i4, norm,
         jnp.asarray(upper_matrix(), jnp.bfloat16),
         scratch=work,
     )

time: 197 us -> 170 us (0.86)
  local copies, waits for them, and re-layouts: 17.5 us -> 1.44 us
  between operations: 14.3 us -> 0.88 us
  starting transfers between devices: 36.3 us -> 45.3 us
  waiting for transfers between devices: 55.6 us -> 49.7 us
  blocking collectives: 33.4 us -> 30.4 us
  Pallas kernels: 38 us -> 40.9 us
    ppermute x18 -> x20, waiting for transfers between devices: 47.2 us -> 28.7 us  [exchange(): return (lax.ppermute(to_high, axis, up), lax.ppermute(to_low, axis, down))]
    unnamed x62 -> x16, local copies, waits for them, and re-layouts: 16.2 us -> 0.06 us
    ppermute x0 -> x6, waiting for transfers between devices: none -> 10.2 us  [from_all(): return [lax.ppermute(own, axis, shift) for shift in shifts]]
    ppermute x18 -> x20, starting transfers between devices: 26.4 us -> 34.4 us  [exchange(): return (lax.ppermute(to_high, axis, up), lax.ppermute(to_low, axis, down))]
    ppermute x0 -> x6, starting transfers between devices: none -> 4.95 us  [from_all(): return [lax.ppermute(own, axis, shift) for shift in shifts]]
    all_to_all x1, starting transfers between devices: 9.9 us -> 5.92 us  [local(): message = lax.all_to_all(message, AXES, 0, 0, tiled=True)]
    all_to_all x1, blocking collectives: 19.8 us -> 16.8 us  [local(): message = lax.all_to_all(message, AXES, 0, 0, tiled=True)]
    pallas_call x8 -> x9, Pallas kernels: 38 us -> 40.9 us  [call(): pl.pallas_call(kernel, out_shape=[jax.ShapeDtypeStruct(shape, F32) for sh...]
  transfers between devices with their start and end apart: 20 -> 27, of which waited for: 13 -> 16; matrix products, arithmetic and copies ran while one was open for 1% -> 0% of each run, Pallas kernels for 6% -> 0%
where the time goes in v3:
time: 170 us; the launch traced here: 169 us
  waiting for transfers between devices  49.7 us (29%)
  starting transfers between devices  45.3 us (27%)
  Pallas kernels  40.9 us (24%)
  blocking collectives  30.4 us (18%)
    pallas_call x9, Pallas kernels, call(): pl.pallas_call(kernel, out_shape=[jax.ShapeDtypeStruct(shape, F32) for sh...  40.9 us
    ppermute x20, starting transfers between devices, exchange(): return (lax.ppermute(to_high, axis, up), lax.ppermute(to_low, axis, down))  34.4 us
    ppermute x20, waiting for transfers between devices, exchange(): return (lax.ppermute(to_high, axis, up), lax.ppermute(to_low, axis, down))  28.7 us
    all_to_all x1, blocking collectives, local(): message = lax.all_to_all(message, AXES, 0, 0, tiled=True)  16.8 us
    all_to_all x1, blocking collectives, local(): sums = lax.all_to_all(sums, AXES, 0, 0, tiled=True)  13.6 us
    all_to_all x1, waiting for transfers between devices, local(): message = lax.all_to_all(message, AXES, 0, 0, tiled=True)  10.8 us
    ppermute x6, waiting for transfers between devices, from_all(): return [lax.ppermute(own, axis, shift) for shift in shifts]  10.2 us
    all_to_all x1, starting transfers between devices, local(): message = lax.all_to_all(message, AXES, 0, 0, tiled=True)  5.92 us
  transfers between devices with their start and end apart: 27, of which 16 were waited for; matrix products, arithmetic and copies ran while one was open for 0% of the time, Pallas kernels for 0%

profile of v3, /device:TPU:1, one launch (start us, length us, event | category | flops | bytes accessed | tf_op | source)
XLA Modules:
  0.0 169.5 jit_solution(6461449612379993616)
XLA Ops:
  1.9 2.2 %collective-permute-start = (f32[16,32,128]{2,1,0:T(8,128)S(1)}, f32[16,32,128]{2,1,0:T(8,128)S(1)}, u32[]{:S(2)}, u32[]{:S(2)}) collective-permute-start(f32[16,32,128]{2,1,0:T(8,128)S(1)} %pad_maximum_fusion), channel_id=1, source_target_pairs={{0,32},{32,64},{64,96},{96,0},{1,33},{33,65},{65,97},{97,1},{2,34}... | collective-permute-start | bytes 786440 | tf_op jit(solution)/shard_map/ppermute | solution.py:742
  8.1 3.1 %collective-permute-done.4 = f32[4,512]{1,0:T(4,128)S(1)} collective-permute-done((f32[4,512]{1,0:T(4,128)}, f32[4,512]{1,0:T(4,128)S(1)}, u32[]{:S(2)}, u32[]{:S(2)}) %collective-permute-start.4) | collective-permute-done | bytes 8224 | tf_op jit(solution)/shard_map/ppermute | solution.py:748
  17.6 5.1 %collective-permute-done.9 = f32[16,512]{1,0:T(8,128)S(1)} collective-permute-done((f32[16,512]{1,0:T(8,128)S(1)}, f32[16,512]{1,0:T(8,128)S(1)}, u32[]{:S(2)}, u32[]{:S(2)}) %collective-permute-start.9) | collective-permute-done | bytes 32800 | tf_op jit(solution)/shard_map/ppermute | solution.py:748
  24.4 3.6 %collective-permute-start.11 = (f32[12,48,128]{2,1,0:T(8,128)S(1)}, f32[12,48,128]{2,1,0:T(8,128)S(1)}, u32[]{:S(2)}, u32[]{:S(2)}) collective-permute-start(f32[12,48,128]{2,1,0:T(8,128)S(1)} %get-tuple-element.52), channel_id=1, source_target_pairs={{1,0},{2,1},{3,2},{4,3},{5,4},{6,5},{7,6},{0,7},{9,8},{10,9},{11,1... | collective-permute-start | bytes 884744 | tf_op jit(solution)/shard_map/ppermute | solution.py:742
  29.6 4.7 %collective-permute-done.11.refs_2_ = f32[12,48,128]{2,1,0:T(8,128)S(1)} collective-permute-done((f32[12,48,128]{2,1,0:T(8,128)S(1)}, f32[12,48,128]{2,1,0:T(8,128)S(1)}, u32[]{:S(2)}, u32[]{:S(2)}) %collective-permute-start.11) | collective-permute-done | bytes 294944 | tf_op jit(solution)/shard_map/ppermute | solution.py:742
  34.2 4.5 %shard_map.79 = (f32[16,16,128]{2,1,0:T(8,128)S(1)}, f32[56,48,2,24,128]{4,3,2,1,0:T(8,128)}) custom-call(f32[96,48,128]{2,1,0:T(8,128)S(1)} %get-tuple-element.51.refs_0_, f32[12,48,128]{2,1,0:T(8,128)S(1)} %collective-permute-done.10.refs_1_, f32[12,48,128]{2,1,0:T(8,128)S(1)} %collective-permute-done.11.refs_2_, bf16[8,256,256]{2,1,0:T(8,128)(2,1)S(1)} %copy-done.3), custom_call_target="tpu_custom_call" | custom-call | tf_op jit(solution)/shard_map/pallas_call | solution.py:101
  46.0 3.8 %collective-permute-start.17 = (f32[64,512]{1,0:T(8,128)S(1)}, f32[64,512]{1,0:T(8,128)S(1)}, u32[]{:S(2)}, u32[]{:S(2)}) collective-permute-start(f32[64,512]{1,0:T(8,128)S(1)} %concatenate.23.refs_2_), channel_id=1, source_target_pairs={{1,0},{2,1},{3,2},{4,3},{5,4},{6,5},{7,6},{0,7},{9,8},{10,9},{11,1... | collective-permute-start | bytes 393224 | tf_op jit(solution)/shard_map/ppermute | solution.py:742
  49.7 2.6 %collective-permute-done.17.refs_4_ = f32[64,512]{1,0:T(8,128)S(1)} collective-permute-done((f32[64,512]{1,0:T(8,128)S(1)}, f32[64,512]{1,0:T(8,128)S(1)}, u32[]{:S(2)}, u32[]{:S(2)}) %collective-permute-start.17) | collective-permute-done | bytes 131104 | tf_op jit(solution)/shard_map/ppermute | solution.py:742
  54.3 6.4 %collective-permute-start.18 = (f32[11,2,24,128]{3,2,1,0:T(8,128)S(1)}, f32[11,2,24,128]{3,2,1,0:T(8,128)S(1)}, u32[]{:S(2)}, u32[]{:S(2)}) collective-permute-start(f32[11,2,24,128]{3,2,1,0:T(8,128)S(1)} %get-tuple-element.60), channel_id=1, source_target_pairs={{0,1},{1,2},{2,3},{3,4},{4,5},{5,6},{6,7},{7,0},{8,9},{9,10},{10,1... | collective-permute-start | bytes 811016 | tf_op jit(solution)/shard_map/ppermute | solution.py:742
  60.7 3.4 %collective-permute-done.18.refs_1_ = f32[11,2,24,128]{3,2,1,0:T(8,128)S(1)} collective-permute-done((f32[11,2,24,128]{3,2,1,0:T(8,128)S(1)}, f32[11,2,24,128]{3,2,1,0:T(8,128)S(1)}, u32[]{:S(2)}, u32[]{:S(2)}) %collective-permute-start.18) | collective-permute-done | bytes 270368 | tf_op jit(solution)/shard_map/ppermute | solution.py:742
  64.1 2.5 %collective-permute-done.19.refs_2_ = f32[11,2,24,128]{3,2,1,0:T(8,128)S(1)} collective-permute-done((f32[11,2,24,128]{3,2,1,0:T(8,128)S(1)}, f32[11,2,24,128]{3,2,1,0:T(8,128)S(1)}, u32[]{:S(2)}, u32[]{:S(2)}) %collective-permute-start.19) | collective-permute-done | bytes 270368 | tf_op jit(solution)/shard_map/ppermute | solution.py:742
  66.6 8.0 %shard_map.81 = (f32[512,128]{1,0:T(8,128)}, f32[60,44,2,24,128]{4,3,2,1,0:T(8,128)}) custom-call(f32[44,2,24,128]{3,2,1,0:T(8,128)S(1)} %get-tuple-element.59.refs_0_, f32[11,2,24,128]{3,2,1,0:T(8,128)S(1)} %collective-permute-done.18.refs_1_, f32[11,2,24,128]{3,2,1,0:T(8,128)S(1)} %collective-permute-done.19.refs_2_, bf16[4,384,256]{2,1,0:T(8,128)(2,1)S(1)} %copy-done.2), custom_call_target="tpu_custom_call" | custom-call | tf_op jit(solution)/shard_map/pallas_call | solution.py:101
  74.6 5.9 %all-to-all-start = ((f32[128,4,128]{2,1,0:T(4,128)}), f32[128,4,128]{2,1,0:T(4,128)S(1)}, u32[]{:S(2)}, u32[]{:S(2)}) async-start(f32[128,4,128]{2,1,0:T(4,128)} %bitcast), calls=%async_computation | async-start | bytes 524288 | tf_op jit(solution)/shard_map/all_to_all | solution.py:821
  80.6 10.8 %all-to-all-done = f32[128,4,128]{2,1,0:T(4,128)S(1)} async-done(((f32[128,4,128]{2,1,0:T(4,128)}), f32[128,4,128]{2,1,0:T(4,128)S(1)}, u32[]{:S(2)}, u32[]{:S(2)}) %all-to-all-start) | async-done | bytes 262176 | tf_op jit(solution)/shard_map/all_to_all | solution.py:821
  91.4 10.9 %shard_map.82 = (f32[16,16,128]{2,1,0:T(8,128)S(1)}, f32[8,8,128]{2,1,0:T(8,128)S(1)}, f32[48,2,24,128]{3,2,1,0:T(8,128)S(1)}, f32[8,16,128]{2,1,0:T(8,128)S(1)}, f32[8,128]{1,0:T(8,128)S(1)}) custom-call(f32[512,128]{1,0:T(8,128)S(1)} %bitcast.10, s32[3]{0:T(128)S(1)} %pad_add_fusion.refs_1_, f32[64,512]{1,0:T(8,128)S(1)} %concatenate.23.refs_2_, ...), custom_call_target="tpu_custom_call" | custom-call | tf_op jit(solution)/shard_map/pallas_call | solution.py:101
  102.6 2.4 %collective-permute-start.21 = (f32[8,16,128]{2,1,0:T(8,128)S(1)}, f32[8,16,128]{2,1,0:T(8,128)S(1)}, u32[]{:S(2)}, u32[]{:S(2)}) collective-permute-start(f32[8,16,128]{2,1,0:T(8,128)S(1)} %get-tuple-element.67), channel_id=1, source_target_pairs={{32,0},{64,32},{96,64},{0,96},{33,1},{65,33},{97,65},{1,97},{34,2}... | collective-permute-start | bytes 196616 | tf_op jit(solution)/shard_map/ppermute | solution.py:742
  108.2 3.1 %collective-permute-done.23.refs_2_ = f32[24,16,128]{2,1,0:T(8,128)S(1)} collective-permute-done((f32[24,16,128]{2,1,0:T(8,128)S(1)}, f32[24,16,128]{2,1,0:T(8,128)S(1)}, u32[]{:S(2)}, u32[]{:S(2)}) %collective-permute-start.23) | collective-permute-done | bytes 196640 | tf_op jit(solution)/shard_map/ppermute | solution.py:742
  111.3 2.4 %collective-permute-done.22.refs_1_ = f32[24,16,128]{2,1,0:T(8,128)S(1)} collective-permute-done((f32[24,16,128]{2,1,0:T(8,128)S(1)}, f32[24,16,128]{2,1,0:T(8,128)S(1)}, u32[]{:S(2)}, u32[]{:S(2)}) %collective-permute-start.22) | collective-permute-done | bytes 196640 | tf_op jit(solution)/shard_map/ppermute | solution.py:742
  114.1 3.5 %collective-permute-start.24 = (f32[6,2,24,128]{3,2,1,0:T(8,128)S(1)}, f32[6,2,24,128]{3,2,1,0:T(8,128)S(1)}, u32[]{:S(2)}, u32[]{:S(2)}) collective-permute-start(f32[6,2,24,128]{3,2,1,0:T(8,128)S(1)} %get-tuple-element.69), channel_id=1, source_target_pairs={{0,1},{1,2},{2,3},{3,4},{4,5},{5,6},{6,7},{7,0},{8,9},{9,10},{10,1... | collective-permute-start | bytes 442376 | tf_op jit(solution)/shard_map/ppermute | solution.py:742
  119.6 2.8 %collective-permute-done.25.refs_2_ = f32[6,2,24,128]{3,2,1,0:T(8,128)S(1)} collective-permute-done((f32[6,2,24,128]{3,2,1,0:T(8,128)S(1)}, f32[6,2,24,128]{3,2,1,0:T(8,128)S(1)}, u32[]{:S(2)}, u32[]{:S(2)}) %collective-permute-start.25) | collective-permute-done | bytes 147488 | tf_op jit(solution)/shard_map/ppermute | solution.py:742
  122.4 4.7 %shard_map.84 = (f32[44,2,24,128]{3,2,1,0:T(8,128)S(1)}, f32[44,24,128]{2,1,0:T(8,128)S(1)}, f32[20,24,128]{2,1,0:T(8,128)S(1)}, f32[20,24,128]{2,1,0:T(8,128)S(1)}, f32[256,128]{1,0:T(8,128)S(1)}) custom-call(f32[24,2,24,128]{3,2,1,0:T(8,128)S(1)} %get-tuple-element.68.refs_0_, f32[6,2,24,128]{3,2,1,0:T(8,128)S(1)} %collective-permute-done.24.refs_1_, ...), custom_call_target="tpu_custom_call" | custom-call | tf_op jit(solution)/shard_map/pallas_call | solution.py:101
  127.1 16.8 %all_to_all.31 = f32[128,2,128]{2,1,0:T(2,128)S(1)} all-to-all(f32[128,2,128]{2,1,0:T(2,128)S(1)} %bitcast.12), channel_id=1, replica_groups=mesh['gx'=4,'gy'=4,'gz'=8] {'gx','gy','gz'}, dimensions={0} | all-to-all | bytes 262144 | tf_op jit(solution)/shard_map/all_to_all | solution.py:840
  143.9 11.0 %shard_map.85 = (f32[32,32,128]{2,1,0:T(8,128)}, f32[128,128]{1,0:T(8,128)S(1)}) custom-call(f32[256,128]{1,0:T(8,128)S(1)} %bitcast.11, s32[3]{0:T(128)S(1)} %pad_add_fusion.refs_1_, f32[64,512]{1,0:T(8,128)S(1)} %concatenate.23.refs_2_, f32[64,512]{1,0:T(8,128)S(1)} %collective-permute-done.16.refs_3_, f32[64,512]{1,0:T(8,128)S(1)} %collective-permute-done.17.refs_4_, ...), custom_call_target="tpu_custom_call" | custom-call | tf_op jit(solution)/shard_map/pallas_call | solution.py:101
  155.0 13.6 %all_to_all.32 = f32[128,1,128]{2,1,0:T(1,128)S(1)} all-to-all(f32[128,1,128]{2,1,0:T(1,128)S(1)} %bitcast.13), channel_id=1, replica_groups=mesh['gx'=4,'gy'=4,'gz'=8] {'gx','gy','gz'}, dimensions={0} | all-to-all | bytes 131072 | tf_op jit(solution)/shard_map/all_to_all | solution.py:848
  (70 shorter events, 31.0 us)
Async XLA Ops:
  1.9 10.4 %collective-permute-start = (f32[16,32,128]{2,1,0:T(8,128)S(1)}, f32[16,32,128]{2,1,0:T(8,128)S(1)}, u32[]{:S(2)}, u32[]{:S(2)}) collective-permute-start(f32[16,32,128]{2,1,0:T(8,128)S(1)} %pad_maximum_fusion), channel_id=1, source_target_pairs={{0,32},{32,64},{64,96},{96,0},{1,33},{33,65},{65,97},{97,1},{2,34}... | collective-permute-start | bytes 786440 | tf_op jit(solution)/shard_map/ppermute | solution.py:742
  4.1 8.2 %collective-permute-start.1 = (f32[16,32,128]{2,1,0:T(8,128)S(1)}, f32[16,32,128]{2,1,0:T(8,128)S(1)}, u32[]{:S(2)}, u32[]{:S(2)}) collective-permute-start(f32[16,32,128]{2,1,0:T(8,128)S(1)} %pad_maximum_fusion.1), channel_id=1, source_target_pairs={{32,0},{64,32},{96,64},{0,96},{33,1},{65,33},{97,65},{1,97},{34,2}... | collective-permute-start | bytes 786440 | tf_op jit(solution)/shard_map/ppermute | solution.py:742
  5.7 5.6 %collective-permute-start.4 = (f32[4,512]{1,0:T(4,128)}, f32[4,512]{1,0:T(4,128)S(1)}, u32[]{:S(2)}, u32[]{:S(2)}) collective-permute-start(f32[4,512]{1,0:T(4,128)} %param.8), channel_id=1, source_target_pairs={{0,96},{32,0},{64,32},{96,64},{1,97},{33,1},{65,33},{97,65},{2,98}... | collective-permute-start | bytes 24584 | tf_op jit(solution)/shard_map/ppermute | solution.py:748
  7.1 5.2 %collective-permute-start.3 = (f32[4,512]{1,0:T(4,128)}, f32[4,512]{1,0:T(4,128)S(1)}, u32[]{:S(2)}, u32[]{:S(2)}) collective-permute-start(f32[4,512]{1,0:T(4,128)} %param.8), channel_id=1, source_target_pairs={{0,64},{32,96},{64,0},{96,32},{1,65},{33,97},{65,1},{97,33},{2,66}... | collective-permute-start | bytes 24584 | tf_op jit(solution)/shard_map/ppermute | solution.py:748
  7.5 4.9 %collective-permute-start.2 = (f32[4,512]{1,0:T(4,128)}, f32[4,512]{1,0:T(4,128)S(1)}, u32[]{:S(2)}, u32[]{:S(2)}) collective-permute-start(f32[4,512]{1,0:T(4,128)} %param.8), channel_id=1, source_target_pairs={{0,32},{32,64},{64,96},{96,0},{1,33},{33,65},{65,97},{97,1},{2,34}... | collective-permute-start | bytes 24584 | tf_op jit(solution)/shard_map/ppermute | solution.py:748
  12.4 11.3 %collective-permute-start.5 = (f32[96,8,128]{2,1,0:T(8,128)S(1)}, f32[96,8,128]{2,1,0:T(8,128)S(1)}, u32[]{:S(2)}, u32[]{:S(2)}) collective-permute-start(f32[96,8,128]{2,1,0:T(8,128)S(1)} %get-tuple-element.44), channel_id=1, source_target_pairs={{0,8},{8,16},{16,24},{24,0},{1,9},{9,17},{17,25},{25,1},{2,10},{10... | collective-permute-start | bytes 1179656 | tf_op jit(solution)/shard_map/ppermute | solution.py:742
  13.7 10.0 %collective-permute-start.6 = (f32[96,8,128]{2,1,0:T(8,128)S(1)}, f32[96,8,128]{2,1,0:T(8,128)S(1)}, u32[]{:S(2)}, u32[]{:S(2)}) collective-permute-start(f32[96,8,128]{2,1,0:T(8,128)S(1)} %get-tuple-element.45), channel_id=1, source_target_pairs={{8,0},{16,8},{24,16},{0,24},{9,1},{17,9},{25,17},{1,25},{10,2},{18... | collective-permute-start | bytes 1179656 | tf_op jit(solution)/shard_map/ppermute | solution.py:742
  15.2 7.5 %collective-permute-start.9 = (f32[16,512]{1,0:T(8,128)S(1)}, f32[16,512]{1,0:T(8,128)S(1)}, u32[]{:S(2)}, u32[]{:S(2)}) collective-permute-start(f32[16,512]{1,0:T(8,128)S(1)} %pad_maximum_fusion.2), channel_id=1, source_target_pairs={{0,24},{8,0},{16,8},{24,16},{1,25},{9,1},{17,9},{25,17},{2,26},{10... | collective-permute-start | bytes 98312 | tf_op jit(solution)/shard_map/ppermute | solution.py:748
  16.5 7.2 %collective-permute-start.8 = (f32[16,512]{1,0:T(8,128)S(1)}, f32[16,512]{1,0:T(8,128)S(1)}, u32[]{:S(2)}, u32[]{:S(2)}) collective-permute-start(f32[16,512]{1,0:T(8,128)S(1)} %pad_maximum_fusion.2), channel_id=1, source_target_pairs={{0,16},{8,24},{16,0},{24,8},{1,17},{9,25},{17,1},{25,9},{2,18},{10... | collective-permute-start | bytes 98312 | tf_op jit(solution)/shard_map/ppermute | solution.py:748
  17.0 6.7 %collective-permute-start.7 = (f32[16,512]{1,0:T(8,128)S(1)}, f32[16,512]{1,0:T(8,128)S(1)}, u32[]{:S(2)}, u32[]{:S(2)}) collective-permute-start(f32[16,512]{1,0:T(8,128)S(1)} %pad_maximum_fusion.2), channel_id=1, source_target_pairs={{0,8},{8,16},{16,24},{24,0},{1,9},{9,17},{17,25},{25,1},{2,10},{10... | collective-permute-start | bytes 98312 | tf_op jit(solution)/shard_map/ppermute | solution.py:748
  24.4 9.8 %collective-permute-start.11 = (f32[12,48,128]{2,1,0:T(8,128)S(1)}, f32[12,48,128]{2,1,0:T(8,128)S(1)}, u32[]{:S(2)}, u32[]{:S(2)}) collective-permute-start(f32[12,48,128]{2,1,0:T(8,128)S(1)} %get-tuple-element.52), channel_id=1, source_target_pairs={{1,0},{2,1},{3,2},{4,3},{5,4},{6,5},{7,6},{0,7},{9,8},{10,9},{11,1... | collective-permute-start | bytes 884744 | tf_op jit(solution)/shard_map/ppermute | solution.py:742
  28.0 6.2 %collective-permute-start.10 = (f32[12,48,128]{2,1,0:T(8,128)S(1)}, f32[12,48,128]{2,1,0:T(8,128)S(1)}, u32[]{:S(2)}, u32[]{:S(2)}) collective-permute-start(f32[12,48,128]{2,1,0:T(8,128)S(1)} %get-tuple-element.52), channel_id=1, source_target_pairs={{0,1},{1,2},{2,3},{3,4},{4,5},{5,6},{6,7},{7,0},{8,9},{9,10},{10,1... | collective-permute-start | bytes 884744 | tf_op jit(solution)/shard_map/ppermute | solution.py:742
  38.8 4.9 %collective-permute-start.12 = (f32[14,16,128]{2,1,0:T(8,128)S(1)}, f32[14,16,128]{2,1,0:T(8,128)S(1)}, u32[]{:S(2)}, u32[]{:S(2)}) collective-permute-start(f32[14,16,128]{2,1,0:T(8,128)S(1)} %get-tuple-element.87), channel_id=1, source_target_pairs={{0,32},{32,64},{64,96},{96,0},{1,33},{33,65},{65,97},{97,1},{2,34}... | collective-permute-start | bytes 344072 | tf_op jit(solution)/shard_map/ppermute | solution.py:742
  43.8 8.6 %collective-permute-start.15 = (f32[44,16,128]{2,1,0:T(8,128)S(1)}, f32[44,16,128]{2,1,0:T(8,128)S(1)}, u32[]{:S(2)}, u32[]{:S(2)}) collective-permute-start(f32[44,16,128]{2,1,0:T(8,128)S(1)} %constant_dynamic-update-slice_fusion.refs_0_), channel_id=1, source_target_pairs={{8,0},{16,8},{24,16},{0,24},{9,1},{17,9},{25,17},{1,25},{10,2},{18... | collective-permute-start | bytes 1081352 | tf_op jit(solution)/shard_map/ppermute | solution.py:742
  45.9 7.8 %collective-permute-start.14 = (f32[44,16,128]{2,1,0:T(8,128)S(1)}, f32[44,16,128]{2,1,0:T(8,128)S(1)}, u32[]{:S(2)}, u32[]{:S(2)}) collective-permute-start(f32[44,16,128]{2,1,0:T(8,128)S(1)} %constant_dynamic-update-slice_fusion.refs_0_), channel_id=1, source_target_pairs={{0,8},{8,16},{16,24},{24,0},{1,9},{9,17},{17,25},{25,1},{2,10},{10... | collective-permute-start | bytes 1081352 | tf_op jit(solution)/shard_map/ppermute | solution.py:742
  46.0 6.4 %collective-permute-start.17 = (f32[64,512]{1,0:T(8,128)S(1)}, f32[64,512]{1,0:T(8,128)S(1)}, u32[]{:S(2)}, u32[]{:S(2)}) collective-permute-start(f32[64,512]{1,0:T(8,128)S(1)} %concatenate.23.refs_2_), channel_id=1, source_target_pairs={{1,0},{2,1},{3,2},{4,3},{5,4},{6,5},{7,6},{0,7},{9,8},{10,9},{11,1... | collective-permute-start | bytes 393224 | tf_op jit(solution)/shard_map/ppermute | solution.py:742
  54.3 9.8 %collective-permute-start.18 = (f32[11,2,24,128]{3,2,1,0:T(8,128)S(1)}, f32[11,2,24,128]{3,2,1,0:T(8,128)S(1)}, u32[]{:S(2)}, u32[]{:S(2)}) collective-permute-start(f32[11,2,24,128]{3,2,1,0:T(8,128)S(1)} %get-tuple-element.60), channel_id=1, source_target_pairs={{0,1},{1,2},{2,3},{3,4},{4,5},{5,6},{6,7},{7,0},{8,9},{9,10},{10,1... | collective-permute-start | bytes 811016 | tf_op jit(solution)/shard_map/ppermute | solution.py:742
  60.7 5.9 %collective-permute-start.19 = (f32[11,2,24,128]{3,2,1,0:T(8,128)S(1)}, f32[11,2,24,128]{3,2,1,0:T(8,128)S(1)}, u32[]{:S(2)}, u32[]{:S(2)}) collective-permute-start(f32[11,2,24,128]{3,2,1,0:T(8,128)S(1)} %get-tuple-element.61), channel_id=1, source_target_pairs={{1,0},{2,1},{3,2},{4,3},{5,4},{6,5},{7,6},{0,7},{9,8},{10,9},{11,1... | collective-permute-start | bytes 811016 | tf_op jit(solution)/shard_map/ppermute | solution.py:742
  74.6 16.8 %all-to-all-start = ((f32[128,4,128]{2,1,0:T(4,128)}), f32[128,4,128]{2,1,0:T(4,128)S(1)}, u32[]{:S(2)}, u32[]{:S(2)}) async-start(f32[128,4,128]{2,1,0:T(4,128)} %bitcast), calls=%async_computation | async-start | bytes 524288 | tf_op jit(solution)/shard_map/all_to_all | solution.py:821
  102.3 4.4 %collective-permute-start.20 = (f32[8,16,128]{2,1,0:T(8,128)S(1)}, f32[8,16,128]{2,1,0:T(8,128)S(1)}, u32[]{:S(2)}, u32[]{:S(2)}) collective-permute-start(f32[8,16,128]{2,1,0:T(8,128)S(1)} %get-tuple-element.67), channel_id=1, source_target_pairs={{0,32},{32,64},{64,96},{96,0},{1,33},{33,65},{65,97},{97,1},{2,34}... | collective-permute-start | bytes 196616 | tf_op jit(solution)/shard_map/ppermute | solution.py:742
  106.7 4.6 %collective-permute-start.23 = (f32[24,16,128]{2,1,0:T(8,128)S(1)}, f32[24,16,128]{2,1,0:T(8,128)S(1)}, u32[]{:S(2)}, u32[]{:S(2)}) collective-permute-start(f32[24,16,128]{2,1,0:T(8,128)S(1)} %constant_dynamic-update-slice_fusion.3.refs_0_), channel_id=1, source_target_pairs={{8,0},{16,8},{24,16},{0,24},{9,1},{17,9},{25,17},{1,25},{10,2},{18... | collective-permute-start | bytes 589832 | tf_op jit(solution)/shard_map/ppermute | solution.py:742
  107.9 5.7 %collective-permute-start.22 = (f32[24,16,128]{2,1,0:T(8,128)S(1)}, f32[24,16,128]{2,1,0:T(8,128)S(1)}, u32[]{:S(2)}, u32[]{:S(2)}) collective-permute-start(f32[24,16,128]{2,1,0:T(8,128)S(1)} %constant_dynamic-update-slice_fusion.3.refs_0_), channel_id=1, source_target_pairs={{0,8},{8,16},{16,24},{24,0},{1,9},{9,17},{17,25},{25,1},{2,10},{10... | collective-permute-start | bytes 589832 | tf_op jit(solution)/shard_map/ppermute | solution.py:742
  114.1 5.6 %collective-permute-start.24 = (f32[6,2,24,128]{3,2,1,0:T(8,128)S(1)}, f32[6,2,24,128]{3,2,1,0:T(8,128)S(1)}, u32[]{:S(2)}, u32[]{:S(2)}) collective-permute-start(f32[6,2,24,128]{3,2,1,0:T(8,128)S(1)} %get-tuple-element.69), channel_id=1, source_target_pairs={{0,1},{1,2},{2,3},{3,4},{4,5},{5,6},{6,7},{7,0},{8,9},{9,10},{10,1... | collective-permute-start | bytes 442376 | tf_op jit(solution)/shard_map/ppermute | solution.py:742
  117.5 4.9 %collective-permute-start.25 = (f32[6,2,24,128]{3,2,1,0:T(8,128)S(1)}, f32[6,2,24,128]{3,2,1,0:T(8,128)S(1)}, u32[]{:S(2)}, u32[]{:S(2)}) collective-permute-start(f32[6,2,24,128]{3,2,1,0:T(8,128)S(1)} %get-tuple-element.70), channel_id=1, source_target_pairs={{1,0},{2,1},{3,2},{4,3},{5,4},{6,5},{7,6},{0,7},{9,8},{10,9},{11,1... | collective-permute-start | bytes 442376 | tf_op jit(solution)/shard_map/ppermute | solution.py:742
  (9 other events, 134.8 us)

commit v4 on v3

--- a/solution.py
+++ b/solution.py
@@ -18,6 +18,7 @@
 X2, Y2 = 20, 24
 GROUP0 = 8
 GROUP1 = 4
+BEGIN, END = 8, 36
 CELLS = 16777216.0
 
 
@@ -104,7 +105,7 @@
         in_specs=[spec(array) for array in inputs],
         out_specs=[pl.BlockSpec(memory_space=space) for space in spaces],
         scratch_shapes=work,
-        compiler_params=pltpu.CompilerParams(vmem_limit_bytes=32 * 1024 * 1024),
+        compiler_params=pltpu.CompilerParams(vmem_limit_bytes=20 * 1024 * 1024),
     )(*inputs)
     results = list(results)
     whole = results.pop() if park else None
@@ -154,6 +155,11 @@
     return (rest - mid.astype(F32)).astype(jnp.bfloat16), mid, high
 
 
+def halves(value):
+    high = value.astype(jnp.bfloat16)
+    return (value - high.astype(F32)).astype(jnp.bfloat16), high
+
+
 def move(pieces, matrix):
     total = None
     for parts in zip(*pieces):
@@ -212,8 +218,11 @@
             message[at + H0 + 32 : at + X0] = high[halo, cut]
 
 
-def pack_z0(f, s, low, high, below, above, split, message, rows, _):
-    block = (iota((Y0, LANES), 1) + 8) % LANES // 16
+def pack_z0(f, s, low, high, below, above, split, to_high, to_low, rows, _):
+    lane = iota((Y0, LANES), 1)
+    block = (lane + 8) % LANES // 16
+    last = lane // 8 % 2 == 1
+    pair = []
     for group in range(2 * X0 // GROUP0):
         packed = jnp.zeros((Y0, LANES), F32)
         for k in range(GROUP0):
@@ -234,19 +243,25 @@
             value = jnp.concatenate([even, odd], axis=0)
             split[item] = value
             packed = jnp.where(block == k, roll(value, 16 * k, 1), packed)
-        message[group] = packed
+        pair.append(packed)
+        if len(pair) == 2:
+            to_high[group // 2] = jnp.where(last, pair[0], roll(pair[1], 8, 1))
+            to_low[group // 2] = jnp.where(last, roll(pair[1], -8, 1), pair[0])
+            pair = []
 
 
 def down0(split, from_low, from_high, matrices, fr, fb, ir, ib, vb, own1, red, screen, copies):
     lane = iota((Y0, LANES), 1)
     groups = 2 * X0 // GROUP0
-    merged = [
-        jnp.where(lane // 8 % 2 == 1, from_low[group], from_high[group]) for group in range(groups)
-    ]
-    merged = thirds(jnp.concatenate(merged, axis=0))
+    merged = []
+    for half in range(groups // 2):
+        left, right = from_low[half], from_high[half]
+        merged.append(jnp.where(lane // 8 % 2 == 1, left, right))
+        merged.append(jnp.where(lane // 8 % 2 == 1, roll(left, -8, 1), roll(right, 8, 1)))
+    merged = halves(jnp.concatenate(merged, axis=0))
     for k in range(GROUP0):
         own = [split[group * GROUP0 + k] for group in range(groups)]
-        result = move([thirds(jnp.concatenate(own, axis=0)), merged], matrices[k])
+        result = move([halves(jnp.concatenate(own, axis=0)), merged], matrices[k])
         for group in range(groups):
             field, plane = divmod(group * GROUP0 + k, X0)
             part = result[Y0 * group : Y0 * group + Y0]
@@ -319,16 +334,20 @@
             to_low[group, colour] = down[colour]
 
 
-def unpack1(coloured, from_low, from_high, matrices, store):
-    items = coloured.shape[0]
-    rows = items // GROUP1 * 48
-    halos = [thirds(ref[...].reshape(rows, LANES)) for ref in (from_low, from_high)]
+def unpack1(coloured, from_low, from_high, matrices, store, first, last):
+    groups = range(first // GROUP1, last // GROUP1)
+    rows = len(groups) * 48
+    halos = [
+        halves(ref[groups.start : groups.stop].reshape(rows, LANES))
+        for ref in (from_low, from_high)
+    ]
     for k in range(GROUP1):
-        own = [coloured[item, colour] for item in range(k, items, GROUP1) for colour in (0, 1)]
-        result = move([thirds(jnp.concatenate(own, axis=0)), *halos], matrices[k])
-        for at in range(items // GROUP1 * 2):
+        own = [coloured[GROUP1 * g + k, colour] for g in groups for colour in (0, 1)]
+        result = move([halves(jnp.concatenate(own, axis=0)), *halos], matrices[k])
+        for at in range(2 * len(groups)):
             part = result[24 * at : 24 * at + 24]
-            store(at // 2 * GROUP1 + k, at % 2, (part[:, :LANES], part[:, LANES:]))
+            item = GROUP1 * groups[at // 2] + k
+            store(item, at % 2, (part[:, :LANES], part[:, LANES:]))
 
 
 def pair_index(rows):
@@ -344,24 +363,25 @@
     return 0.5 * pick(pairs, pair_index(Y2))
 
 
-def down12(f1, i1, b1, f2, i2, v2, red):
+def down12(f1, i1, b1, f2, i2, v2, red, begin, end):
     def first(p):
         red[p] = f1[p, 0] * i1[p, 0]
 
-    loop(0, X1, first, 4)
+    loop(begin, end, first, 4)
 
     def black(p, parity):
         b1[p] = (f1[p, 1] + sum1(red, p, parity, False)) * i1[p, 1]
 
-    black(1, 1)
-    plane_pairs(2, X1 - 2, black)
-    black(X1 - 2, 0)
+    black(begin + 1, 1)
+    plane_pairs(begin + 2, end - 2, black)
+    black(end - 2, 0)
 
     def restrict(i):
         plane = 2 * i + 2
         f2[i] = coarse12(sum1(b1, plane, 0, True) + sum1(b1, plane + 1, 1, True))
 
-    loop(0, X2, restrict, 4)
+    begin2, end2 = begin // 2, end // 2 - 2
+    loop(begin2, end2, restrict, 4)
 
     def red2(p):
         v2[p] = jnp.where(is_red((Y2, LANES), p), f2[p] * i2[p], 0.0)
@@ -370,8 +390,8 @@
         fresh = (f2[p] + sum2(v2, p)) * i2[p]
         v2[p] = jnp.where(is_red((Y2, LANES), p), v2[p], fresh)
 
-    loop(0, X2, red2, 4)
-    loop(1, X2 - 1, black2, 3)
+    loop(begin2, end2, red2, 4)
+    loop(begin2 + 1, end2 - 1, black2, 3)
 
 
 def coarse23(total, sums, x3):
@@ -396,43 +416,60 @@
     return [rows[0] + rows[1], rows[2] + rows[3]]
 
 
-def down12_first(coloured, from_low, from_high, matrices, f1, i1, b1, f2, i2, v2, message, red, sums, copies):
+def screens12(coloured, from_low, from_high, matrices, f1, i1, i2, begin, end):
     def store(plane, colour, halves):
         f1[plane, colour], i1[plane, colour] = halves
 
-    unpack1(coloured, from_low, from_high, matrices, store)
+    unpack1(coloured, from_low, from_high, matrices, store, begin, end)
 
     def screen2(i):
         plane = 2 * i + 2
         total = i1[plane, 0] + i1[plane, 1] + i1[plane + 1, 0] + i1[plane + 1, 1]
         i2[i] = coarse12(total)
 
-    loop(0, X2, screen2, 4)
+    loop(begin // 2, end // 2 - 2, screen2, 4)
+
+
+def invert12(i1, i2, begin, end):
+    def invert1(p):
+        i1[p] = 1.0 / (6.0 + i1[p])
+
+    def invert2(p):
+        i2[p] = 1.0 / (6.0 + i2[p])
+
+    loop(begin, end, invert1, 4)
+    loop(begin // 2, end // 2 - 2, invert2, 4)
+
+
+def first_message(
+    coloured, from_low, from_high, matrices, message, f1, i1, b1, f2, i2, v2, red, sums, _
+):
+    screens12(coloured, from_low, from_high, matrices, f1, i1, i2, BEGIN, END)
     rows = []
     for x3 in range(4):
         plane = 2 * x3 + H2
         rows.append(coarse23(i2[plane] + i2[plane + 1], sums, x3))
-
-    def invert1(p):
-        i1[p] = 1.0 / (6.0 + i1[p])
-
-    def invert2(p):
-        i2[p] = 1.0 / (6.0 + i2[p])
-
-    loop(0, X1, invert1, 4)
-    loop(0, X2, invert2, 4)
-    for at in (4, 5, 8):
-        copies[at].start()
-    down12(f1, i1, b1, f2, i2, v2, red)
-    for at in (6, 7, 9):
-        copies[at].start()
+    invert12(i1, i2, BEGIN, END)
+    down12(f1, i1, b1, f2, i2, v2, red, BEGIN, END)
     tile = source3(v2, sums) + [rows[0] + rows[1], rows[2] + rows[3]]
     tile = jnp.concatenate(tile + tile, axis=0)
     for i in range(64):
         message[8 * i : 8 * i + 8, :] = tile
 
 
-def down12_next(coloured, from_low, from_high, matrices, i1, i2, f1, b1, f2, v2, message, red, sums, copies):
+def down12_first(
+    coloured, from_low, from_high, matrices, f1, i1, b1, f2, i2, v2, red, copies
+):
+    screens12(coloured, from_low, from_high, matrices, f1, i1, i2, 0, X1)
+    invert12(i1, i2, 0, X1)
+    for at in (4, 5, 8):
+        copies[at].start()
+    down12(f1, i1, b1, f2, i2, v2, red, 0, X1)
+    for at in (6, 7, 9):
+        copies[at].start()
+
+
+def sources12(coloured, from_low, from_high, matrices, f1):
     def store(item, colour, halves):
         block, i = divmod(item, 8)
         for half in (0, 1):
@@ -440,10 +477,16 @@
             if 0 <= plane < X1:
                 f1[plane, colour] = halves[half]
 
-    unpack1(coloured, from_low, from_high, matrices, store)
+    unpack1(coloured, from_low, from_high, matrices, store, 0, 24)
+
+
+def down12_next(
+    coloured, from_low, from_high, matrices, i1, i2, f1, b1, f2, v2, message, red, sums, copies
+):
+    sources12(coloured, from_low, from_high, matrices, f1)
     for at in (4, 5):
         copies[at].wait()
-    down12(f1, i1, b1, f2, i2, v2, red)
+    down12(f1, i1, b1, f2, i2, v2, red, 0, X1)
     tile = jnp.concatenate(source3(v2, sums) * 4, axis=0)
     for i in range(32):
         message[8 * i : 8 * i + 8, :] = tile
@@ -521,7 +564,7 @@
     planes = []
     for x5 in range(4):
         z5 = lane % 64 // 2
-        index = (place[1] + 4 - sub // 2) % 4 * 16 + (place[0] + 4 - x5) % 4 * 4 + z5 % 4
+        index = (place[0] + 4 - x5) % 4 * 16 + (place[1] + 4 - sub // 2) % 4 * 4 + z5 % 4
         apart = (z5 // 4 + 8 - place[2]) % 8
         same = pick(answer[:, :LANES], index + jnp.where(apart == 7, 64, 0))
         part = jnp.where(apart == 1, pick(answer[:, LANES:], index), same)
@@ -679,9 +722,9 @@
 
 def final(
     message, place, near, before, after, f2, i2, v2, f1, i1, b1, fr, fb, ir, ib, b, i3, i4,
-    norm, matrix,
-    field, sums,
-    f3, e3, wide, tall, e2, er, eb, w, r, last, copies,
+    norm,
+    sums, r, last,
+    f3, e3, wide, tall, e2, er, eb, w, copies,
 ):
     unpack3(message, 2, 0, f3)
     coarse_solve(f3[...], i3[...], i4[...], place, (near, before, after), e3, wide)
@@ -717,6 +760,13 @@
 
     squared = own_sum(sum_over(squares))
 
+    low = iota((1, LANES), 1) < 64
+    both = jnp.where(low, roll(norm[0:1, :], -OWN, 1), roll(squared, 64 - OWN, 1))
+    for i in range(16):
+        sums[8 * i : 8 * i + 8, :] = jnp.broadcast_to(both, (8, LANES))
+
+
+def weave(r, last, matrix, field, _):
     def finish(i):
         parts = []
         for x in (0, 1):
@@ -729,10 +779,6 @@
             field[2 * i + at // 2 - H0, pl.ds(at % 2, 16, stride=2), :] = rows
 
     loop(H0 // 2, H0 // 2 + 16, finish)
-    low = iota((1, LANES), 1) < 64
-    both = jnp.where(low, roll(norm[0:1, :], -OWN, 1), roll(squared, 64 - OWN, 1))
-    for i in range(16):
-        sums[8 * i : 8 * i + 8, :] = jnp.broadcast_to(both, (8, LANES))
 
 
 def exchange(to_high, to_low, axis):
@@ -758,7 +804,7 @@
     own = jnp.concatenate([from_low, own, from_high], axis=0)
     below, above = exchange(own, own, "gy")
     if beside:
-        (below, above), beside = together((below, above), exchange(*beside, "gz"))
+        (above,), beside = together((above,), exchange(*beside, "gz"))
     items = own.shape[0]
     message = (items // GROUP1, 2, 24, LANES)
     coloured, to_high, to_low = call(
@@ -774,17 +820,17 @@
         jnp.concatenate([f[:H0], s[:H0]], axis=0),
         "gx",
     )
-    (low, high), others = together((low, high), from_all(coarse_inverse, "gx"))
+    messages = call(pack_y0, [(2 * X0, 8, LANES)] * 2, f, s, low, high)
+    messages, others = together(messages, from_all(coarse_inverse, "gy"))
     inverse = jnp.concatenate([coarse_inverse, *others], axis=0)
-    messages = call(pack_y0, [(2 * X0, 8, LANES)] * 2, f, s, low, high)
     below, above = exchange(*messages, "gy")
-    (below, above), others = together((below, above), from_all(inverse, "gy"))
+    (below, above), others = together((below, above), from_all(inverse, "gx"))
     inverse = jnp.concatenate([inverse, *others], axis=0)
     groups = 2 * X0 // GROUP0
     line0, line1, line2 = (Y0, LANES), (24, LANES), (Y2, LANES)
-    split, message = call(
+    split, to_high, to_low = call(
         pack_z0,
-        [(2 * X0, *line0), (groups, *line0)],
+        [(2 * X0, *line0), (groups // 2, *line0), (groups // 2, *line0)],
         *(f, s, low, high, below, above),
         scratch=[(16, *line0)],
     )
@@ -795,14 +841,22 @@
         down0,
         [Parked(level0, lambda ref, k=k: ref.at[k]) for k in range(5)] + [(16, 16, LANES)],
         split,
-        *exchange(message, message, "gz"),
+        *exchange(to_high, to_low, "gz"),
         jnp.asarray(lower_matrices(), jnp.bfloat16),
         scratch=[level0, (X0, *line1)],
         park=(56, *level0),
     )
     level1_parts, others = exchange1(own1, own1[:H1], own1[16 - H1 :], (inverse, inverse))
     inverse = (inverse, *others)
-    f1, i1, b1, f2, i2, v2, message = call(
+    (message,) = call(
+        first_message,
+        [(512, LANES)],
+        *level1_parts,
+        matrices1,
+        scratch=[both1, both1, level1, level2, level2, level2, level1, (4, *line2)],
+    )
+    message = lax.all_to_all(message, AXES, 0, 0, tiled=True)
+    f1, i1, b1, f2, i2, v2 = call(
         down12_first,
         [
             Parked(both1, lambda ref: ref.at[0]),
@@ -811,14 +865,12 @@
             Parked(level2, lambda ref: ref.at[2, 0:X2, 1]),
             Parked(level2, lambda ref: ref.at[3, 0:X2, 0]),
             Parked(level2, lambda ref: ref.at[3, 0:X2, 1]),
-            (512, LANES),
         ],
         *level1_parts,
         matrices1,
-        scratch=[level1, (4, *line2)],
+        scratch=[level1],
         park=(60, *both1),
     )
-    message = lax.all_to_all(message, AXES, 0, 0, tiled=True)
     whole = (16, 16, LANES)
     work = [whole, whole, (8, 16, LANES), (X0 // 2, *line1), level2, level1, level1]
     work += [level0, level0, level0]
@@ -838,14 +890,15 @@
         scratch=[level1, (4, *line2)],
     )
     message = lax.all_to_all(message, AXES, 0, 0, tiled=True)
-    field, sums = call(
+    sums, red, black = call(
         final,
-        [(32, 32, LANES), (128, LANES)],
+        [(128, LANES), level0, level0],
         message, place, *inverse, f2, i2, v2, f1, i1, b1, fr, fb, ir, ib, bnew, i3, i4, norm,
-        jnp.asarray(upper_matrix(), jnp.bfloat16),
-        scratch=work,
+        scratch=work[:-2],
     )
     sums = lax.all_to_all(sums, AXES, 0, 0, tiled=True)
+    matrix = jnp.asarray(upper_matrix(), jnp.bfloat16)
+    (field,) = call(weave, [(32, 32, LANES)], red, black, matrix)
     squares = jnp.sum(sums.reshape(128, 2, 64), axis=(0, 2))
     return field, jnp.sqrt(squares / CELLS)
 

time: 170 us -> 165 us (0.971)
  blocking collectives: 30.4 us -> 16.8 us
  Pallas kernels: 40.9 us -> 44.6 us
  waiting for transfers between devices: 49.7 us -> 53.2 us
  local copies, waits for them, and re-layouts: 1.44 us -> 3.16 us
    all_to_all x1 -> x0, blocking collectives: 13.6 us -> none  [local(): sums = lax.all_to_all(sums, AXES, 0, 0, tiled=True)]
    ppermute x20, waiting for transfers between devices: 28.7 us -> 36.9 us  [exchange(): return (lax.ppermute(to_high, axis, up), lax.ppermute(to_low, axis, down))]
    all_to_all x0 -> x1, waiting for transfers between devices: none -> 6.85 us  [local(): sums = lax.all_to_all(sums, AXES, 0, 0, tiled=True)]
    all_to_all x1, waiting for transfers between devices: 10.8 us -> 4.46 us  [local(): message = lax.all_to_all(message, AXES, 0, 0, tiled=True)]
    ppermute x20, starting transfers between devices: 34.4 us -> 28.5 us  [exchange(): return (lax.ppermute(to_high, axis, up), lax.ppermute(to_low, axis, down))]
    ppermute x6, waiting for transfers between devices: 10.2 us -> 4.97 us  [from_all(): return [lax.ppermute(own, axis, shift) for shift in shifts]]
    all_to_all x0 -> x1, starting transfers between devices: none -> 4.4 us  [local(): sums = lax.all_to_all(sums, AXES, 0, 0, tiled=True)]
    pallas_call x9 -> x11, Pallas kernels: 40.9 us -> 44.6 us  [call(): pl.pallas_call(kernel, out_shape=[jax.ShapeDtypeStruct(shape, F32) for sh...]
  transfers between devices with their start and end apart: 27 -> 28, of which waited for: 16 -> 21; matrix products, arithmetic and copies ran while one was open for 0% -> 0% of each run, Pallas kernels for 0% -> 5%
where the time goes in v4:
time: 165 us
  waiting for transfers between devices  53.2 us (32%)
  starting transfers between devices  45.6 us (28%)
  Pallas kernels  44.6 us (27%)
  blocking collectives  16.8 us (10%)
  local copies, waits for them, and re-layouts  3.16 us (2%)
    pallas_call x11, Pallas kernels, call(): pl.pallas_call(kernel, out_shape=[jax.ShapeDtypeStruct(shape, F32) for sh...  44.6 us
    ppermute x20, waiting for transfers between devices, exchange(): return (lax.ppermute(to_high, axis, up), lax.ppermute(to_low, axis, down))  36.9 us
    ppermute x20, starting transfers between devices, exchange(): return (lax.ppermute(to_high, axis, up), lax.ppermute(to_low, axis, down))  28.5 us
    all_to_all x1, blocking collectives, local(): message = lax.all_to_all(message, AXES, 0, 0, tiled=True)  16.8 us
    all_to_all x1, waiting for transfers between devices, local(): sums = lax.all_to_all(sums, AXES, 0, 0, tiled=True)  6.85 us
    all_to_all x1, starting transfers between devices, local(): message = lax.all_to_all(message, AXES, 0, 0, tiled=True)  6.57 us
    ppermute x6, starting transfers between devices, from_all(): return [lax.ppermute(own, axis, shift) for shift in shifts]  6.12 us
    ppermute x6, waiting for transfers between devices, from_all(): return [lax.ppermute(own, axis, shift) for shift in shifts]  4.97 us
  transfers between devices with their start and end apart: 28, of which 21 were waited for; matrix products, arithmetic and copies ran while one was open for 0% of the time, Pallas kernels for 5%

profile of v4, /device:TPU:1, one launch (start us, length us, event | category | flops | bytes accessed | tf_op | source)
XLA Modules:
  0.0 165.1 jit_solution(9889977986416099575)
XLA Ops:
  17.9 3.3 %collective-permute-done.8 = f32[16,512]{1,0:T(8,128)S(1)} collective-permute-done((f32[16,512]{1,0:T(8,128)S(1)}, f32[16,512]{1,0:T(8,128)S(1)}, u32[]{:S(2)}, u32[]{:S(2)}) %collective-permute-start.8) | collective-permute-done | bytes 32800 | tf_op jit(solution)/shard_map/ppermute | solution.py:794
  22.9 6.0 %collective-permute-start.10 = (f32[6,48,128]{2,1,0:T(8,128)S(1)}, f32[6,48,128]{2,1,0:T(8,128)S(1)}, u32[]{:S(2)}, u32[]{:S(2)}) collective-permute-start(f32[6,48,128]{2,1,0:T(8,128)S(1)} %get-tuple-element.51), channel_id=1, source_target_pairs={{0,1},{1,2},{2,3},{3,4},{4,5},{5,6},{6,7},{7,0},{8,9},{9,10},{10,1... | collective-permute-start | bytes 442376 | tf_op jit(solution)/shard_map/ppermute | solution.py:788
  33.4 3.9 %shard_map.79 = (f32[16,16,128]{2,1,0:T(8,128)S(1)}, f32[56,48,2,24,128]{4,3,2,1,0:T(8,128)}) custom-call(f32[96,48,128]{2,1,0:T(8,128)S(1)} %get-tuple-element.50.refs_0_, f32[6,48,128]{2,1,0:T(8,128)S(1)} %collective-permute-done.10.refs_1_, f32[6,48,128]{2,1,0:T(8,128)S(1)} %collective-permute-done.11.refs_2_, bf16[8,256,256]{2,1,0:T(8,128)(2,1)S(1)} %copy-done.3), custom_call_target="tpu_custom_call" | custom-call | tf_op jit(solution)/shard_map/pallas_call | solution.py:102
  37.5 2.7 %collective-permute-start.13 = (f32[14,16,128]{2,1,0:T(8,128)S(1)}, f32[14,16,128]{2,1,0:T(8,128)S(1)}, u32[]{:S(2)}, u32[]{:S(2)}) collective-permute-start(f32[14,16,128]{2,1,0:T(8,128)S(1)} %get-tuple-element.84), channel_id=1, source_target_pairs={{32,0},{64,32},{96,64},{0,96},{33,1},{65,33},{97,65},{1,97},{34,2}... | collective-permute-start | bytes 344072 | tf_op jit(solution)/shard_map/ppermute | solution.py:788
  40.1 3.5 %collective-permute-done.12 = f32[14,16,128]{2,1,0:T(8,128)S(1)} collective-permute-done((f32[14,16,128]{2,1,0:T(8,128)S(1)}, f32[14,16,128]{2,1,0:T(8,128)S(1)}, u32[]{:S(2)}, u32[]{:S(2)}) %collective-permute-start.12) | collective-permute-done | bytes 114720 | tf_op jit(solution)/shard_map/ppermute | solution.py:788
  47.3 2.9 %collective-permute-done.17.refs_4_ = f32[64,512]{1,0:T(8,128)S(1)} collective-permute-done((f32[64,512]{1,0:T(8,128)S(1)}, f32[64,512]{1,0:T(8,128)S(1)}, u32[]{:S(2)}, u32[]{:S(2)}) %collective-permute-start.17) | collective-permute-done | bytes 131104 | tf_op jit(solution)/shard_map/ppermute | solution.py:788
  50.2 3.0 %collective-permute-done.15.refs_2_ = f32[44,16,128]{2,1,0:T(8,128)S(1)} collective-permute-done((f32[44,16,128]{2,1,0:T(8,128)S(1)}, f32[44,16,128]{2,1,0:T(8,128)S(1)}, u32[]{:S(2)}, u32[]{:S(2)}) %collective-permute-start.15) | collective-permute-done | bytes 360480 | tf_op jit(solution)/shard_map/ppermute | solution.py:788
  53.2 2.6 %collective-permute-done.14.refs_1_ = f32[44,16,128]{2,1,0:T(8,128)S(1)} collective-permute-done((f32[44,16,128]{2,1,0:T(8,128)S(1)}, f32[44,16,128]{2,1,0:T(8,128)S(1)}, u32[]{:S(2)}, u32[]{:S(2)}) %collective-permute-start.14) | collective-permute-done | bytes 360480 | tf_op jit(solution)/shard_map/ppermute | solution.py:788
  60.2 3.4 %collective-permute-done.18.refs_1_ = f32[11,2,24,128]{3,2,1,0:T(8,128)S(1)} collective-permute-done((f32[11,2,24,128]{3,2,1,0:T(8,128)S(1)}, f32[11,2,24,128]{3,2,1,0:T(8,128)S(1)}, u32[]{:S(2)}, u32[]{:S(2)}) %collective-permute-start.18) | collective-permute-done | bytes 270368 | tf_op jit(solution)/shard_map/ppermute | solution.py:788
  63.6 2.8 %collective-permute-done.19.refs_2_ = f32[11,2,24,128]{3,2,1,0:T(8,128)S(1)} collective-permute-done((f32[11,2,24,128]{3,2,1,0:T(8,128)S(1)}, f32[11,2,24,128]{3,2,1,0:T(8,128)S(1)}, u32[]{:S(2)}, u32[]{:S(2)}) %collective-permute-start.19) | collective-permute-done | bytes 270368 | tf_op jit(solution)/shard_map/ppermute | solution.py:788
  66.4 4.5 %shard_map.81 = f32[512,128]{1,0:T(8,128)} custom-call(f32[44,2,24,128]{3,2,1,0:T(8,128)S(1)} %get-tuple-element.58.refs_0_, f32[11,2,24,128]{3,2,1,0:T(8,128)S(1)} %collective-permute-done.18.refs_1_, f32[11,2,24,128]{3,2,1,0:T(8,128)S(1)} %collective-permute-done.19.refs_2_, bf16[4,384,256]{2,1,0:T(8,128)(2,1)S(1)} %copy-done), custom_call_target="tpu_custom_call" | custom-call | tf_op jit(solution)/shard_map/pallas_call | solution.py:102
  70.9 6.6 %all-to-all-start = ((f32[128,4,128]{2,1,0:T(4,128)}), f32[128,4,128]{2,1,0:T(4,128)S(1)}, u32[]{:S(2)}, u32[]{:S(2)}) async-start(f32[128,4,128]{2,1,0:T(4,128)} %bitcast), calls=%async_computation | async-start | bytes 524288 | tf_op jit(solution)/shard_map/all_to_all | solution.py:858
  77.5 6.3 %shard_map.82.refs_5_.refs_4_.refs_6_ = f32[60,44,2,24,128]{4,3,2,1,0:T(8,128)} custom-call(f32[44,2,24,128]{3,2,1,0:T(8,128)S(1)} %get-tuple-element.58.refs_0_, f32[11,2,24,128]{3,2,1,0:T(8,128)S(1)} %collective-permute-done.18.refs_1_, f32[11,2,24,128]{3,2,1,0:T(8,128)S(1)} %collective-permute-done.19.refs_2_, bf16[4,384,256]{2,1,0:T(8,128)(2,1)S(1)} %copy-done), custom_call_target="tpu_custom_call" | custom-call | tf_op jit(solution)/shard_map/pallas_call | solution.py:102
  83.9 4.5 %all-to-all-done = f32[128,4,128]{2,1,0:T(4,128)S(1)} async-done(((f32[128,4,128]{2,1,0:T(4,128)}), f32[128,4,128]{2,1,0:T(4,128)S(1)}, u32[]{:S(2)}, u32[]{:S(2)}) %all-to-all-start) | async-done | bytes 262176 | tf_op jit(solution)/shard_map/all_to_all | solution.py:858
  88.3 10.9 %shard_map.83 = (f32[16,16,128]{2,1,0:T(8,128)S(1)}, f32[8,8,128]{2,1,0:T(8,128)S(1)}, f32[48,2,24,128]{3,2,1,0:T(8,128)S(1)}, f32[8,16,128]{2,1,0:T(8,128)S(1)}, f32[8,128]{1,0:T(8,128)S(1)}) custom-call(f32[512,128]{1,0:T(8,128)S(1)} %bitcast.10, s32[3]{0:T(128)S(1)} %pad_add_fusion.refs_1_, f32[64,512]{1,0:T(8,128)S(1)} %concatenate.23.refs_2_, ...), custom_call_target="tpu_custom_call" | custom-call | tf_op jit(solution)/shard_map/pallas_call | solution.py:102
  105.2 3.1 %collective-permute-done.23.refs_2_ = f32[24,16,128]{2,1,0:T(8,128)S(1)} collective-permute-done((f32[24,16,128]{2,1,0:T(8,128)S(1)}, f32[24,16,128]{2,1,0:T(8,128)S(1)}, u32[]{:S(2)}, u32[]{:S(2)}) %collective-permute-start.23) | collective-permute-done | bytes 196640 | tf_op jit(solution)/shard_map/ppermute | solution.py:788
  111.0 3.5 %collective-permute-start.24 = (f32[6,2,24,128]{3,2,1,0:T(8,128)S(1)}, f32[6,2,24,128]{3,2,1,0:T(8,128)S(1)}, u32[]{:S(2)}, u32[]{:S(2)}) collective-permute-start(f32[6,2,24,128]{3,2,1,0:T(8,128)S(1)} %get-tuple-element.66), channel_id=1, source_target_pairs={{0,1},{1,2},{2,3},{3,4},{4,5},{5,6},{6,7},{7,0},{8,9},{9,10},{10,1... | collective-permute-start | bytes 442376 | tf_op jit(solution)/shard_map/ppermute | solution.py:788
  116.6 2.8 %collective-permute-done.25.refs_2_ = f32[6,2,24,128]{3,2,1,0:T(8,128)S(1)} collective-permute-done((f32[6,2,24,128]{3,2,1,0:T(8,128)S(1)}, f32[6,2,24,128]{3,2,1,0:T(8,128)S(1)}, u32[]{:S(2)}, u32[]{:S(2)}) %collective-permute-start.25) | collective-permute-done | bytes 147488 | tf_op jit(solution)/shard_map/ppermute | solution.py:788
  119.4 5.0 %shard_map.85 = (f32[44,2,24,128]{3,2,1,0:T(8,128)S(1)}, f32[44,24,128]{2,1,0:T(8,128)S(1)}, f32[20,24,128]{2,1,0:T(8,128)S(1)}, f32[20,24,128]{2,1,0:T(8,128)S(1)}, f32[256,128]{1,0:T(8,128)S(1)}) custom-call(f32[24,2,24,128]{3,2,1,0:T(8,128)S(1)} %get-tuple-element.65.refs_0_, f32[6,2,24,128]{3,2,1,0:T(8,128)S(1)} %collective-permute-done.24.refs_1_, ...), custom_call_target="tpu_custom_call" | custom-call | tf_op jit(solution)/shard_map/pallas_call | solution.py:102
  124.4 16.8 %all_to_all.31 = f32[128,2,128]{2,1,0:T(2,128)S(1)} all-to-all(f32[128,2,128]{2,1,0:T(2,128)S(1)} %bitcast.12), channel_id=1, replica_groups=mesh['gx'=4,'gy'=4,'gz'=8] {'gx','gy','gz'}, dimensions={0} | all-to-all | bytes 262144 | tf_op jit(solution)/shard_map/all_to_all | solution.py:892
  141.2 9.1 %shard_map.86 = (f32[128,128]{1,0:T(8,128)}, f32[48,2,24,128]{3,2,1,0:T(8,128)S(1)}, f32[48,2,24,128]{3,2,1,0:T(8,128)S(1)}) custom-call(f32[256,128]{1,0:T(8,128)S(1)} %bitcast.11, s32[3]{0:T(128)S(1)} %pad_add_fusion.refs_1_, f32[64,512]{1,0:T(8,128)S(1)} %concatenate.23.refs_2_, f32[64,512]{1,0:T(8,128)S(1)} %collective-permute-done.16.refs_3_, ...), custom_call_target="tpu_custom_call" | custom-call | tf_op jit(solution)/shard_map/pallas_call | solution.py:102
  150.3 4.4 %all-to-all-start.2 = ((f32[128,1,128]{2,1,0:T(1,128)}), f32[128,1,128]{2,1,0:T(1,128)S(1)}, u32[]{:S(2)}, u32[]{:S(2)}) async-start(f32[128,1,128]{2,1,0:T(1,128)} %bitcast.8), calls=%async_computation.2 | async-start | bytes 131072 | tf_op jit(solution)/shard_map/all_to_all | solution.py:899
  154.7 2.7 %shard_map.87 = f32[32,32,128]{2,1,0:T(8,128)} custom-call(f32[48,2,24,128]{3,2,1,0:T(8,128)S(1)} %get-tuple-element.77.refs_0_, f32[48,2,24,128]{3,2,1,0:T(8,128)S(1)} %get-tuple-element.78.refs_1_, bf16[256,128]{1,0:T(8,128)(2,1)S(1)} %copy-done.6), custom_call_target="tpu_custom_call" | custom-call | tf_op jit(solution)/shard_map/pallas_call | solution.py:102
  157.4 6.8 %all-to-all-done.2 = f32[128,1,128]{2,1,0:T(1,128)S(1)} async-done(((f32[128,1,128]{2,1,0:T(1,128)}), f32[128,1,128]{2,1,0:T(1,128)S(1)}, u32[]{:S(2)}, u32[]{:S(2)}) %all-to-all-start.2) | async-done | bytes 65568 | tf_op jit(solution)/shard_map/all_to_all | solution.py:899
  (77 shorter events, 43.3 us)
Async XLA Ops:
  1.9 9.5 %collective-permute-start = (f32[16,32,128]{2,1,0:T(8,128)S(1)}, f32[16,32,128]{2,1,0:T(8,128)S(1)}, u32[]{:S(2)}, u32[]{:S(2)}) collective-permute-start(f32[16,32,128]{2,1,0:T(8,128)S(1)} %pad_maximum_fusion), channel_id=1, source_target_pairs={{0,32},{32,64},{64,96},{96,0},{1,33},{33,65},{65,97},{97,1},{2,34}... | collective-permute-start | bytes 786440 | tf_op jit(solution)/shard_map/ppermute | solution.py:788
  4.1 7.3 %collective-permute-start.1 = (f32[16,32,128]{2,1,0:T(8,128)S(1)}, f32[16,32,128]{2,1,0:T(8,128)S(1)}, u32[]{:S(2)}, u32[]{:S(2)}) collective-permute-start(f32[16,32,128]{2,1,0:T(8,128)S(1)} %pad_maximum_fusion.1), channel_id=1, source_target_pairs={{32,0},{64,32},{96,64},{0,96},{33,1},{65,33},{97,65},{1,97},{34,2}... | collective-permute-start | bytes 786440 | tf_op jit(solution)/shard_map/ppermute | solution.py:788
  5.7 5.8 %collective-permute-start.4 = (f32[4,512]{1,0:T(4,128)S(1)}, f32[4,512]{1,0:T(4,128)S(1)}, u32[]{:S(2)}, u32[]{:S(2)}) collective-permute-start(f32[4,512]{1,0:T(4,128)S(1)} %copy-done.7), channel_id=1, source_target_pairs={{0,24},{8,0},{16,8},{24,16},{1,25},{9,1},{17,9},{25,17},{2,26},{10... | collective-permute-start | bytes 24584 | tf_op jit(solution)/shard_map/ppermute | solution.py:794
  12.4 9.3 %collective-permute-start.5 = (f32[96,8,128]{2,1,0:T(8,128)S(1)}, f32[96,8,128]{2,1,0:T(8,128)S(1)}, u32[]{:S(2)}, u32[]{:S(2)}) collective-permute-start(f32[96,8,128]{2,1,0:T(8,128)S(1)} %get-tuple-element.43), channel_id=1, source_target_pairs={{0,8},{8,16},{16,24},{24,0},{1,9},{9,17},{17,25},{25,1},{2,10},{10... | collective-permute-start | bytes 1179656 | tf_op jit(solution)/shard_map/ppermute | solution.py:788
  12.7 9.0 %collective-permute-start.6 = (f32[96,8,128]{2,1,0:T(8,128)S(1)}, f32[96,8,128]{2,1,0:T(8,128)S(1)}, u32[]{:S(2)}, u32[]{:S(2)}) collective-permute-start(f32[96,8,128]{2,1,0:T(8,128)S(1)} %get-tuple-element.44), channel_id=1, source_target_pairs={{8,0},{16,8},{24,16},{0,24},{9,1},{17,9},{25,17},{1,25},{10,2},{18... | collective-permute-start | bytes 1179656 | tf_op jit(solution)/shard_map/ppermute | solution.py:788
  16.9 4.4 %collective-permute-start.8 = (f32[16,512]{1,0:T(8,128)S(1)}, f32[16,512]{1,0:T(8,128)S(1)}, u32[]{:S(2)}, u32[]{:S(2)}) collective-permute-start(f32[16,512]{1,0:T(8,128)S(1)} %pad_maximum_fusion.2), channel_id=1, source_target_pairs={{0,64},{32,96},{64,0},{96,32},{1,65},{33,97},{65,1},{97,33},{2,66}... | collective-permute-start | bytes 98312 | tf_op jit(solution)/shard_map/ppermute | solution.py:794
  17.1 4.6 %collective-permute-start.7 = (f32[16,512]{1,0:T(8,128)S(1)}, f32[16,512]{1,0:T(8,128)S(1)}, u32[]{:S(2)}, u32[]{:S(2)}) collective-permute-start(f32[16,512]{1,0:T(8,128)S(1)} %pad_maximum_fusion.2), channel_id=1, source_target_pairs={{0,32},{32,64},{64,96},{96,0},{1,33},{33,65},{65,97},{97,1},{2,34}... | collective-permute-start | bytes 98312 | tf_op jit(solution)/shard_map/ppermute | solution.py:794
  22.9 8.1 %collective-permute-start.10 = (f32[6,48,128]{2,1,0:T(8,128)S(1)}, f32[6,48,128]{2,1,0:T(8,128)S(1)}, u32[]{:S(2)}, u32[]{:S(2)}) collective-permute-start(f32[6,48,128]{2,1,0:T(8,128)S(1)} %get-tuple-element.51), channel_id=1, source_target_pairs={{0,1},{1,2},{2,3},{3,4},{4,5},{5,6},{6,7},{7,0},{8,9},{9,10},{10,1... | collective-permute-start | bytes 442376 | tf_op jit(solution)/shard_map/ppermute | solution.py:788
  28.8 4.6 %collective-permute-start.11 = (f32[6,48,128]{2,1,0:T(8,128)S(1)}, f32[6,48,128]{2,1,0:T(8,128)S(1)}, u32[]{:S(2)}, u32[]{:S(2)}) collective-permute-start(f32[6,48,128]{2,1,0:T(8,128)S(1)} %get-tuple-element.52), channel_id=1, source_target_pairs={{1,0},{2,1},{3,2},{4,3},{5,4},{6,5},{7,6},{0,7},{9,8},{10,9},{11,1... | collective-permute-start | bytes 442376 | tf_op jit(solution)/shard_map/ppermute | solution.py:788
  37.4 6.3 %collective-permute-start.12 = (f32[14,16,128]{2,1,0:T(8,128)S(1)}, f32[14,16,128]{2,1,0:T(8,128)S(1)}, u32[]{:S(2)}, u32[]{:S(2)}) collective-permute-start(f32[14,16,128]{2,1,0:T(8,128)S(1)} %get-tuple-element.85), channel_id=1, source_target_pairs={{0,32},{32,64},{64,96},{96,0},{1,33},{33,65},{65,97},{97,1},{2,34}... | collective-permute-start | bytes 344072 | tf_op jit(solution)/shard_map/ppermute | solution.py:788
  37.5 6.2 %collective-permute-start.13 = (f32[14,16,128]{2,1,0:T(8,128)S(1)}, f32[14,16,128]{2,1,0:T(8,128)S(1)}, u32[]{:S(2)}, u32[]{:S(2)}) collective-permute-start(f32[14,16,128]{2,1,0:T(8,128)S(1)} %get-tuple-element.84), channel_id=1, source_target_pairs={{32,0},{64,32},{96,64},{0,96},{33,1},{65,33},{97,65},{1,97},{34,2}... | collective-permute-start | bytes 344072 | tf_op jit(solution)/shard_map/ppermute | solution.py:788
  43.7 9.5 %collective-permute-start.15 = (f32[44,16,128]{2,1,0:T(8,128)S(1)}, f32[44,16,128]{2,1,0:T(8,128)S(1)}, u32[]{:S(2)}, u32[]{:S(2)}) collective-permute-start(f32[44,16,128]{2,1,0:T(8,128)S(1)} %constant_dynamic-update-slice_fusion.refs_0_), channel_id=1, source_target_pairs={{8,0},{16,8},{24,16},{0,24},{9,1},{17,9},{25,17},{1,25},{10,2},{18... | collective-permute-start | bytes 1081352 | tf_op jit(solution)/shard_map/ppermute | solution.py:788
  45.5 10.3 %collective-permute-start.14 = (f32[44,16,128]{2,1,0:T(8,128)S(1)}, f32[44,16,128]{2,1,0:T(8,128)S(1)}, u32[]{:S(2)}, u32[]{:S(2)}) collective-permute-start(f32[44,16,128]{2,1,0:T(8,128)S(1)} %constant_dynamic-update-slice_fusion.refs_0_), channel_id=1, source_target_pairs={{0,8},{8,16},{16,24},{24,0},{1,9},{9,17},{17,25},{25,1},{2,10},{10... | collective-permute-start | bytes 1081352 | tf_op jit(solution)/shard_map/ppermute | solution.py:788
  45.5 4.7 %collective-permute-start.17 = (f32[64,512]{1,0:T(8,128)S(1)}, f32[64,512]{1,0:T(8,128)S(1)}, u32[]{:S(2)}, u32[]{:S(2)}) collective-permute-start(f32[64,512]{1,0:T(8,128)S(1)} %concatenate.23.refs_2_), channel_id=1, source_target_pairs={{1,0},{2,1},{3,2},{4,3},{5,4},{6,5},{7,6},{0,7},{9,8},{10,9},{11,1... | collective-permute-start | bytes 393224 | tf_op jit(solution)/shard_map/ppermute | solution.py:788
  58.2 5.5 %collective-permute-start.18 = (f32[11,2,24,128]{3,2,1,0:T(8,128)S(1)}, f32[11,2,24,128]{3,2,1,0:T(8,128)S(1)}, u32[]{:S(2)}, u32[]{:S(2)}) collective-permute-start(f32[11,2,24,128]{3,2,1,0:T(8,128)S(1)} %get-tuple-element.59), channel_id=1, source_target_pairs={{0,1},{1,2},{2,3},{3,4},{4,5},{5,6},{6,7},{7,0},{8,9},{9,10},{10,1... | collective-permute-start | bytes 811016 | tf_op jit(solution)/shard_map/ppermute | solution.py:788
  60.2 6.2 %collective-permute-start.19 = (f32[11,2,24,128]{3,2,1,0:T(8,128)S(1)}, f32[11,2,24,128]{3,2,1,0:T(8,128)S(1)}, u32[]{:S(2)}, u32[]{:S(2)}) collective-permute-start(f32[11,2,24,128]{3,2,1,0:T(8,128)S(1)} %get-tuple-element.60), channel_id=1, source_target_pairs={{1,0},{2,1},{3,2},{4,3},{5,4},{6,5},{7,6},{0,7},{9,8},{10,9},{11,1... | collective-permute-start | bytes 811016 | tf_op jit(solution)/shard_map/ppermute | solution.py:788
  70.9 17.5 %all-to-all-start = ((f32[128,4,128]{2,1,0:T(4,128)}), f32[128,4,128]{2,1,0:T(4,128)S(1)}, u32[]{:S(2)}, u32[]{:S(2)}) async-start(f32[128,4,128]{2,1,0:T(4,128)} %bitcast), calls=%async_computation | async-start | bytes 524288 | tf_op jit(solution)/shard_map/all_to_all | solution.py:858
  99.2 4.4 %collective-permute-start.20 = (f32[8,16,128]{2,1,0:T(8,128)S(1)}, f32[8,16,128]{2,1,0:T(8,128)S(1)}, u32[]{:S(2)}, u32[]{:S(2)}) collective-permute-start(f32[8,16,128]{2,1,0:T(8,128)S(1)} %get-tuple-element.64), channel_id=1, source_target_pairs={{0,32},{32,64},{64,96},{96,0},{1,33},{33,65},{65,97},{97,1},{2,34}... | collective-permute-start | bytes 196616 | tf_op jit(solution)/shard_map/ppermute | solution.py:788
  99.6 4.0 %collective-permute-start.21 = (f32[8,16,128]{2,1,0:T(8,128)S(1)}, f32[8,16,128]{2,1,0:T(8,128)S(1)}, u32[]{:S(2)}, u32[]{:S(2)}) collective-permute-start(f32[8,16,128]{2,1,0:T(8,128)S(1)} %get-tuple-element.64), channel_id=1, source_target_pairs={{32,0},{64,32},{96,64},{0,96},{33,1},{65,33},{97,65},{1,97},{34,2}... | collective-permute-start | bytes 196616 | tf_op jit(solution)/shard_map/ppermute | solution.py:788
  103.6 4.6 %collective-permute-start.23 = (f32[24,16,128]{2,1,0:T(8,128)S(1)}, f32[24,16,128]{2,1,0:T(8,128)S(1)}, u32[]{:S(2)}, u32[]{:S(2)}) collective-permute-start(f32[24,16,128]{2,1,0:T(8,128)S(1)} %constant_dynamic-update-slice_fusion.3.refs_0_), channel_id=1, source_target_pairs={{8,0},{16,8},{24,16},{0,24},{9,1},{17,9},{25,17},{1,25},{10,2},{18... | collective-permute-start | bytes 589832 | tf_op jit(solution)/shard_map/ppermute | solution.py:788
  104.9 5.7 %collective-permute-start.22 = (f32[24,16,128]{2,1,0:T(8,128)S(1)}, f32[24,16,128]{2,1,0:T(8,128)S(1)}, u32[]{:S(2)}, u32[]{:S(2)}) collective-permute-start(f32[24,16,128]{2,1,0:T(8,128)S(1)} %constant_dynamic-update-slice_fusion.3.refs_0_), channel_id=1, source_target_pairs={{0,8},{8,16},{16,24},{24,0},{1,9},{9,17},{17,25},{25,1},{2,10},{10... | collective-permute-start | bytes 589832 | tf_op jit(solution)/shard_map/ppermute | solution.py:788
  111.0 5.6 %collective-permute-start.24 = (f32[6,2,24,128]{3,2,1,0:T(8,128)S(1)}, f32[6,2,24,128]{3,2,1,0:T(8,128)S(1)}, u32[]{:S(2)}, u32[]{:S(2)}) collective-permute-start(f32[6,2,24,128]{3,2,1,0:T(8,128)S(1)} %get-tuple-element.66), channel_id=1, source_target_pairs={{0,1},{1,2},{2,3},{3,4},{4,5},{5,6},{6,7},{7,0},{8,9},{9,10},{10,1... | collective-permute-start | bytes 442376 | tf_op jit(solution)/shard_map/ppermute | solution.py:788
  114.5 4.9 %collective-permute-start.25 = (f32[6,2,24,128]{3,2,1,0:T(8,128)S(1)}, f32[6,2,24,128]{3,2,1,0:T(8,128)S(1)}, u32[]{:S(2)}, u32[]{:S(2)}) collective-permute-start(f32[6,2,24,128]{3,2,1,0:T(8,128)S(1)} %get-tuple-element.67), channel_id=1, source_target_pairs={{1,0},{2,1},{3,2},{4,3},{5,4},{6,5},{7,6},{0,7},{9,8},{10,9},{11,1... | collective-permute-start | bytes 442376 | tf_op jit(solution)/shard_map/ppermute | solution.py:788
  150.3 13.9 %all-to-all-start.2 = ((f32[128,1,128]{2,1,0:T(1,128)}), f32[128,1,128]{2,1,0:T(1,128)S(1)}, u32[]{:S(2)}, u32[]{:S(2)}) async-start(f32[128,1,128]{2,1,0:T(1,128)} %bitcast.8), calls=%async_computation.2 | async-start | bytes 131072 | tf_op jit(solution)/shard_map/all_to_all | solution.py:899
  (12 other events, 103.6 us)

commit v5 on v4

--- a/solution.py
+++ b/solution.py
@@ -209,13 +209,38 @@
     return (iota(shape, 0) + iota(shape, 1) + plane) % 2 == 0
 
 
+TILES = 40
+
+
 def pack_y0(f, s, low, high, to_high, to_low, _):
+    row = iota((8, LANES), 0)
     for field, own in enumerate((f, s)):
-        at, halo = field * X0, slice(field * H0, field * H0 + H0)
-        for cut, message in ((slice(24, 32), to_high), (slice(0, 8), to_low)):
-            message[at : at + H0] = low[halo, cut]
-            message[at + H0 : at + H0 + 32] = own[:, cut]
-            message[at + H0 + 32 : at + X0] = high[halo, cut]
+        at = field * TILES
+        to_high[at : at + 32] = own[:, 24:32]
+        to_low[at : at + 32] = own[:, 0:8]
+        for side, halo in enumerate((low, high)):
+            first = field * H0 + (H0 if side == 0 else -1)
+            step = -1 if side == 0 else 1
+            for dx in range(1, 5):
+                near, far = first + step * dx, first + step * (8 - dx)
+                tile = at + 32 + 4 * side + dx - 1
+                above = roll(halo[far, 24:32], dx, 0)
+                to_high[tile] = jnp.where(row >= dx, halo[near, 24:32], above)
+                below = roll(halo[far, 0:8], 8 - dx, 0)
+                to_low[tile] = jnp.where(row < 8 - dx, halo[near, 0:8], below)
+
+
+def rows_y0(tiles, field, plane, above):
+    at = field * TILES
+    if H0 <= plane < H0 + 32:
+        return tiles[at + plane - H0]
+    side = 0 if plane < H0 else 1
+    dx = H0 - plane if side == 0 else plane - H0 - 31
+    tile = at + 31 + 4 * side
+    if dx <= 4:
+        return tiles[tile + dx]
+    near = max(8 - dx, 1)
+    return roll(tiles[tile + near], near - 8 if above else -near, 0)
 
 
 def pack_z0(f, s, low, high, below, above, split, to_high, to_low, rows, _):
@@ -230,14 +255,14 @@
             field, plane = divmod(item, X0)
             own = (f, s)[field]
             slot = item % 16
-            rows[slot, 0:8, :] = below[item]
+            rows[slot, 0:8, :] = rows_y0(below, field, plane, False)
             if plane < H0:
                 rows[slot, 8:40, :] = low[field * H0 + plane]
             elif plane < H0 + 32:
                 rows[slot, 8:40, :] = own[plane - H0]
             else:
                 rows[slot, 8:40, :] = high[field * H0 + plane - H0 - 32]
-            rows[slot, 40:48, :] = above[item]
+            rows[slot, 40:48, :] = rows_y0(above, field, plane, True)
             even = rows[slot, pl.ds(0, 24, stride=2), :]
             odd = rows[slot, pl.ds(1, 24, stride=2), :]
             value = jnp.concatenate([even, odd], axis=0)
@@ -820,7 +845,7 @@
         jnp.concatenate([f[:H0], s[:H0]], axis=0),
         "gx",
     )
-    messages = call(pack_y0, [(2 * X0, 8, LANES)] * 2, f, s, low, high)
+    messages = call(pack_y0, [(2 * TILES, 8, LANES)] * 2, f, s, low, high)
     messages, others = together(messages, from_all(coarse_inverse, "gy"))
     inverse = jnp.concatenate([coarse_inverse, *others], axis=0)
     below, above = exchange(*messages, "gy")

time: 165 us -> 164 us (level)
  transfers between devices with their start and end apart: 28 -> 28, of which waited for: 21 -> 21; matrix products, arithmetic and copies ran while one was open for 0% -> 0% of each run, Pallas kernels for 5% -> 6%
where the time goes in v5:
time: 164 us
  waiting for transfers between devices  52.1 us (32%)
  starting transfers between devices  45.3 us (28%)
  Pallas kernels  44.6 us (27%)
  blocking collectives  16.8 us (10%)
  local copies, waits for them, and re-layouts  3.16 us (2%)
    pallas_call x11, Pallas kernels, call(): pl.pallas_call(kernel, out_shape=[jax.ShapeDtypeStruct(shape, F32) for sh...  44.6 us
    ppermute x20, waiting for transfers between devices, exchange(): return (lax.ppermute(to_high, axis, up), lax.ppermute(to_low, axis, down))  35.8 us
    ppermute x20, starting transfers between devices, exchange(): return (lax.ppermute(to_high, axis, up), lax.ppermute(to_low, axis, down))  28.2 us
    all_to_all x1, blocking collectives, local(): message = lax.all_to_all(message, AXES, 0, 0, tiled=True)  16.8 us
    all_to_all x1, waiting for transfers between devices, local(): sums = lax.all_to_all(sums, AXES, 0, 0, tiled=True)  6.85 us
    all_to_all x1, starting transfers between devices, local(): message = lax.all_to_all(message, AXES, 0, 0, tiled=True)  6.57 us
    ppermute x6, starting transfers between devices, from_all(): return [lax.ppermute(own, axis, shift) for shift in shifts]  6.12 us
    ppermute x6, waiting for transfers between devices, from_all(): return [lax.ppermute(own, axis, shift) for shift in shifts]  4.97 us
  transfers between devices with their start and end apart: 28, of which 21 were waited for; matrix products, arithmetic and copies ran while one was open for 0% of the time, Pallas kernels for 6%

profile of v5, /device:TPU:1, one launch (start us, length us, event | category | flops | bytes accessed | tf_op | source)
XLA Modules:
  0.0 163.8 jit_solution(7028172955839373093)
XLA Ops:
  5.7 2.5 %collective-permute-start.4 = (f32[4,512]{1,0:T(4,128)S(1)}, f32[4,512]{1,0:T(4,128)S(1)}, u32[]{:S(2)}, u32[]{:S(2)}) collective-permute-start(f32[4,512]{1,0:T(4,128)S(1)} %copy-done.7), channel_id=1, source_target_pairs={{0,24},{8,0},{16,8},{24,16},{1,25},{9,1},{17,9},{25,17},{2,26},{10... | collective-permute-start | bytes 24584 | tf_op jit(solution)/shard_map/ppermute | solution.py:819
  17.9 3.3 %collective-permute-done.8 = f32[16,512]{1,0:T(8,128)S(1)} collective-permute-done((f32[16,512]{1,0:T(8,128)S(1)}, f32[16,512]{1,0:T(8,128)S(1)}, u32[]{:S(2)}, u32[]{:S(2)}) %collective-permute-start.8) | collective-permute-done | bytes 32800 | tf_op jit(solution)/shard_map/ppermute | solution.py:819
  22.9 6.0 %collective-permute-start.10 = (f32[6,48,128]{2,1,0:T(8,128)S(1)}, f32[6,48,128]{2,1,0:T(8,128)S(1)}, u32[]{:S(2)}, u32[]{:S(2)}) collective-permute-start(f32[6,48,128]{2,1,0:T(8,128)S(1)} %get-tuple-element.51), channel_id=1, source_target_pairs={{0,1},{1,2},{2,3},{3,4},{4,5},{5,6},{6,7},{7,0},{8,9},{9,10},{10,1... | collective-permute-start | bytes 442376 | tf_op jit(solution)/shard_map/ppermute | solution.py:813
  33.4 3.9 %shard_map.79 = (f32[16,16,128]{2,1,0:T(8,128)S(1)}, f32[56,48,2,24,128]{4,3,2,1,0:T(8,128)}) custom-call(f32[96,48,128]{2,1,0:T(8,128)S(1)} %get-tuple-element.50.refs_0_, f32[6,48,128]{2,1,0:T(8,128)S(1)} %collective-permute-done.10.refs_1_, f32[6,48,128]{2,1,0:T(8,128)S(1)} %collective-permute-done.11.refs_2_, bf16[8,256,256]{2,1,0:T(8,128)(2,1)S(1)} %copy-done.3), custom_call_target="tpu_custom_call" | custom-call | tf_op jit(solution)/shard_map/pallas_call | solution.py:102
  37.5 2.7 %collective-permute-start.13 = (f32[14,16,128]{2,1,0:T(8,128)S(1)}, f32[14,16,128]{2,1,0:T(8,128)S(1)}, u32[]{:S(2)}, u32[]{:S(2)}) collective-permute-start(f32[14,16,128]{2,1,0:T(8,128)S(1)} %get-tuple-element.84), channel_id=1, source_target_pairs={{32,0},{64,32},{96,64},{0,96},{33,1},{65,33},{97,65},{1,97},{34,2}... | collective-permute-start | bytes 344072 | tf_op jit(solution)/shard_map/ppermute | solution.py:813
  40.1 3.5 %collective-permute-done.12 = f32[14,16,128]{2,1,0:T(8,128)S(1)} collective-permute-done((f32[14,16,128]{2,1,0:T(8,128)S(1)}, f32[14,16,128]{2,1,0:T(8,128)S(1)}, u32[]{:S(2)}, u32[]{:S(2)}) %collective-permute-start.12) | collective-permute-done | bytes 114720 | tf_op jit(solution)/shard_map/ppermute | solution.py:813
  47.1 2.9 %collective-permute-done.17.refs_4_ = f32[64,512]{1,0:T(8,128)S(1)} collective-permute-done((f32[64,512]{1,0:T(8,128)S(1)}, f32[64,512]{1,0:T(8,128)S(1)}, u32[]{:S(2)}, u32[]{:S(2)}) %collective-permute-start.17) | collective-permute-done | bytes 131104 | tf_op jit(solution)/shard_map/ppermute | solution.py:813
  50.0 3.2 %collective-permute-done.15.refs_2_ = f32[44,16,128]{2,1,0:T(8,128)S(1)} collective-permute-done((f32[44,16,128]{2,1,0:T(8,128)S(1)}, f32[44,16,128]{2,1,0:T(8,128)S(1)}, u32[]{:S(2)}, u32[]{:S(2)}) %collective-permute-start.15) | collective-permute-done | bytes 360480 | tf_op jit(solution)/shard_map/ppermute | solution.py:813
  58.9 3.4 %collective-permute-done.18.refs_1_ = f32[11,2,24,128]{3,2,1,0:T(8,128)S(1)} collective-permute-done((f32[11,2,24,128]{3,2,1,0:T(8,128)S(1)}, f32[11,2,24,128]{3,2,1,0:T(8,128)S(1)}, u32[]{:S(2)}, u32[]{:S(2)}) %collective-permute-start.18) | collective-permute-done | bytes 270368 | tf_op jit(solution)/shard_map/ppermute | solution.py:813
  62.3 2.8 %collective-permute-done.19.refs_2_ = f32[11,2,24,128]{3,2,1,0:T(8,128)S(1)} collective-permute-done((f32[11,2,24,128]{3,2,1,0:T(8,128)S(1)}, f32[11,2,24,128]{3,2,1,0:T(8,128)S(1)}, u32[]{:S(2)}, u32[]{:S(2)}) %collective-permute-start.19) | collective-permute-done | bytes 270368 | tf_op jit(solution)/shard_map/ppermute | solution.py:813
  65.1 4.5 %shard_map.81 = f32[512,128]{1,0:T(8,128)} custom-call(f32[44,2,24,128]{3,2,1,0:T(8,128)S(1)} %get-tuple-element.58.refs_0_, f32[11,2,24,128]{3,2,1,0:T(8,128)S(1)} %collective-permute-done.18.refs_1_, f32[11,2,24,128]{3,2,1,0:T(8,128)S(1)} %collective-permute-done.19.refs_2_, bf16[4,384,256]{2,1,0:T(8,128)(2,1)S(1)} %copy-done), custom_call_target="tpu_custom_call" | custom-call | tf_op jit(solution)/shard_map/pallas_call | solution.py:102
  69.5 6.6 %all-to-all-start = ((f32[128,4,128]{2,1,0:T(4,128)}), f32[128,4,128]{2,1,0:T(4,128)S(1)}, u32[]{:S(2)}, u32[]{:S(2)}) async-start(f32[128,4,128]{2,1,0:T(4,128)} %bitcast), calls=%async_computation | async-start | bytes 524288 | tf_op jit(solution)/shard_map/all_to_all | solution.py:883
  76.2 6.3 %shard_map.82.refs_5_.refs_4_.refs_6_ = f32[60,44,2,24,128]{4,3,2,1,0:T(8,128)} custom-call(f32[44,2,24,128]{3,2,1,0:T(8,128)S(1)} %get-tuple-element.58.refs_0_, f32[11,2,24,128]{3,2,1,0:T(8,128)S(1)} %collective-permute-done.18.refs_1_, f32[11,2,24,128]{3,2,1,0:T(8,128)S(1)} %collective-permute-done.19.refs_2_, bf16[4,384,256]{2,1,0:T(8,128)(2,1)S(1)} %copy-done), custom_call_target="tpu_custom_call" | custom-call | tf_op jit(solution)/shard_map/pallas_call | solution.py:102
  82.5 4.5 %all-to-all-done = f32[128,4,128]{2,1,0:T(4,128)S(1)} async-done(((f32[128,4,128]{2,1,0:T(4,128)}), f32[128,4,128]{2,1,0:T(4,128)S(1)}, u32[]{:S(2)}, u32[]{:S(2)}) %all-to-all-start) | async-done | bytes 262176 | tf_op jit(solution)/shard_map/all_to_all | solution.py:883
  87.0 10.9 %shard_map.83 = (f32[16,16,128]{2,1,0:T(8,128)S(1)}, f32[8,8,128]{2,1,0:T(8,128)S(1)}, f32[48,2,24,128]{3,2,1,0:T(8,128)S(1)}, f32[8,16,128]{2,1,0:T(8,128)S(1)}, f32[8,128]{1,0:T(8,128)S(1)}) custom-call(f32[512,128]{1,0:T(8,128)S(1)} %bitcast.10, s32[3]{0:T(128)S(1)} %pad_add_fusion.refs_1_, f32[64,512]{1,0:T(8,128)S(1)} %concatenate.23.refs_2_, ...), custom_call_target="tpu_custom_call" | custom-call | tf_op jit(solution)/shard_map/pallas_call | solution.py:102
  103.8 3.1 %collective-permute-done.23.refs_2_ = f32[24,16,128]{2,1,0:T(8,128)S(1)} collective-permute-done((f32[24,16,128]{2,1,0:T(8,128)S(1)}, f32[24,16,128]{2,1,0:T(8,128)S(1)}, u32[]{:S(2)}, u32[]{:S(2)}) %collective-permute-start.23) | collective-permute-done | bytes 196640 | tf_op jit(solution)/shard_map/ppermute | solution.py:813
  109.6 3.5 %collective-permute-start.24 = (f32[6,2,24,128]{3,2,1,0:T(8,128)S(1)}, f32[6,2,24,128]{3,2,1,0:T(8,128)S(1)}, u32[]{:S(2)}, u32[]{:S(2)}) collective-permute-start(f32[6,2,24,128]{3,2,1,0:T(8,128)S(1)} %get-tuple-element.66), channel_id=1, source_target_pairs={{0,1},{1,2},{2,3},{3,4},{4,5},{5,6},{6,7},{7,0},{8,9},{9,10},{10,1... | collective-permute-start | bytes 442376 | tf_op jit(solution)/shard_map/ppermute | solution.py:813
  115.2 2.8 %collective-permute-done.25.refs_2_ = f32[6,2,24,128]{3,2,1,0:T(8,128)S(1)} collective-permute-done((f32[6,2,24,128]{3,2,1,0:T(8,128)S(1)}, f32[6,2,24,128]{3,2,1,0:T(8,128)S(1)}, u32[]{:S(2)}, u32[]{:S(2)}) %collective-permute-start.25) | collective-permute-done | bytes 147488 | tf_op jit(solution)/shard_map/ppermute | solution.py:813
  118.0 5.0 %shard_map.85 = (f32[44,2,24,128]{3,2,1,0:T(8,128)S(1)}, f32[44,24,128]{2,1,0:T(8,128)S(1)}, f32[20,24,128]{2,1,0:T(8,128)S(1)}, f32[20,24,128]{2,1,0:T(8,128)S(1)}, f32[256,128]{1,0:T(8,128)S(1)}) custom-call(f32[24,2,24,128]{3,2,1,0:T(8,128)S(1)} %get-tuple-element.65.refs_0_, f32[6,2,24,128]{3,2,1,0:T(8,128)S(1)} %collective-permute-done.24.refs_1_, ...), custom_call_target="tpu_custom_call" | custom-call | tf_op jit(solution)/shard_map/pallas_call | solution.py:102
  123.0 16.8 %all_to_all.31 = f32[128,2,128]{2,1,0:T(2,128)S(1)} all-to-all(f32[128,2,128]{2,1,0:T(2,128)S(1)} %bitcast.12), channel_id=1, replica_groups=mesh['gx'=4,'gy'=4,'gz'=8] {'gx','gy','gz'}, dimensions={0} | all-to-all | bytes 262144 | tf_op jit(solution)/shard_map/all_to_all | solution.py:917
  139.8 9.1 %shard_map.86 = (f32[128,128]{1,0:T(8,128)}, f32[48,2,24,128]{3,2,1,0:T(8,128)S(1)}, f32[48,2,24,128]{3,2,1,0:T(8,128)S(1)}) custom-call(f32[256,128]{1,0:T(8,128)S(1)} %bitcast.11, s32[3]{0:T(128)S(1)} %pad_add_fusion.refs_1_, f32[64,512]{1,0:T(8,128)S(1)} %concatenate.23.refs_2_, f32[64,512]{1,0:T(8,128)S(1)} %collective-permute-done.16.refs_3_, ...), custom_call_target="tpu_custom_call" | custom-call | tf_op jit(solution)/shard_map/pallas_call | solution.py:102
  148.9 4.4 %all-to-all-start.2 = ((f32[128,1,128]{2,1,0:T(1,128)}), f32[128,1,128]{2,1,0:T(1,128)S(1)}, u32[]{:S(2)}, u32[]{:S(2)}) async-start(f32[128,1,128]{2,1,0:T(1,128)} %bitcast.8), calls=%async_computation.2 | async-start | bytes 131072 | tf_op jit(solution)/shard_map/all_to_all | solution.py:924
  153.4 2.7 %shard_map.87 = f32[32,32,128]{2,1,0:T(8,128)} custom-call(f32[48,2,24,128]{3,2,1,0:T(8,128)S(1)} %get-tuple-element.77.refs_0_, f32[48,2,24,128]{3,2,1,0:T(8,128)S(1)} %get-tuple-element.78.refs_1_, bf16[256,128]{1,0:T(8,128)(2,1)S(1)} %copy-done.6), custom_call_target="tpu_custom_call" | custom-call | tf_op jit(solution)/shard_map/pallas_call | solution.py:102
  156.0 6.8 %all-to-all-done.2 = f32[128,1,128]{2,1,0:T(1,128)S(1)} async-done(((f32[128,1,128]{2,1,0:T(1,128)}), f32[128,1,128]{2,1,0:T(1,128)S(1)}, u32[]{:S(2)}, u32[]{:S(2)}) %all-to-all-start.2) | async-done | bytes 65568 | tf_op jit(solution)/shard_map/all_to_all | solution.py:924
  (77 shorter events, 41.8 us)
Async XLA Ops:
  1.9 9.5 %collective-permute-start = (f32[16,32,128]{2,1,0:T(8,128)S(1)}, f32[16,32,128]{2,1,0:T(8,128)S(1)}, u32[]{:S(2)}, u32[]{:S(2)}) collective-permute-start(f32[16,32,128]{2,1,0:T(8,128)S(1)} %pad_maximum_fusion), channel_id=1, source_target_pairs={{0,32},{32,64},{64,96},{96,0},{1,33},{33,65},{65,97},{97,1},{2,34}... | collective-permute-start | bytes 786440 | tf_op jit(solution)/shard_map/ppermute | solution.py:813
  4.1 7.3 %collective-permute-start.1 = (f32[16,32,128]{2,1,0:T(8,128)S(1)}, f32[16,32,128]{2,1,0:T(8,128)S(1)}, u32[]{:S(2)}, u32[]{:S(2)}) collective-permute-start(f32[16,32,128]{2,1,0:T(8,128)S(1)} %pad_maximum_fusion.1), channel_id=1, source_target_pairs={{32,0},{64,32},{96,64},{0,96},{33,1},{65,33},{97,65},{1,97},{34,2}... | collective-permute-start | bytes 786440 | tf_op jit(solution)/shard_map/ppermute | solution.py:813
  5.7 5.9 %collective-permute-start.4 = (f32[4,512]{1,0:T(4,128)S(1)}, f32[4,512]{1,0:T(4,128)S(1)}, u32[]{:S(2)}, u32[]{:S(2)}) collective-permute-start(f32[4,512]{1,0:T(4,128)S(1)} %copy-done.7), channel_id=1, source_target_pairs={{0,24},{8,0},{16,8},{24,16},{1,25},{9,1},{17,9},{25,17},{2,26},{10... | collective-permute-start | bytes 24584 | tf_op jit(solution)/shard_map/ppermute | solution.py:819
  12.4 9.3 %collective-permute-start.5 = (f32[80,8,128]{2,1,0:T(8,128)S(1)}, f32[80,8,128]{2,1,0:T(8,128)S(1)}, u32[]{:S(2)}, u32[]{:S(2)}) collective-permute-start(f32[80,8,128]{2,1,0:T(8,128)S(1)} %get-tuple-element.43), channel_id=1, source_target_pairs={{0,8},{8,16},{16,24},{24,0},{1,9},{9,17},{17,25},{25,1},{2,10},{10... | collective-permute-start | bytes 983048 | tf_op jit(solution)/shard_map/ppermute | solution.py:813
  12.7 9.0 %collective-permute-start.6 = (f32[80,8,128]{2,1,0:T(8,128)S(1)}, f32[80,8,128]{2,1,0:T(8,128)S(1)}, u32[]{:S(2)}, u32[]{:S(2)}) collective-permute-start(f32[80,8,128]{2,1,0:T(8,128)S(1)} %get-tuple-element.44), channel_id=1, source_target_pairs={{8,0},{16,8},{24,16},{0,24},{9,1},{17,9},{25,17},{1,25},{10,2},{18... | collective-permute-start | bytes 983048 | tf_op jit(solution)/shard_map/ppermute | solution.py:813
  16.9 4.4 %collective-permute-start.8 = (f32[16,512]{1,0:T(8,128)S(1)}, f32[16,512]{1,0:T(8,128)S(1)}, u32[]{:S(2)}, u32[]{:S(2)}) collective-permute-start(f32[16,512]{1,0:T(8,128)S(1)} %pad_maximum_fusion.2), channel_id=1, source_target_pairs={{0,64},{32,96},{64,0},{96,32},{1,65},{33,97},{65,1},{97,33},{2,66}... | collective-permute-start | bytes 98312 | tf_op jit(solution)/shard_map/ppermute | solution.py:819
  17.1 4.6 %collective-permute-start.7 = (f32[16,512]{1,0:T(8,128)S(1)}, f32[16,512]{1,0:T(8,128)S(1)}, u32[]{:S(2)}, u32[]{:S(2)}) collective-permute-start(f32[16,512]{1,0:T(8,128)S(1)} %pad_maximum_fusion.2), channel_id=1, source_target_pairs={{0,32},{32,64},{64,96},{96,0},{1,33},{33,65},{65,97},{97,1},{2,34}... | collective-permute-start | bytes 98312 | tf_op jit(solution)/shard_map/ppermute | solution.py:819
  22.9 8.1 %collective-permute-start.10 = (f32[6,48,128]{2,1,0:T(8,128)S(1)}, f32[6,48,128]{2,1,0:T(8,128)S(1)}, u32[]{:S(2)}, u32[]{:S(2)}) collective-permute-start(f32[6,48,128]{2,1,0:T(8,128)S(1)} %get-tuple-element.51), channel_id=1, source_target_pairs={{0,1},{1,2},{2,3},{3,4},{4,5},{5,6},{6,7},{7,0},{8,9},{9,10},{10,1... | collective-permute-start | bytes 442376 | tf_op jit(solution)/shard_map/ppermute | solution.py:813
  28.8 4.6 %collective-permute-start.11 = (f32[6,48,128]{2,1,0:T(8,128)S(1)}, f32[6,48,128]{2,1,0:T(8,128)S(1)}, u32[]{:S(2)}, u32[]{:S(2)}) collective-permute-start(f32[6,48,128]{2,1,0:T(8,128)S(1)} %get-tuple-element.52), channel_id=1, source_target_pairs={{1,0},{2,1},{3,2},{4,3},{5,4},{6,5},{7,6},{0,7},{9,8},{10,9},{11,1... | collective-permute-start | bytes 442376 | tf_op jit(solution)/shard_map/ppermute | solution.py:813
  37.4 6.3 %collective-permute-start.12 = (f32[14,16,128]{2,1,0:T(8,128)S(1)}, f32[14,16,128]{2,1,0:T(8,128)S(1)}, u32[]{:S(2)}, u32[]{:S(2)}) collective-permute-start(f32[14,16,128]{2,1,0:T(8,128)S(1)} %get-tuple-element.85), channel_id=1, source_target_pairs={{0,32},{32,64},{64,96},{96,0},{1,33},{33,65},{65,97},{97,1},{2,34}... | collective-permute-start | bytes 344072 | tf_op jit(solution)/shard_map/ppermute | solution.py:813
  37.5 6.2 %collective-permute-start.13 = (f32[14,16,128]{2,1,0:T(8,128)S(1)}, f32[14,16,128]{2,1,0:T(8,128)S(1)}, u32[]{:S(2)}, u32[]{:S(2)}) collective-permute-start(f32[14,16,128]{2,1,0:T(8,128)S(1)} %get-tuple-element.84), channel_id=1, source_target_pairs={{32,0},{64,32},{96,64},{0,96},{33,1},{65,33},{97,65},{1,97},{34,2}... | collective-permute-start | bytes 344072 | tf_op jit(solution)/shard_map/ppermute | solution.py:813
  43.7 9.5 %collective-permute-start.15 = (f32[44,16,128]{2,1,0:T(8,128)S(1)}, f32[44,16,128]{2,1,0:T(8,128)S(1)}, u32[]{:S(2)}, u32[]{:S(2)}) collective-permute-start(f32[44,16,128]{2,1,0:T(8,128)S(1)} %constant_dynamic-update-slice_fusion.refs_0_), channel_id=1, source_target_pairs={{8,0},{16,8},{24,16},{0,24},{9,1},{17,9},{25,17},{1,25},{10,2},{18... | collective-permute-start | bytes 1081352 | tf_op jit(solution)/shard_map/ppermute | solution.py:813
  44.1 10.3 %collective-permute-start.14 = (f32[44,16,128]{2,1,0:T(8,128)S(1)}, f32[44,16,128]{2,1,0:T(8,128)S(1)}, u32[]{:S(2)}, u32[]{:S(2)}) collective-permute-start(f32[44,16,128]{2,1,0:T(8,128)S(1)} %constant_dynamic-update-slice_fusion.refs_0_), channel_id=1, source_target_pairs={{0,8},{8,16},{16,24},{24,0},{1,9},{9,17},{17,25},{25,1},{2,10},{10... | collective-permute-start | bytes 1081352 | tf_op jit(solution)/shard_map/ppermute | solution.py:813
  45.3 4.7 %collective-permute-start.17 = (f32[64,512]{1,0:T(8,128)S(1)}, f32[64,512]{1,0:T(8,128)S(1)}, u32[]{:S(2)}, u32[]{:S(2)}) collective-permute-start(f32[64,512]{1,0:T(8,128)S(1)} %concatenate.23.refs_2_), channel_id=1, source_target_pairs={{1,0},{2,1},{3,2},{4,3},{5,4},{6,5},{7,6},{0,7},{9,8},{10,9},{11,1... | collective-permute-start | bytes 393224 | tf_op jit(solution)/shard_map/ppermute | solution.py:813
  56.8 5.5 %collective-permute-start.18 = (f32[11,2,24,128]{3,2,1,0:T(8,128)S(1)}, f32[11,2,24,128]{3,2,1,0:T(8,128)S(1)}, u32[]{:S(2)}, u32[]{:S(2)}) collective-permute-start(f32[11,2,24,128]{3,2,1,0:T(8,128)S(1)} %get-tuple-element.59), channel_id=1, source_target_pairs={{0,1},{1,2},{2,3},{3,4},{4,5},{5,6},{6,7},{7,0},{8,9},{9,10},{10,1... | collective-permute-start | bytes 811016 | tf_op jit(solution)/shard_map/ppermute | solution.py:813
  58.9 6.2 %collective-permute-start.19 = (f32[11,2,24,128]{3,2,1,0:T(8,128)S(1)}, f32[11,2,24,128]{3,2,1,0:T(8,128)S(1)}, u32[]{:S(2)}, u32[]{:S(2)}) collective-permute-start(f32[11,2,24,128]{3,2,1,0:T(8,128)S(1)} %get-tuple-element.60), channel_id=1, source_target_pairs={{1,0},{2,1},{3,2},{4,3},{5,4},{6,5},{7,6},{0,7},{9,8},{10,9},{11,1... | collective-permute-start | bytes 811016 | tf_op jit(solution)/shard_map/ppermute | solution.py:813
  69.5 17.5 %all-to-all-start = ((f32[128,4,128]{2,1,0:T(4,128)}), f32[128,4,128]{2,1,0:T(4,128)S(1)}, u32[]{:S(2)}, u32[]{:S(2)}) async-start(f32[128,4,128]{2,1,0:T(4,128)} %bitcast), calls=%async_computation | async-start | bytes 524288 | tf_op jit(solution)/shard_map/all_to_all | solution.py:883
  97.9 4.4 %collective-permute-start.20 = (f32[8,16,128]{2,1,0:T(8,128)S(1)}, f32[8,16,128]{2,1,0:T(8,128)S(1)}, u32[]{:S(2)}, u32[]{:S(2)}) collective-permute-start(f32[8,16,128]{2,1,0:T(8,128)S(1)} %get-tuple-element.64), channel_id=1, source_target_pairs={{0,32},{32,64},{64,96},{96,0},{1,33},{33,65},{65,97},{97,1},{2,34}... | collective-permute-start | bytes 196616 | tf_op jit(solution)/shard_map/ppermute | solution.py:813
  98.2 4.0 %collective-permute-start.21 = (f32[8,16,128]{2,1,0:T(8,128)S(1)}, f32[8,16,128]{2,1,0:T(8,128)S(1)}, u32[]{:S(2)}, u32[]{:S(2)}) collective-permute-start(f32[8,16,128]{2,1,0:T(8,128)S(1)} %get-tuple-element.64), channel_id=1, source_target_pairs={{32,0},{64,32},{96,64},{0,96},{33,1},{65,33},{97,65},{1,97},{34,2}... | collective-permute-start | bytes 196616 | tf_op jit(solution)/shard_map/ppermute | solution.py:813
  102.3 4.6 %collective-permute-start.23 = (f32[24,16,128]{2,1,0:T(8,128)S(1)}, f32[24,16,128]{2,1,0:T(8,128)S(1)}, u32[]{:S(2)}, u32[]{:S(2)}) collective-permute-start(f32[24,16,128]{2,1,0:T(8,128)S(1)} %constant_dynamic-update-slice_fusion.3.refs_0_), channel_id=1, source_target_pairs={{8,0},{16,8},{24,16},{0,24},{9,1},{17,9},{25,17},{1,25},{10,2},{18... | collective-permute-start | bytes 589832 | tf_op jit(solution)/shard_map/ppermute | solution.py:813
  103.5 5.7 %collective-permute-start.22 = (f32[24,16,128]{2,1,0:T(8,128)S(1)}, f32[24,16,128]{2,1,0:T(8,128)S(1)}, u32[]{:S(2)}, u32[]{:S(2)}) collective-permute-start(f32[24,16,128]{2,1,0:T(8,128)S(1)} %constant_dynamic-update-slice_fusion.3.refs_0_), channel_id=1, source_target_pairs={{0,8},{8,16},{16,24},{24,0},{1,9},{9,17},{17,25},{25,1},{2,10},{10... | collective-permute-start | bytes 589832 | tf_op jit(solution)/shard_map/ppermute | solution.py:813
  109.6 5.6 %collective-permute-start.24 = (f32[6,2,24,128]{3,2,1,0:T(8,128)S(1)}, f32[6,2,24,128]{3,2,1,0:T(8,128)S(1)}, u32[]{:S(2)}, u32[]{:S(2)}) collective-permute-start(f32[6,2,24,128]{3,2,1,0:T(8,128)S(1)} %get-tuple-element.66), channel_id=1, source_target_pairs={{0,1},{1,2},{2,3},{3,4},{4,5},{5,6},{6,7},{7,0},{8,9},{9,10},{10,1... | collective-permute-start | bytes 442376 | tf_op jit(solution)/shard_map/ppermute | solution.py:813
  113.1 4.9 %collective-permute-start.25 = (f32[6,2,24,128]{3,2,1,0:T(8,128)S(1)}, f32[6,2,24,128]{3,2,1,0:T(8,128)S(1)}, u32[]{:S(2)}, u32[]{:S(2)}) collective-permute-start(f32[6,2,24,128]{3,2,1,0:T(8,128)S(1)} %get-tuple-element.67), channel_id=1, source_target_pairs={{1,0},{2,1},{3,2},{4,3},{5,4},{6,5},{7,6},{0,7},{9,8},{10,9},{11,1... | collective-permute-start | bytes 442376 | tf_op jit(solution)/shard_map/ppermute | solution.py:813
  148.9 13.9 %all-to-all-start.2 = ((f32[128,1,128]{2,1,0:T(1,128)}), f32[128,1,128]{2,1,0:T(1,128)S(1)}, u32[]{:S(2)}, u32[]{:S(2)}) async-start(f32[128,1,128]{2,1,0:T(1,128)} %bitcast.8), calls=%async_computation.2 | async-start | bytes 131072 | tf_op jit(solution)/shard_map/all_to_all | solution.py:924
  (12 other events, 105.6 us)

commit v6 on v5

--- a/solution.py
+++ b/solution.py
@@ -34,7 +34,7 @@
     return jnp.take_along_axis(value, index, axis=1, mode="promise_in_bounds")
 
 
-def loop(start, stop, body, unroll=2):
+def loop(start, stop, body, unroll=4):
     def step(index, carry):
         body(index)
         return carry

time: 164 us -> 164 us (level)
  transfers between devices with their start and end apart: 28 -> 28, of which waited for: 21 -> 21; matrix products, arithmetic and copies ran while one was open for 0% -> 0% of each run, Pallas kernels for 6% -> 5%
where the time goes in v6:
time: 164 us
  waiting for transfers between devices  52.7 us (32%)
  starting transfers between devices  45.3 us (28%)
  Pallas kernels  43.8 us (27%)
  blocking collectives  16.8 us (10%)
  local copies, waits for them, and re-layouts  3.16 us (2%)
    pallas_call x11, Pallas kernels, call(): pl.pallas_call(kernel, out_shape=[jax.ShapeDtypeStruct(shape, F32) for sh...  43.8 us
    ppermute x20, waiting for transfers between devices, exchange(): return (lax.ppermute(to_high, axis, up), lax.ppermute(to_low, axis, down))  35.8 us
    ppermute x20, starting transfers between devices, exchange(): return (lax.ppermute(to_high, axis, up), lax.ppermute(to_low, axis, down))  28.2 us
    all_to_all x1, blocking collectives, local(): message = lax.all_to_all(message, AXES, 0, 0, tiled=True)  16.8 us
    all_to_all x1, waiting for transfers between devices, local(): sums = lax.all_to_all(sums, AXES, 0, 0, tiled=True)  7.45 us
    all_to_all x1, starting transfers between devices, local(): message = lax.all_to_all(message, AXES, 0, 0, tiled=True)  6.57 us
    ppermute x6, starting transfers between devices, from_all(): return [lax.ppermute(own, axis, shift) for shift in shifts]  6.12 us
    ppermute x6, waiting for transfers between devices, from_all(): return [lax.ppermute(own, axis, shift) for shift in shifts]  4.97 us
  transfers between devices with their start and end apart: 28, of which 21 were waited for; matrix products, arithmetic and copies ran while one was open for 0% of the time, Pallas kernels for 5%

profile of v6, /device:TPU:1, one launch (start us, length us, event | category | flops | bytes accessed | tf_op | source)
XLA Modules:
  0.0 163.5 jit_solution(15463925115275846250)
XLA Ops:
  5.7 2.5 %collective-permute-start.4 = (f32[4,512]{1,0:T(4,128)S(1)}, f32[4,512]{1,0:T(4,128)S(1)}, u32[]{:S(2)}, u32[]{:S(2)}) collective-permute-start(f32[4,512]{1,0:T(4,128)S(1)} %copy-done.7), channel_id=1, source_target_pairs={{0,24},{8,0},{16,8},{24,16},{1,25},{9,1},{17,9},{25,17},{2,26},{10... | collective-permute-start | bytes 24584 | tf_op jit(solution)/shard_map/ppermute | solution.py:819
  17.9 3.3 %collective-permute-done.8 = f32[16,512]{1,0:T(8,128)S(1)} collective-permute-done((f32[16,512]{1,0:T(8,128)S(1)}, f32[16,512]{1,0:T(8,128)S(1)}, u32[]{:S(2)}, u32[]{:S(2)}) %collective-permute-start.8) | collective-permute-done | bytes 32800 | tf_op jit(solution)/shard_map/ppermute | solution.py:819
  22.9 6.0 %collective-permute-start.10 = (f32[6,48,128]{2,1,0:T(8,128)S(1)}, f32[6,48,128]{2,1,0:T(8,128)S(1)}, u32[]{:S(2)}, u32[]{:S(2)}) collective-permute-start(f32[6,48,128]{2,1,0:T(8,128)S(1)} %get-tuple-element.51), channel_id=1, source_target_pairs={{0,1},{1,2},{2,3},{3,4},{4,5},{5,6},{6,7},{7,0},{8,9},{9,10},{10,1... | collective-permute-start | bytes 442376 | tf_op jit(solution)/shard_map/ppermute | solution.py:813
  30.9 2.5 %collective-permute-done.11.refs_2_ = f32[6,48,128]{2,1,0:T(8,128)S(1)} collective-permute-done((f32[6,48,128]{2,1,0:T(8,128)S(1)}, f32[6,48,128]{2,1,0:T(8,128)S(1)}, u32[]{:S(2)}, u32[]{:S(2)}) %collective-permute-start.11) | collective-permute-done | bytes 147488 | tf_op jit(solution)/shard_map/ppermute | solution.py:813
  33.4 3.9 %shard_map.79 = (f32[16,16,128]{2,1,0:T(8,128)S(1)}, f32[56,48,2,24,128]{4,3,2,1,0:T(8,128)}) custom-call(f32[96,48,128]{2,1,0:T(8,128)S(1)} %get-tuple-element.50.refs_0_, f32[6,48,128]{2,1,0:T(8,128)S(1)} %collective-permute-done.10.refs_1_, f32[6,48,128]{2,1,0:T(8,128)S(1)} %collective-permute-done.11.refs_2_, bf16[8,256,256]{2,1,0:T(8,128)(2,1)S(1)} %copy-done.3), custom_call_target="tpu_custom_call" | custom-call | tf_op jit(solution)/shard_map/pallas_call | solution.py:102
  37.5 2.7 %collective-permute-start.13 = (f32[14,16,128]{2,1,0:T(8,128)S(1)}, f32[14,16,128]{2,1,0:T(8,128)S(1)}, u32[]{:S(2)}, u32[]{:S(2)}) collective-permute-start(f32[14,16,128]{2,1,0:T(8,128)S(1)} %get-tuple-element.84), channel_id=1, source_target_pairs={{32,0},{64,32},{96,64},{0,96},{33,1},{65,33},{97,65},{1,97},{34,2}... | collective-permute-start | bytes 344072 | tf_op jit(solution)/shard_map/ppermute | solution.py:813
  40.1 3.5 %collective-permute-done.12 = f32[14,16,128]{2,1,0:T(8,128)S(1)} collective-permute-done((f32[14,16,128]{2,1,0:T(8,128)S(1)}, f32[14,16,128]{2,1,0:T(8,128)S(1)}, u32[]{:S(2)}, u32[]{:S(2)}) %collective-permute-start.12) | collective-permute-done | bytes 114720 | tf_op jit(solution)/shard_map/ppermute | solution.py:813
  47.1 2.9 %collective-permute-done.17.refs_4_ = f32[64,512]{1,0:T(8,128)S(1)} collective-permute-done((f32[64,512]{1,0:T(8,128)S(1)}, f32[64,512]{1,0:T(8,128)S(1)}, u32[]{:S(2)}, u32[]{:S(2)}) %collective-permute-start.17) | collective-permute-done | bytes 131104 | tf_op jit(solution)/shard_map/ppermute | solution.py:813
  50.0 3.2 %collective-permute-done.15.refs_2_ = f32[44,16,128]{2,1,0:T(8,128)S(1)} collective-permute-done((f32[44,16,128]{2,1,0:T(8,128)S(1)}, f32[44,16,128]{2,1,0:T(8,128)S(1)}, u32[]{:S(2)}, u32[]{:S(2)}) %collective-permute-start.15) | collective-permute-done | bytes 360480 | tf_op jit(solution)/shard_map/ppermute | solution.py:813
  58.9 3.4 %collective-permute-done.18.refs_1_ = f32[11,2,24,128]{3,2,1,0:T(8,128)S(1)} collective-permute-done((f32[11,2,24,128]{3,2,1,0:T(8,128)S(1)}, f32[11,2,24,128]{3,2,1,0:T(8,128)S(1)}, u32[]{:S(2)}, u32[]{:S(2)}) %collective-permute-start.18) | collective-permute-done | bytes 270368 | tf_op jit(solution)/shard_map/ppermute | solution.py:813
  62.3 2.8 %collective-permute-done.19.refs_2_ = f32[11,2,24,128]{3,2,1,0:T(8,128)S(1)} collective-permute-done((f32[11,2,24,128]{3,2,1,0:T(8,128)S(1)}, f32[11,2,24,128]{3,2,1,0:T(8,128)S(1)}, u32[]{:S(2)}, u32[]{:S(2)}) %collective-permute-start.19) | collective-permute-done | bytes 270368 | tf_op jit(solution)/shard_map/ppermute | solution.py:813
  65.1 4.5 %shard_map.81 = f32[512,128]{1,0:T(8,128)} custom-call(f32[44,2,24,128]{3,2,1,0:T(8,128)S(1)} %get-tuple-element.58.refs_0_, f32[11,2,24,128]{3,2,1,0:T(8,128)S(1)} %collective-permute-done.18.refs_1_, f32[11,2,24,128]{3,2,1,0:T(8,128)S(1)} %collective-permute-done.19.refs_2_, bf16[4,384,256]{2,1,0:T(8,128)(2,1)S(1)} %copy-done), custom_call_target="tpu_custom_call" | custom-call | tf_op jit(solution)/shard_map/pallas_call | solution.py:102
  69.5 6.6 %all-to-all-start = ((f32[128,4,128]{2,1,0:T(4,128)}), f32[128,4,128]{2,1,0:T(4,128)S(1)}, u32[]{:S(2)}, u32[]{:S(2)}) async-start(f32[128,4,128]{2,1,0:T(4,128)} %bitcast), calls=%async_computation | async-start | bytes 524288 | tf_op jit(solution)/shard_map/all_to_all | solution.py:883
  76.2 6.3 %shard_map.82.refs_5_.refs_4_.refs_6_ = f32[60,44,2,24,128]{4,3,2,1,0:T(8,128)} custom-call(f32[44,2,24,128]{3,2,1,0:T(8,128)S(1)} %get-tuple-element.58.refs_0_, f32[11,2,24,128]{3,2,1,0:T(8,128)S(1)} %collective-permute-done.18.refs_1_, f32[11,2,24,128]{3,2,1,0:T(8,128)S(1)} %collective-permute-done.19.refs_2_, bf16[4,384,256]{2,1,0:T(8,128)(2,1)S(1)} %copy-done), custom_call_target="tpu_custom_call" | custom-call | tf_op jit(solution)/shard_map/pallas_call | solution.py:102
  82.5 4.5 %all-to-all-done = f32[128,4,128]{2,1,0:T(4,128)S(1)} async-done(((f32[128,4,128]{2,1,0:T(4,128)}), f32[128,4,128]{2,1,0:T(4,128)S(1)}, u32[]{:S(2)}, u32[]{:S(2)}) %all-to-all-start) | async-done | bytes 262176 | tf_op jit(solution)/shard_map/all_to_all | solution.py:883
  87.0 10.6 %shard_map.83 = (f32[16,16,128]{2,1,0:T(8,128)S(1)}, f32[8,8,128]{2,1,0:T(8,128)S(1)}, f32[48,2,24,128]{3,2,1,0:T(8,128)S(1)}, f32[8,16,128]{2,1,0:T(8,128)S(1)}, f32[8,128]{1,0:T(8,128)S(1)}) custom-call(f32[512,128]{1,0:T(8,128)S(1)} %bitcast.10, s32[3]{0:T(128)S(1)} %pad_add_fusion.refs_1_, f32[64,512]{1,0:T(8,128)S(1)} %concatenate.23.refs_2_, ...), custom_call_target="tpu_custom_call" | custom-call | tf_op jit(solution)/shard_map/pallas_call | solution.py:102
  103.6 3.1 %collective-permute-done.23.refs_2_ = f32[24,16,128]{2,1,0:T(8,128)S(1)} collective-permute-done((f32[24,16,128]{2,1,0:T(8,128)S(1)}, f32[24,16,128]{2,1,0:T(8,128)S(1)}, u32[]{:S(2)}, u32[]{:S(2)}) %collective-permute-start.23) | collective-permute-done | bytes 196640 | tf_op jit(solution)/shard_map/ppermute | solution.py:813
  109.4 3.5 %collective-permute-start.24 = (f32[6,2,24,128]{3,2,1,0:T(8,128)S(1)}, f32[6,2,24,128]{3,2,1,0:T(8,128)S(1)}, u32[]{:S(2)}, u32[]{:S(2)}) collective-permute-start(f32[6,2,24,128]{3,2,1,0:T(8,128)S(1)} %get-tuple-element.66), channel_id=1, source_target_pairs={{0,1},{1,2},{2,3},{3,4},{4,5},{5,6},{6,7},{7,0},{8,9},{9,10},{10,1... | collective-permute-start | bytes 442376 | tf_op jit(solution)/shard_map/ppermute | solution.py:813
  115.0 2.8 %collective-permute-done.25.refs_2_ = f32[6,2,24,128]{3,2,1,0:T(8,128)S(1)} collective-permute-done((f32[6,2,24,128]{3,2,1,0:T(8,128)S(1)}, f32[6,2,24,128]{3,2,1,0:T(8,128)S(1)}, u32[]{:S(2)}, u32[]{:S(2)}) %collective-permute-start.25) | collective-permute-done | bytes 147488 | tf_op jit(solution)/shard_map/ppermute | solution.py:813
  117.8 5.0 %shard_map.85 = (f32[44,2,24,128]{3,2,1,0:T(8,128)S(1)}, f32[44,24,128]{2,1,0:T(8,128)S(1)}, f32[20,24,128]{2,1,0:T(8,128)S(1)}, f32[20,24,128]{2,1,0:T(8,128)S(1)}, f32[256,128]{1,0:T(8,128)S(1)}) custom-call(f32[24,2,24,128]{3,2,1,0:T(8,128)S(1)} %get-tuple-element.65.refs_0_, f32[6,2,24,128]{3,2,1,0:T(8,128)S(1)} %collective-permute-done.24.refs_1_, ...), custom_call_target="tpu_custom_call" | custom-call | tf_op jit(solution)/shard_map/pallas_call | solution.py:102
  122.8 16.8 %all_to_all.31 = f32[128,2,128]{2,1,0:T(2,128)S(1)} all-to-all(f32[128,2,128]{2,1,0:T(2,128)S(1)} %bitcast.12), channel_id=1, replica_groups=mesh['gx'=4,'gy'=4,'gz'=8] {'gx','gy','gz'}, dimensions={0} | all-to-all | bytes 262144 | tf_op jit(solution)/shard_map/all_to_all | solution.py:917
  139.6 9.1 %shard_map.86 = (f32[128,128]{1,0:T(8,128)}, f32[48,2,24,128]{3,2,1,0:T(8,128)S(1)}, f32[48,2,24,128]{3,2,1,0:T(8,128)S(1)}) custom-call(f32[256,128]{1,0:T(8,128)S(1)} %bitcast.11, s32[3]{0:T(128)S(1)} %pad_add_fusion.refs_1_, f32[64,512]{1,0:T(8,128)S(1)} %concatenate.23.refs_2_, f32[64,512]{1,0:T(8,128)S(1)} %collective-permute-done.16.refs_3_, ...), custom_call_target="tpu_custom_call" | custom-call | tf_op jit(solution)/shard_map/pallas_call | solution.py:102
  148.7 4.4 %all-to-all-start.2 = ((f32[128,1,128]{2,1,0:T(1,128)}), f32[128,1,128]{2,1,0:T(1,128)S(1)}, u32[]{:S(2)}, u32[]{:S(2)}) async-start(f32[128,1,128]{2,1,0:T(1,128)} %bitcast.8), calls=%async_computation.2 | async-start | bytes 131072 | tf_op jit(solution)/shard_map/all_to_all | solution.py:924
  155.2 7.4 %all-to-all-done.2 = f32[128,1,128]{2,1,0:T(1,128)S(1)} async-done(((f32[128,1,128]{2,1,0:T(1,128)}), f32[128,1,128]{2,1,0:T(1,128)S(1)}, u32[]{:S(2)}, u32[]{:S(2)}) %all-to-all-start.2) | async-done | bytes 65568 | tf_op jit(solution)/shard_map/all_to_all | solution.py:924
  (77 shorter events, 41.4 us)
Async XLA Ops:
  1.9 9.5 %collective-permute-start = (f32[16,32,128]{2,1,0:T(8,128)S(1)}, f32[16,32,128]{2,1,0:T(8,128)S(1)}, u32[]{:S(2)}, u32[]{:S(2)}) collective-permute-start(f32[16,32,128]{2,1,0:T(8,128)S(1)} %pad_maximum_fusion), channel_id=1, source_target_pairs={{0,32},{32,64},{64,96},{96,0},{1,33},{33,65},{65,97},{97,1},{2,34}... | collective-permute-start | bytes 786440 | tf_op jit(solution)/shard_map/ppermute | solution.py:813
  4.1 7.3 %collective-permute-start.1 = (f32[16,32,128]{2,1,0:T(8,128)S(1)}, f32[16,32,128]{2,1,0:T(8,128)S(1)}, u32[]{:S(2)}, u32[]{:S(2)}) collective-permute-start(f32[16,32,128]{2,1,0:T(8,128)S(1)} %pad_maximum_fusion.1), channel_id=1, source_target_pairs={{32,0},{64,32},{96,64},{0,96},{33,1},{65,33},{97,65},{1,97},{34,2}... | collective-permute-start | bytes 786440 | tf_op jit(solution)/shard_map/ppermute | solution.py:813
  5.7 5.9 %collective-permute-start.4 = (f32[4,512]{1,0:T(4,128)S(1)}, f32[4,512]{1,0:T(4,128)S(1)}, u32[]{:S(2)}, u32[]{:S(2)}) collective-permute-start(f32[4,512]{1,0:T(4,128)S(1)} %copy-done.7), channel_id=1, source_target_pairs={{0,24},{8,0},{16,8},{24,16},{1,25},{9,1},{17,9},{25,17},{2,26},{10... | collective-permute-start | bytes 24584 | tf_op jit(solution)/shard_map/ppermute | solution.py:819
  12.4 9.3 %collective-permute-start.5 = (f32[80,8,128]{2,1,0:T(8,128)S(1)}, f32[80,8,128]{2,1,0:T(8,128)S(1)}, u32[]{:S(2)}, u32[]{:S(2)}) collective-permute-start(f32[80,8,128]{2,1,0:T(8,128)S(1)} %get-tuple-element.43), channel_id=1, source_target_pairs={{0,8},{8,16},{16,24},{24,0},{1,9},{9,17},{17,25},{25,1},{2,10},{10... | collective-permute-start | bytes 983048 | tf_op jit(solution)/shard_map/ppermute | solution.py:813
  12.7 9.0 %collective-permute-start.6 = (f32[80,8,128]{2,1,0:T(8,128)S(1)}, f32[80,8,128]{2,1,0:T(8,128)S(1)}, u32[]{:S(2)}, u32[]{:S(2)}) collective-permute-start(f32[80,8,128]{2,1,0:T(8,128)S(1)} %get-tuple-element.44), channel_id=1, source_target_pairs={{8,0},{16,8},{24,16},{0,24},{9,1},{17,9},{25,17},{1,25},{10,2},{18... | collective-permute-start | bytes 983048 | tf_op jit(solution)/shard_map/ppermute | solution.py:813
  16.9 4.4 %collective-permute-start.8 = (f32[16,512]{1,0:T(8,128)S(1)}, f32[16,512]{1,0:T(8,128)S(1)}, u32[]{:S(2)}, u32[]{:S(2)}) collective-permute-start(f32[16,512]{1,0:T(8,128)S(1)} %pad_maximum_fusion.2), channel_id=1, source_target_pairs={{0,64},{32,96},{64,0},{96,32},{1,65},{33,97},{65,1},{97,33},{2,66}... | collective-permute-start | bytes 98312 | tf_op jit(solution)/shard_map/ppermute | solution.py:819
  17.1 4.6 %collective-permute-start.7 = (f32[16,512]{1,0:T(8,128)S(1)}, f32[16,512]{1,0:T(8,128)S(1)}, u32[]{:S(2)}, u32[]{:S(2)}) collective-permute-start(f32[16,512]{1,0:T(8,128)S(1)} %pad_maximum_fusion.2), channel_id=1, source_target_pairs={{0,32},{32,64},{64,96},{96,0},{1,33},{33,65},{65,97},{97,1},{2,34}... | collective-permute-start | bytes 98312 | tf_op jit(solution)/shard_map/ppermute | solution.py:819
  22.9 8.1 %collective-permute-start.10 = (f32[6,48,128]{2,1,0:T(8,128)S(1)}, f32[6,48,128]{2,1,0:T(8,128)S(1)}, u32[]{:S(2)}, u32[]{:S(2)}) collective-permute-start(f32[6,48,128]{2,1,0:T(8,128)S(1)} %get-tuple-element.51), channel_id=1, source_target_pairs={{0,1},{1,2},{2,3},{3,4},{4,5},{5,6},{6,7},{7,0},{8,9},{9,10},{10,1... | collective-permute-start | bytes 442376 | tf_op jit(solution)/shard_map/ppermute | solution.py:813
  28.8 4.6 %collective-permute-start.11 = (f32[6,48,128]{2,1,0:T(8,128)S(1)}, f32[6,48,128]{2,1,0:T(8,128)S(1)}, u32[]{:S(2)}, u32[]{:S(2)}) collective-permute-start(f32[6,48,128]{2,1,0:T(8,128)S(1)} %get-tuple-element.52), channel_id=1, source_target_pairs={{1,0},{2,1},{3,2},{4,3},{5,4},{6,5},{7,6},{0,7},{9,8},{10,9},{11,1... | collective-permute-start | bytes 442376 | tf_op jit(solution)/shard_map/ppermute | solution.py:813
  37.4 6.3 %collective-permute-start.12 = (f32[14,16,128]{2,1,0:T(8,128)S(1)}, f32[14,16,128]{2,1,0:T(8,128)S(1)}, u32[]{:S(2)}, u32[]{:S(2)}) collective-permute-start(f32[14,16,128]{2,1,0:T(8,128)S(1)} %get-tuple-element.85), channel_id=1, source_target_pairs={{0,32},{32,64},{64,96},{96,0},{1,33},{33,65},{65,97},{97,1},{2,34}... | collective-permute-start | bytes 344072 | tf_op jit(solution)/shard_map/ppermute | solution.py:813
  37.5 6.2 %collective-permute-start.13 = (f32[14,16,128]{2,1,0:T(8,128)S(1)}, f32[14,16,128]{2,1,0:T(8,128)S(1)}, u32[]{:S(2)}, u32[]{:S(2)}) collective-permute-start(f32[14,16,128]{2,1,0:T(8,128)S(1)} %get-tuple-element.84), channel_id=1, source_target_pairs={{32,0},{64,32},{96,64},{0,96},{33,1},{65,33},{97,65},{1,97},{34,2}... | collective-permute-start | bytes 344072 | tf_op jit(solution)/shard_map/ppermute | solution.py:813
  43.7 9.5 %collective-permute-start.15 = (f32[44,16,128]{2,1,0:T(8,128)S(1)}, f32[44,16,128]{2,1,0:T(8,128)S(1)}, u32[]{:S(2)}, u32[]{:S(2)}) collective-permute-start(f32[44,16,128]{2,1,0:T(8,128)S(1)} %constant_dynamic-update-slice_fusion.refs_0_), channel_id=1, source_target_pairs={{8,0},{16,8},{24,16},{0,24},{9,1},{17,9},{25,17},{1,25},{10,2},{18... | collective-permute-start | bytes 1081352 | tf_op jit(solution)/shard_map/ppermute | solution.py:813
  44.1 10.3 %collective-permute-start.14 = (f32[44,16,128]{2,1,0:T(8,128)S(1)}, f32[44,16,128]{2,1,0:T(8,128)S(1)}, u32[]{:S(2)}, u32[]{:S(2)}) collective-permute-start(f32[44,16,128]{2,1,0:T(8,128)S(1)} %constant_dynamic-update-slice_fusion.refs_0_), channel_id=1, source_target_pairs={{0,8},{8,16},{16,24},{24,0},{1,9},{9,17},{17,25},{25,1},{2,10},{10... | collective-permute-start | bytes 1081352 | tf_op jit(solution)/shard_map/ppermute | solution.py:813
  45.3 4.7 %collective-permute-start.17 = (f32[64,512]{1,0:T(8,128)S(1)}, f32[64,512]{1,0:T(8,128)S(1)}, u32[]{:S(2)}, u32[]{:S(2)}) collective-permute-start(f32[64,512]{1,0:T(8,128)S(1)} %concatenate.23.refs_2_), channel_id=1, source_target_pairs={{1,0},{2,1},{3,2},{4,3},{5,4},{6,5},{7,6},{0,7},{9,8},{10,9},{11,1... | collective-permute-start | bytes 393224 | tf_op jit(solution)/shard_map/ppermute | solution.py:813
  56.8 5.5 %collective-permute-start.18 = (f32[11,2,24,128]{3,2,1,0:T(8,128)S(1)}, f32[11,2,24,128]{3,2,1,0:T(8,128)S(1)}, u32[]{:S(2)}, u32[]{:S(2)}) collective-permute-start(f32[11,2,24,128]{3,2,1,0:T(8,128)S(1)} %get-tuple-element.59), channel_id=1, source_target_pairs={{0,1},{1,2},{2,3},{3,4},{4,5},{5,6},{6,7},{7,0},{8,9},{9,10},{10,1... | collective-permute-start | bytes 811016 | tf_op jit(solution)/shard_map/ppermute | solution.py:813
  58.9 6.2 %collective-permute-start.19 = (f32[11,2,24,128]{3,2,1,0:T(8,128)S(1)}, f32[11,2,24,128]{3,2,1,0:T(8,128)S(1)}, u32[]{:S(2)}, u32[]{:S(2)}) collective-permute-start(f32[11,2,24,128]{3,2,1,0:T(8,128)S(1)} %get-tuple-element.60), channel_id=1, source_target_pairs={{1,0},{2,1},{3,2},{4,3},{5,4},{6,5},{7,6},{0,7},{9,8},{10,9},{11,1... | collective-permute-start | bytes 811016 | tf_op jit(solution)/shard_map/ppermute | solution.py:813
  69.5 17.5 %all-to-all-start = ((f32[128,4,128]{2,1,0:T(4,128)}), f32[128,4,128]{2,1,0:T(4,128)S(1)}, u32[]{:S(2)}, u32[]{:S(2)}) async-start(f32[128,4,128]{2,1,0:T(4,128)} %bitcast), calls=%async_computation | async-start | bytes 524288 | tf_op jit(solution)/shard_map/all_to_all | solution.py:883
  97.6 4.4 %collective-permute-start.20 = (f32[8,16,128]{2,1,0:T(8,128)S(1)}, f32[8,16,128]{2,1,0:T(8,128)S(1)}, u32[]{:S(2)}, u32[]{:S(2)}) collective-permute-start(f32[8,16,128]{2,1,0:T(8,128)S(1)} %get-tuple-element.64), channel_id=1, source_target_pairs={{0,32},{32,64},{64,96},{96,0},{1,33},{33,65},{65,97},{97,1},{2,34}... | collective-permute-start | bytes 196616 | tf_op jit(solution)/shard_map/ppermute | solution.py:813
  98.0 4.0 %collective-permute-start.21 = (f32[8,16,128]{2,1,0:T(8,128)S(1)}, f32[8,16,128]{2,1,0:T(8,128)S(1)}, u32[]{:S(2)}, u32[]{:S(2)}) collective-permute-start(f32[8,16,128]{2,1,0:T(8,128)S(1)} %get-tuple-element.64), channel_id=1, source_target_pairs={{32,0},{64,32},{96,64},{0,96},{33,1},{65,33},{97,65},{1,97},{34,2}... | collective-permute-start | bytes 196616 | tf_op jit(solution)/shard_map/ppermute | solution.py:813
  102.0 4.6 %collective-permute-start.23 = (f32[24,16,128]{2,1,0:T(8,128)S(1)}, f32[24,16,128]{2,1,0:T(8,128)S(1)}, u32[]{:S(2)}, u32[]{:S(2)}) collective-permute-start(f32[24,16,128]{2,1,0:T(8,128)S(1)} %constant_dynamic-update-slice_fusion.3.refs_0_), channel_id=1, source_target_pairs={{8,0},{16,8},{24,16},{0,24},{9,1},{17,9},{25,17},{1,25},{10,2},{18... | collective-permute-start | bytes 589832 | tf_op jit(solution)/shard_map/ppermute | solution.py:813
  103.3 5.7 %collective-permute-start.22 = (f32[24,16,128]{2,1,0:T(8,128)S(1)}, f32[24,16,128]{2,1,0:T(8,128)S(1)}, u32[]{:S(2)}, u32[]{:S(2)}) collective-permute-start(f32[24,16,128]{2,1,0:T(8,128)S(1)} %constant_dynamic-update-slice_fusion.3.refs_0_), channel_id=1, source_target_pairs={{0,8},{8,16},{16,24},{24,0},{1,9},{9,17},{17,25},{25,1},{2,10},{10... | collective-permute-start | bytes 589832 | tf_op jit(solution)/shard_map/ppermute | solution.py:813
  109.4 5.6 %collective-permute-start.24 = (f32[6,2,24,128]{3,2,1,0:T(8,128)S(1)}, f32[6,2,24,128]{3,2,1,0:T(8,128)S(1)}, u32[]{:S(2)}, u32[]{:S(2)}) collective-permute-start(f32[6,2,24,128]{3,2,1,0:T(8,128)S(1)} %get-tuple-element.66), channel_id=1, source_target_pairs={{0,1},{1,2},{2,3},{3,4},{4,5},{5,6},{6,7},{7,0},{8,9},{9,10},{10,1... | collective-permute-start | bytes 442376 | tf_op jit(solution)/shard_map/ppermute | solution.py:813
  112.9 4.9 %collective-permute-start.25 = (f32[6,2,24,128]{3,2,1,0:T(8,128)S(1)}, f32[6,2,24,128]{3,2,1,0:T(8,128)S(1)}, u32[]{:S(2)}, u32[]{:S(2)}) collective-permute-start(f32[6,2,24,128]{3,2,1,0:T(8,128)S(1)} %get-tuple-element.67), channel_id=1, source_target_pairs={{1,0},{2,1},{3,2},{4,3},{5,4},{6,5},{7,6},{0,7},{9,8},{10,9},{11,1... | collective-permute-start | bytes 442376 | tf_op jit(solution)/shard_map/ppermute | solution.py:813
  148.7 13.9 %all-to-all-start.2 = ((f32[128,1,128]{2,1,0:T(1,128)}), f32[128,1,128]{2,1,0:T(1,128)S(1)}, u32[]{:S(2)}, u32[]{:S(2)}) async-start(f32[128,1,128]{2,1,0:T(1,128)} %bitcast.8), calls=%async_computation.2 | async-start | bytes 131072 | tf_op jit(solution)/shard_map/all_to_all | solution.py:924
  (12 other events, 105.6 us)

commit v7 on v5

--- a/solution.py
+++ b/solution.py
@@ -336,7 +336,7 @@
     return total + sum0(values, plane + 1, 1, 1, True)
 
 
-def pack_z1(own, below, above, coloured, to_high, to_low, _):
+def pack_z1(own, halos, coloured, to_high, to_low, _):
     block = iota((24, LANES), 1) % 64 // 14
     for group in range(own.shape[0] // GROUP1):
         up = [jnp.zeros((24, LANES), F32)] * 2
@@ -344,7 +344,13 @@
         for k in range(GROUP1):
             item = group * GROUP1 + k
             even, odd = [
-                jnp.concatenate([ref[item, pl.ds(q, 8, stride=2), :] for ref in (below, own, above)], axis=0)
+                jnp.concatenate(
+                    [
+                        ref[at, pl.ds(q, 8, stride=2), :]
+                        for ref, at in ((halos, item), (own, item), (halos, own.shape[0] + item))
+                    ],
+                    axis=0,
+                )
                 for q in (0, 1)
             ]
             here = even_lanes((24, LANES), item)
@@ -833,7 +839,7 @@
     items = own.shape[0]
     message = (items // GROUP1, 2, 24, LANES)
     coloured, to_high, to_low = call(
-        pack_z1, [(items, 2, 24, LANES), message, message], own, below, above
+        pack_z1, [(items, 2, 24, LANES), message, message], own, jnp.concatenate([below, above])
     )
     return (coloured, *exchange(to_high, to_low, "gz")), beside
 

time: 164 us -> 162 us (0.988)
  local copies, waits for them, and re-layouts: 3.16 us -> 1.44 us
    unnamed x20 -> x16, local copies, waits for them, and re-layouts: 1.78 us -> 0.06 us
where the time goes in v7:
time: 162 us
  waiting for transfers between devices  52.1 us (32%)
  starting transfers between devices  45.3 us (28%)
  Pallas kernels  44.6 us (28%)
  blocking collectives  16.8 us (10%)
    pallas_call x11, Pallas kernels, call(): pl.pallas_call(kernel, out_shape=[jax.ShapeDtypeStruct(shape, F32) for sh...  44.6 us
    ppermute x20, waiting for transfers between devices, exchange(): return (lax.ppermute(to_high, axis, up), lax.ppermute(to_low, axis, down))  35.8 us
    ppermute x20, starting transfers between devices, exchange(): return (lax.ppermute(to_high, axis, up), lax.ppermute(to_low, axis, down))  28.2 us
    all_to_all x1, blocking collectives, local(): message = lax.all_to_all(message, AXES, 0, 0, tiled=True)  16.8 us
    all_to_all x1, waiting for transfers between devices, local(): sums = lax.all_to_all(sums, AXES, 0, 0, tiled=True)  6.86 us
    all_to_all x1, starting transfers between devices, local(): message = lax.all_to_all(message, AXES, 0, 0, tiled=True)  6.57 us
    ppermute x6, starting transfers between devices, from_all(): return [lax.ppermute(own, axis, shift) for shift in shifts]  6.12 us
    ppermute x6, waiting for transfers between devices, from_all(): return [lax.ppermute(own, axis, shift) for shift in shifts]  4.97 us
  transfers between devices with their start and end apart: 28, of which 21 were waited for; matrix products, arithmetic and copies ran while one was open for 0% of the time, Pallas kernels for 6%

profile of v7, /device:TPU:1, one launch (start us, length us, event | category | flops | bytes accessed | tf_op | source)
XLA Modules:
  0.0 162.1 jit_solution(11000242764140395906)
XLA Ops:
  5.7 2.5 %collective-permute-start.4 = (f32[4,512]{1,0:T(4,128)S(1)}, f32[4,512]{1,0:T(4,128)S(1)}, u32[]{:S(2)}, u32[]{:S(2)}) collective-permute-start(f32[4,512]{1,0:T(4,128)S(1)} %copy-done.5), channel_id=1, source_target_pairs={{0,24},{8,0},{16,8},{24,16},{1,25},{9,1},{17,9},{25,17},{2,26},{10... | collective-permute-start | bytes 24584 | tf_op jit(solution)/shard_map/ppermute | solution.py:825
  17.9 3.3 %collective-permute-done.8 = f32[16,512]{1,0:T(8,128)S(1)} collective-permute-done((f32[16,512]{1,0:T(8,128)S(1)}, f32[16,512]{1,0:T(8,128)S(1)}, u32[]{:S(2)}, u32[]{:S(2)}) %collective-permute-start.8) | collective-permute-done | bytes 32800 | tf_op jit(solution)/shard_map/ppermute | solution.py:825
  22.9 6.0 %collective-permute-start.10 = (f32[6,48,128]{2,1,0:T(8,128)S(1)}, f32[6,48,128]{2,1,0:T(8,128)S(1)}, u32[]{:S(2)}, u32[]{:S(2)}) collective-permute-start(f32[6,48,128]{2,1,0:T(8,128)S(1)} %get-tuple-element.51), channel_id=1, source_target_pairs={{0,1},{1,2},{2,3},{3,4},{4,5},{5,6},{6,7},{7,0},{8,9},{9,10},{10,1... | collective-permute-start | bytes 442376 | tf_op jit(solution)/shard_map/ppermute | solution.py:819
  33.4 3.9 %shard_map.79 = (f32[16,16,128]{2,1,0:T(8,128)S(1)}, f32[56,48,2,24,128]{4,3,2,1,0:T(8,128)}) custom-call(f32[96,48,128]{2,1,0:T(8,128)S(1)} %get-tuple-element.50.refs_0_, f32[6,48,128]{2,1,0:T(8,128)S(1)} %collective-permute-done.10.refs_1_, f32[6,48,128]{2,1,0:T(8,128)S(1)} %collective-permute-done.11.refs_2_, bf16[8,256,256]{2,1,0:T(8,128)(2,1)S(1)} %copy-done.3), custom_call_target="tpu_custom_call" | custom-call | tf_op jit(solution)/shard_map/pallas_call | solution.py:102
  37.5 2.7 %collective-permute-start.13 = (f32[14,16,128]{2,1,0:T(8,128)S(1)}, f32[14,16,128]{2,1,0:T(8,128)S(1)}, u32[]{:S(2)}, u32[]{:S(2)}) collective-permute-start(f32[14,16,128]{2,1,0:T(8,128)S(1)} %get-tuple-element.84), channel_id=1, source_target_pairs={{32,0},{64,32},{96,64},{0,96},{33,1},{65,33},{97,65},{1,97},{34,2}... | collective-permute-start | bytes 344072 | tf_op jit(solution)/shard_map/ppermute | solution.py:819
  40.1 3.5 %collective-permute-done.12 = f32[14,16,128]{2,1,0:T(8,128)S(1)} collective-permute-done((f32[14,16,128]{2,1,0:T(8,128)S(1)}, f32[14,16,128]{2,1,0:T(8,128)S(1)}, u32[]{:S(2)}, u32[]{:S(2)}) %collective-permute-start.12) | collective-permute-done | bytes 114720 | tf_op jit(solution)/shard_map/ppermute | solution.py:819
  47.1 2.9 %collective-permute-done.17.refs_4_ = f32[64,512]{1,0:T(8,128)S(1)} collective-permute-done((f32[64,512]{1,0:T(8,128)S(1)}, f32[64,512]{1,0:T(8,128)S(1)}, u32[]{:S(2)}, u32[]{:S(2)}) %collective-permute-start.17) | collective-permute-done | bytes 131104 | tf_op jit(solution)/shard_map/ppermute | solution.py:819
  50.0 3.2 %collective-permute-done.15 = f32[44,16,128]{2,1,0:T(8,128)S(1)} collective-permute-done((f32[44,16,128]{2,1,0:T(8,128)S(1)}, f32[44,16,128]{2,1,0:T(8,128)S(1)}, u32[]{:S(2)}, u32[]{:S(2)}) %collective-permute-start.15) | collective-permute-done | bytes 360480 | tf_op jit(solution)/shard_map/ppermute | solution.py:819
  57.2 3.4 %collective-permute-done.18.refs_1_ = f32[11,2,24,128]{3,2,1,0:T(8,128)S(1)} collective-permute-done((f32[11,2,24,128]{3,2,1,0:T(8,128)S(1)}, f32[11,2,24,128]{3,2,1,0:T(8,128)S(1)}, u32[]{:S(2)}, u32[]{:S(2)}) %collective-permute-start.18) | collective-permute-done | bytes 270368 | tf_op jit(solution)/shard_map/ppermute | solution.py:819
  60.6 2.8 %collective-permute-done.19.refs_2_ = f32[11,2,24,128]{3,2,1,0:T(8,128)S(1)} collective-permute-done((f32[11,2,24,128]{3,2,1,0:T(8,128)S(1)}, f32[11,2,24,128]{3,2,1,0:T(8,128)S(1)}, u32[]{:S(2)}, u32[]{:S(2)}) %collective-permute-start.19) | collective-permute-done | bytes 270368 | tf_op jit(solution)/shard_map/ppermute | solution.py:819
  63.4 4.5 %shard_map.81 = f32[512,128]{1,0:T(8,128)} custom-call(f32[44,2,24,128]{3,2,1,0:T(8,128)S(1)} %get-tuple-element.58.refs_0_, f32[11,2,24,128]{3,2,1,0:T(8,128)S(1)} %collective-permute-done.18.refs_1_, f32[11,2,24,128]{3,2,1,0:T(8,128)S(1)} %collective-permute-done.19.refs_2_, bf16[4,384,256]{2,1,0:T(8,128)(2,1)S(1)} %copy-done), custom_call_target="tpu_custom_call" | custom-call | tf_op jit(solution)/shard_map/pallas_call | solution.py:102
  67.8 6.6 %all-to-all-start = ((f32[128,4,128]{2,1,0:T(4,128)}), f32[128,4,128]{2,1,0:T(4,128)S(1)}, u32[]{:S(2)}, u32[]{:S(2)}) async-start(f32[128,4,128]{2,1,0:T(4,128)} %bitcast), calls=%async_computation | async-start | bytes 524288 | tf_op jit(solution)/shard_map/all_to_all | solution.py:889
  74.5 6.3 %shard_map.82.refs_5_.refs_4_.refs_6_ = f32[60,44,2,24,128]{4,3,2,1,0:T(8,128)} custom-call(f32[44,2,24,128]{3,2,1,0:T(8,128)S(1)} %get-tuple-element.58.refs_0_, f32[11,2,24,128]{3,2,1,0:T(8,128)S(1)} %collective-permute-done.18.refs_1_, f32[11,2,24,128]{3,2,1,0:T(8,128)S(1)} %collective-permute-done.19.refs_2_, bf16[4,384,256]{2,1,0:T(8,128)(2,1)S(1)} %copy-done), custom_call_target="tpu_custom_call" | custom-call | tf_op jit(solution)/shard_map/pallas_call | solution.py:102
  80.8 4.5 %all-to-all-done = f32[128,4,128]{2,1,0:T(4,128)S(1)} async-done(((f32[128,4,128]{2,1,0:T(4,128)}), f32[128,4,128]{2,1,0:T(4,128)S(1)}, u32[]{:S(2)}, u32[]{:S(2)}) %all-to-all-start) | async-done | bytes 262176 | tf_op jit(solution)/shard_map/all_to_all | solution.py:889
  85.3 10.9 %shard_map.83 = (f32[16,16,128]{2,1,0:T(8,128)S(1)}, f32[8,8,128]{2,1,0:T(8,128)S(1)}, f32[48,2,24,128]{3,2,1,0:T(8,128)S(1)}, f32[8,16,128]{2,1,0:T(8,128)S(1)}, f32[8,128]{1,0:T(8,128)S(1)}) custom-call(f32[512,128]{1,0:T(8,128)S(1)} %bitcast.10, s32[3]{0:T(128)S(1)} %pad_add_fusion.refs_1_, f32[64,512]{1,0:T(8,128)S(1)} %concatenate.29.refs_2_, ...), custom_call_target="tpu_custom_call" | custom-call | tf_op jit(solution)/shard_map/pallas_call | solution.py:102
  102.2 3.1 %collective-permute-done.23 = f32[24,16,128]{2,1,0:T(8,128)S(1)} collective-permute-done((f32[24,16,128]{2,1,0:T(8,128)S(1)}, f32[24,16,128]{2,1,0:T(8,128)S(1)}, u32[]{:S(2)}, u32[]{:S(2)}) %collective-permute-start.23) | collective-permute-done | bytes 196640 | tf_op jit(solution)/shard_map/ppermute | solution.py:819
  108.0 3.5 %collective-permute-start.24 = (f32[6,2,24,128]{3,2,1,0:T(8,128)S(1)}, f32[6,2,24,128]{3,2,1,0:T(8,128)S(1)}, u32[]{:S(2)}, u32[]{:S(2)}) collective-permute-start(f32[6,2,24,128]{3,2,1,0:T(8,128)S(1)} %get-tuple-element.66), channel_id=1, source_target_pairs={{0,1},{1,2},{2,3},{3,4},{4,5},{5,6},{6,7},{7,0},{8,9},{9,10},{10,1... | collective-permute-start | bytes 442376 | tf_op jit(solution)/shard_map/ppermute | solution.py:819
  113.6 2.8 %collective-permute-done.25.refs_2_ = f32[6,2,24,128]{3,2,1,0:T(8,128)S(1)} collective-permute-done((f32[6,2,24,128]{3,2,1,0:T(8,128)S(1)}, f32[6,2,24,128]{3,2,1,0:T(8,128)S(1)}, u32[]{:S(2)}, u32[]{:S(2)}) %collective-permute-start.25) | collective-permute-done | bytes 147488 | tf_op jit(solution)/shard_map/ppermute | solution.py:819
  116.4 5.0 %shard_map.85 = (f32[44,2,24,128]{3,2,1,0:T(8,128)S(1)}, f32[44,24,128]{2,1,0:T(8,128)S(1)}, f32[20,24,128]{2,1,0:T(8,128)S(1)}, f32[20,24,128]{2,1,0:T(8,128)S(1)}, f32[256,128]{1,0:T(8,128)S(1)}) custom-call(f32[24,2,24,128]{3,2,1,0:T(8,128)S(1)} %get-tuple-element.65.refs_0_, f32[6,2,24,128]{3,2,1,0:T(8,128)S(1)} %collective-permute-done.24.refs_1_, ...), custom_call_target="tpu_custom_call" | custom-call | tf_op jit(solution)/shard_map/pallas_call | solution.py:102
  121.4 16.8 %all_to_all.31 = f32[128,2,128]{2,1,0:T(2,128)S(1)} all-to-all(f32[128,2,128]{2,1,0:T(2,128)S(1)} %bitcast.12), channel_id=1, replica_groups=mesh['gx'=4,'gy'=4,'gz'=8] {'gx','gy','gz'}, dimensions={0} | all-to-all | bytes 262144 | tf_op jit(solution)/shard_map/all_to_all | solution.py:923
  138.2 9.1 %shard_map.86 = (f32[128,128]{1,0:T(8,128)}, f32[48,2,24,128]{3,2,1,0:T(8,128)S(1)}, f32[48,2,24,128]{3,2,1,0:T(8,128)S(1)}) custom-call(f32[256,128]{1,0:T(8,128)S(1)} %bitcast.11, s32[3]{0:T(128)S(1)} %pad_add_fusion.refs_1_, f32[64,512]{1,0:T(8,128)S(1)} %concatenate.29.refs_2_, f32[64,512]{1,0:T(8,128)S(1)} %collective-permute-done.16.refs_3_, ...), custom_call_target="tpu_custom_call" | custom-call | tf_op jit(solution)/shard_map/pallas_call | solution.py:102
  147.3 4.4 %all-to-all-start.2 = ((f32[128,1,128]{2,1,0:T(1,128)}), f32[128,1,128]{2,1,0:T(1,128)S(1)}, u32[]{:S(2)}, u32[]{:S(2)}) async-start(f32[128,1,128]{2,1,0:T(1,128)} %bitcast.8), calls=%async_computation.2 | async-start | bytes 131072 | tf_op jit(solution)/shard_map/all_to_all | solution.py:930
  151.7 2.7 %shard_map.87 = f32[32,32,128]{2,1,0:T(8,128)} custom-call(f32[48,2,24,128]{3,2,1,0:T(8,128)S(1)} %get-tuple-element.77.refs_0_, f32[48,2,24,128]{3,2,1,0:T(8,128)S(1)} %get-tuple-element.78.refs_1_, bf16[256,128]{1,0:T(8,128)(2,1)S(1)} %copy-done.4), custom_call_target="tpu_custom_call" | custom-call | tf_op jit(solution)/shard_map/pallas_call | solution.py:102
  154.4 6.9 %all-to-all-done.2 = f32[128,1,128]{2,1,0:T(1,128)S(1)} async-done(((f32[128,1,128]{2,1,0:T(1,128)}), f32[128,1,128]{2,1,0:T(1,128)S(1)}, u32[]{:S(2)}, u32[]{:S(2)}) %all-to-all-start.2) | async-done | bytes 65568 | tf_op jit(solution)/shard_map/all_to_all | solution.py:930
  (75 shorter events, 40.2 us)
Async XLA Ops:
  1.9 9.5 %collective-permute-start = (f32[16,32,128]{2,1,0:T(8,128)S(1)}, f32[16,32,128]{2,1,0:T(8,128)S(1)}, u32[]{:S(2)}, u32[]{:S(2)}) collective-permute-start(f32[16,32,128]{2,1,0:T(8,128)S(1)} %pad_maximum_fusion.2), channel_id=1, source_target_pairs={{0,32},{32,64},{64,96},{96,0},{1,33},{33,65},{65,97},{97,1},{2,34}... | collective-permute-start | bytes 786440 | tf_op jit(solution)/shard_map/ppermute | solution.py:819
  4.1 7.3 %collective-permute-start.1 = (f32[16,32,128]{2,1,0:T(8,128)S(1)}, f32[16,32,128]{2,1,0:T(8,128)S(1)}, u32[]{:S(2)}, u32[]{:S(2)}) collective-permute-start(f32[16,32,128]{2,1,0:T(8,128)S(1)} %pad_maximum_fusion.3), channel_id=1, source_target_pairs={{32,0},{64,32},{96,64},{0,96},{33,1},{65,33},{97,65},{1,97},{34,2}... | collective-permute-start | bytes 786440 | tf_op jit(solution)/shard_map/ppermute | solution.py:819
  5.7 5.9 %collective-permute-start.4 = (f32[4,512]{1,0:T(4,128)S(1)}, f32[4,512]{1,0:T(4,128)S(1)}, u32[]{:S(2)}, u32[]{:S(2)}) collective-permute-start(f32[4,512]{1,0:T(4,128)S(1)} %copy-done.5), channel_id=1, source_target_pairs={{0,24},{8,0},{16,8},{24,16},{1,25},{9,1},{17,9},{25,17},{2,26},{10... | collective-permute-start | bytes 24584 | tf_op jit(solution)/shard_map/ppermute | solution.py:825
  12.4 9.3 %collective-permute-start.5 = (f32[80,8,128]{2,1,0:T(8,128)S(1)}, f32[80,8,128]{2,1,0:T(8,128)S(1)}, u32[]{:S(2)}, u32[]{:S(2)}) collective-permute-start(f32[80,8,128]{2,1,0:T(8,128)S(1)} %get-tuple-element.43), channel_id=1, source_target_pairs={{0,8},{8,16},{16,24},{24,0},{1,9},{9,17},{17,25},{25,1},{2,10},{10... | collective-permute-start | bytes 983048 | tf_op jit(solution)/shard_map/ppermute | solution.py:819
  12.7 9.0 %collective-permute-start.6 = (f32[80,8,128]{2,1,0:T(8,128)S(1)}, f32[80,8,128]{2,1,0:T(8,128)S(1)}, u32[]{:S(2)}, u32[]{:S(2)}) collective-permute-start(f32[80,8,128]{2,1,0:T(8,128)S(1)} %get-tuple-element.44), channel_id=1, source_target_pairs={{8,0},{16,8},{24,16},{0,24},{9,1},{17,9},{25,17},{1,25},{10,2},{18... | collective-permute-start | bytes 983048 | tf_op jit(solution)/shard_map/ppermute | solution.py:819
  16.9 4.4 %collective-permute-start.8 = (f32[16,512]{1,0:T(8,128)S(1)}, f32[16,512]{1,0:T(8,128)S(1)}, u32[]{:S(2)}, u32[]{:S(2)}) collective-permute-start(f32[16,512]{1,0:T(8,128)S(1)} %pad_maximum_fusion.4), channel_id=1, source_target_pairs={{0,64},{32,96},{64,0},{96,32},{1,65},{33,97},{65,1},{97,33},{2,66}... | collective-permute-start | bytes 98312 | tf_op jit(solution)/shard_map/ppermute | solution.py:825
  17.1 4.6 %collective-permute-start.7 = (f32[16,512]{1,0:T(8,128)S(1)}, f32[16,512]{1,0:T(8,128)S(1)}, u32[]{:S(2)}, u32[]{:S(2)}) collective-permute-start(f32[16,512]{1,0:T(8,128)S(1)} %pad_maximum_fusion.4), channel_id=1, source_target_pairs={{0,32},{32,64},{64,96},{96,0},{1,33},{33,65},{65,97},{97,1},{2,34}... | collective-permute-start | bytes 98312 | tf_op jit(solution)/shard_map/ppermute | solution.py:825
  22.9 8.1 %collective-permute-start.10 = (f32[6,48,128]{2,1,0:T(8,128)S(1)}, f32[6,48,128]{2,1,0:T(8,128)S(1)}, u32[]{:S(2)}, u32[]{:S(2)}) collective-permute-start(f32[6,48,128]{2,1,0:T(8,128)S(1)} %get-tuple-element.51), channel_id=1, source_target_pairs={{0,1},{1,2},{2,3},{3,4},{4,5},{5,6},{6,7},{7,0},{8,9},{9,10},{10,1... | collective-permute-start | bytes 442376 | tf_op jit(solution)/shard_map/ppermute | solution.py:819
  28.8 4.6 %collective-permute-start.11 = (f32[6,48,128]{2,1,0:T(8,128)S(1)}, f32[6,48,128]{2,1,0:T(8,128)S(1)}, u32[]{:S(2)}, u32[]{:S(2)}) collective-permute-start(f32[6,48,128]{2,1,0:T(8,128)S(1)} %get-tuple-element.52), channel_id=1, source_target_pairs={{1,0},{2,1},{3,2},{4,3},{5,4},{6,5},{7,6},{0,7},{9,8},{10,9},{11,1... | collective-permute-start | bytes 442376 | tf_op jit(solution)/shard_map/ppermute | solution.py:819
  37.4 6.3 %collective-permute-start.12 = (f32[14,16,128]{2,1,0:T(8,128)S(1)}, f32[14,16,128]{2,1,0:T(8,128)S(1)}, u32[]{:S(2)}, u32[]{:S(2)}) collective-permute-start(f32[14,16,128]{2,1,0:T(8,128)S(1)} %get-tuple-element.85), channel_id=1, source_target_pairs={{0,32},{32,64},{64,96},{96,0},{1,33},{33,65},{65,97},{97,1},{2,34}... | collective-permute-start | bytes 344072 | tf_op jit(solution)/shard_map/ppermute | solution.py:819
  37.5 6.2 %collective-permute-start.13 = (f32[14,16,128]{2,1,0:T(8,128)S(1)}, f32[14,16,128]{2,1,0:T(8,128)S(1)}, u32[]{:S(2)}, u32[]{:S(2)}) collective-permute-start(f32[14,16,128]{2,1,0:T(8,128)S(1)} %get-tuple-element.84), channel_id=1, source_target_pairs={{32,0},{64,32},{96,64},{0,96},{33,1},{65,33},{97,65},{1,97},{34,2}... | collective-permute-start | bytes 344072 | tf_op jit(solution)/shard_map/ppermute | solution.py:819
  43.7 9.5 %collective-permute-start.15 = (f32[44,16,128]{2,1,0:T(8,128)S(1)}, f32[44,16,128]{2,1,0:T(8,128)S(1)}, u32[]{:S(2)}, u32[]{:S(2)}) collective-permute-start(f32[44,16,128]{2,1,0:T(8,128)S(1)} %constant_dynamic-update-slice_fusion.refs_0_), channel_id=1, source_target_pairs={{8,0},{16,8},{24,16},{0,24},{9,1},{17,9},{25,17},{1,25},{10,2},{18... | collective-permute-start | bytes 1081352 | tf_op jit(solution)/shard_map/ppermute | solution.py:819
  44.1 10.3 %collective-permute-start.14 = (f32[44,16,128]{2,1,0:T(8,128)S(1)}, f32[44,16,128]{2,1,0:T(8,128)S(1)}, u32[]{:S(2)}, u32[]{:S(2)}) collective-permute-start(f32[44,16,128]{2,1,0:T(8,128)S(1)} %constant_dynamic-update-slice_fusion.refs_0_), channel_id=1, source_target_pairs={{0,8},{8,16},{16,24},{24,0},{1,9},{9,17},{17,25},{25,1},{2,10},{10... | collective-permute-start | bytes 1081352 | tf_op jit(solution)/shard_map/ppermute | solution.py:819
  45.3 4.7 %collective-permute-start.17 = (f32[64,512]{1,0:T(8,128)S(1)}, f32[64,512]{1,0:T(8,128)S(1)}, u32[]{:S(2)}, u32[]{:S(2)}) collective-permute-start(f32[64,512]{1,0:T(8,128)S(1)} %concatenate.29.refs_2_), channel_id=1, source_target_pairs={{1,0},{2,1},{3,2},{4,3},{5,4},{6,5},{7,6},{0,7},{9,8},{10,9},{11,1... | collective-permute-start | bytes 393224 | tf_op jit(solution)/shard_map/ppermute | solution.py:819
  55.1 5.5 %collective-permute-start.18 = (f32[11,2,24,128]{3,2,1,0:T(8,128)S(1)}, f32[11,2,24,128]{3,2,1,0:T(8,128)S(1)}, u32[]{:S(2)}, u32[]{:S(2)}) collective-permute-start(f32[11,2,24,128]{3,2,1,0:T(8,128)S(1)} %get-tuple-element.59), channel_id=1, source_target_pairs={{0,1},{1,2},{2,3},{3,4},{4,5},{5,6},{6,7},{7,0},{8,9},{9,10},{10,1... | collective-permute-start | bytes 811016 | tf_op jit(solution)/shard_map/ppermute | solution.py:819
  57.2 6.2 %collective-permute-start.19 = (f32[11,2,24,128]{3,2,1,0:T(8,128)S(1)}, f32[11,2,24,128]{3,2,1,0:T(8,128)S(1)}, u32[]{:S(2)}, u32[]{:S(2)}) collective-permute-start(f32[11,2,24,128]{3,2,1,0:T(8,128)S(1)} %get-tuple-element.60), channel_id=1, source_target_pairs={{1,0},{2,1},{3,2},{4,3},{5,4},{6,5},{7,6},{0,7},{9,8},{10,9},{11,1... | collective-permute-start | bytes 811016 | tf_op jit(solution)/shard_map/ppermute | solution.py:819
  67.8 17.4 %all-to-all-start = ((f32[128,4,128]{2,1,0:T(4,128)}), f32[128,4,128]{2,1,0:T(4,128)S(1)}, u32[]{:S(2)}, u32[]{:S(2)}) async-start(f32[128,4,128]{2,1,0:T(4,128)} %bitcast), calls=%async_computation | async-start | bytes 524288 | tf_op jit(solution)/shard_map/all_to_all | solution.py:889
  96.2 4.4 %collective-permute-start.20 = (f32[8,16,128]{2,1,0:T(8,128)S(1)}, f32[8,16,128]{2,1,0:T(8,128)S(1)}, u32[]{:S(2)}, u32[]{:S(2)}) collective-permute-start(f32[8,16,128]{2,1,0:T(8,128)S(1)} %get-tuple-element.64), channel_id=1, source_target_pairs={{0,32},{32,64},{64,96},{96,0},{1,33},{33,65},{65,97},{97,1},{2,34}... | collective-permute-start | bytes 196616 | tf_op jit(solution)/shard_map/ppermute | solution.py:819
  96.6 4.0 %collective-permute-start.21 = (f32[8,16,128]{2,1,0:T(8,128)S(1)}, f32[8,16,128]{2,1,0:T(8,128)S(1)}, u32[]{:S(2)}, u32[]{:S(2)}) collective-permute-start(f32[8,16,128]{2,1,0:T(8,128)S(1)} %get-tuple-element.64), channel_id=1, source_target_pairs={{32,0},{64,32},{96,64},{0,96},{33,1},{65,33},{97,65},{1,97},{34,2}... | collective-permute-start | bytes 196616 | tf_op jit(solution)/shard_map/ppermute | solution.py:819
  100.6 4.6 %collective-permute-start.23 = (f32[24,16,128]{2,1,0:T(8,128)S(1)}, f32[24,16,128]{2,1,0:T(8,128)S(1)}, u32[]{:S(2)}, u32[]{:S(2)}) collective-permute-start(f32[24,16,128]{2,1,0:T(8,128)S(1)} %constant_dynamic-update-slice_fusion.3.refs_0_), channel_id=1, source_target_pairs={{8,0},{16,8},{24,16},{0,24},{9,1},{17,9},{25,17},{1,25},{10,2},{18... | collective-permute-start | bytes 589832 | tf_op jit(solution)/shard_map/ppermute | solution.py:819
  101.9 5.7 %collective-permute-start.22 = (f32[24,16,128]{2,1,0:T(8,128)S(1)}, f32[24,16,128]{2,1,0:T(8,128)S(1)}, u32[]{:S(2)}, u32[]{:S(2)}) collective-permute-start(f32[24,16,128]{2,1,0:T(8,128)S(1)} %constant_dynamic-update-slice_fusion.3.refs_0_), channel_id=1, source_target_pairs={{0,8},{8,16},{16,24},{24,0},{1,9},{9,17},{17,25},{25,1},{2,10},{10... | collective-permute-start | bytes 589832 | tf_op jit(solution)/shard_map/ppermute | solution.py:819
  108.0 5.6 %collective-permute-start.24 = (f32[6,2,24,128]{3,2,1,0:T(8,128)S(1)}, f32[6,2,24,128]{3,2,1,0:T(8,128)S(1)}, u32[]{:S(2)}, u32[]{:S(2)}) collective-permute-start(f32[6,2,24,128]{3,2,1,0:T(8,128)S(1)} %get-tuple-element.66), channel_id=1, source_target_pairs={{0,1},{1,2},{2,3},{3,4},{4,5},{5,6},{6,7},{7,0},{8,9},{9,10},{10,1... | collective-permute-start | bytes 442376 | tf_op jit(solution)/shard_map/ppermute | solution.py:819
  111.5 4.9 %collective-permute-start.25 = (f32[6,2,24,128]{3,2,1,0:T(8,128)S(1)}, f32[6,2,24,128]{3,2,1,0:T(8,128)S(1)}, u32[]{:S(2)}, u32[]{:S(2)}) collective-permute-start(f32[6,2,24,128]{3,2,1,0:T(8,128)S(1)} %get-tuple-element.67), channel_id=1, source_target_pairs={{1,0},{2,1},{3,2},{4,3},{5,4},{6,5},{7,6},{0,7},{9,8},{10,9},{11,1... | collective-permute-start | bytes 442376 | tf_op jit(solution)/shard_map/ppermute | solution.py:819
  147.3 13.9 %all-to-all-start.2 = ((f32[128,1,128]{2,1,0:T(1,128)}), f32[128,1,128]{2,1,0:T(1,128)S(1)}, u32[]{:S(2)}, u32[]{:S(2)}) async-start(f32[128,1,128]{2,1,0:T(1,128)} %bitcast.8), calls=%async_computation.2 | async-start | bytes 131072 | tf_op jit(solution)/shard_map/all_to_all | solution.py:930
  (10 other events, 94.3 us)

commit v8 on v7

--- a/solution.py
+++ b/solution.py
@@ -585,13 +585,13 @@
         spread = jnp.where(sub // 2 == lane // 32, pick(pairs, 2 * (lane % 32)), 0.0)
         rows.append(0.5 * jnp.sum(spread, axis=0, keepdims=True))
     vector = jnp.broadcast_to(jnp.concatenate(rows, axis=1), (8, 512))
-    answer = lax.dot_general(
-        vector,
-        jnp.concatenate([ref[...] for ref in inverse] + [jnp.zeros((64, 512), F32)], axis=0),
-        (((1,), (1,)), ((), ())),
-        precision=lax.Precision.HIGHEST,
-        preferred_element_type=F32,
-    )
+    rows = jnp.concatenate([ref[...] for ref in inverse] + [jnp.zeros((64, 512), F32)], axis=0)
+    (low, high), (rows_low, rows_high) = halves(vector), halves(rows)
+    answer = jnp.zeros((8, 256), F32)
+    for left, right in ((low, rows_high), (high, rows_low), (high, rows_high)):
+        answer = answer + lax.dot_general(
+            left, right, (((1,), (1,)), ((), ())), preferred_element_type=F32
+        )
     planes = []
     for x5 in range(4):
         z5 = lane % 64 // 2

time: 162 us -> 162 us (level)
  no operation moved by 1% of the time
where the time goes in v8:
time: 162 us
  waiting for transfers between devices  52.1 us (32%)
  starting transfers between devices  45.3 us (28%)
  Pallas kernels  44.2 us (27%)
  blocking collectives  16.8 us (10%)
    pallas_call x11, Pallas kernels, call(): pl.pallas_call(kernel, out_shape=[jax.ShapeDtypeStruct(shape, F32) for sh...  44.2 us
    ppermute x20, waiting for transfers between devices, exchange(): return (lax.ppermute(to_high, axis, up), lax.ppermute(to_low, axis, down))  35.8 us
    ppermute x20, starting transfers between devices, exchange(): return (lax.ppermute(to_high, axis, up), lax.ppermute(to_low, axis, down))  28.2 us
    all_to_all x1, blocking collectives, local(): message = lax.all_to_all(message, AXES, 0, 0, tiled=True)  16.8 us
    all_to_all x1, waiting for transfers between devices, local(): sums = lax.all_to_all(sums, AXES, 0, 0, tiled=True)  6.85 us
    all_to_all x1, starting transfers between devices, local(): message = lax.all_to_all(message, AXES, 0, 0, tiled=True)  6.57 us
    ppermute x6, starting transfers between devices, from_all(): return [lax.ppermute(own, axis, shift) for shift in shifts]  6.12 us
    ppermute x6, waiting for transfers between devices, from_all(): return [lax.ppermute(own, axis, shift) for shift in shifts]  4.97 us
  transfers between devices with their start and end apart: 28, of which 21 were waited for; matrix products, arithmetic and copies ran while one was open for 0% of the time, Pallas kernels for 6%

profile of v8, /device:TPU:1, one launch (start us, length us, event | category | flops | bytes accessed | tf_op | source)
XLA Modules:
  0.0 161.7 jit_solution(14531877983870931777)
XLA Ops:
  5.7 2.5 %collective-permute-start.4 = (f32[4,512]{1,0:T(4,128)S(1)}, f32[4,512]{1,0:T(4,128)S(1)}, u32[]{:S(2)}, u32[]{:S(2)}) collective-permute-start(f32[4,512]{1,0:T(4,128)S(1)} %copy-done.5), channel_id=1, source_target_pairs={{0,24},{8,0},{16,8},{24,16},{1,25},{9,1},{17,9},{25,17},{2,26},{10... | collective-permute-start | bytes 24584 | tf_op jit(solution)/shard_map/ppermute | solution.py:825
  17.9 3.3 %collective-permute-done.8 = f32[16,512]{1,0:T(8,128)S(1)} collective-permute-done((f32[16,512]{1,0:T(8,128)S(1)}, f32[16,512]{1,0:T(8,128)S(1)}, u32[]{:S(2)}, u32[]{:S(2)}) %collective-permute-start.8) | collective-permute-done | bytes 32800 | tf_op jit(solution)/shard_map/ppermute | solution.py:825
  22.9 6.0 %collective-permute-start.10 = (f32[6,48,128]{2,1,0:T(8,128)S(1)}, f32[6,48,128]{2,1,0:T(8,128)S(1)}, u32[]{:S(2)}, u32[]{:S(2)}) collective-permute-start(f32[6,48,128]{2,1,0:T(8,128)S(1)} %get-tuple-element.51), channel_id=1, source_target_pairs={{0,1},{1,2},{2,3},{3,4},{4,5},{5,6},{6,7},{7,0},{8,9},{9,10},{10,1... | collective-permute-start | bytes 442376 | tf_op jit(solution)/shard_map/ppermute | solution.py:819
  33.4 3.9 %shard_map.79 = (f32[16,16,128]{2,1,0:T(8,128)S(1)}, f32[56,48,2,24,128]{4,3,2,1,0:T(8,128)}) custom-call(f32[96,48,128]{2,1,0:T(8,128)S(1)} %get-tuple-element.50.refs_0_, f32[6,48,128]{2,1,0:T(8,128)S(1)} %collective-permute-done.10.refs_1_, f32[6,48,128]{2,1,0:T(8,128)S(1)} %collective-permute-done.11.refs_2_, bf16[8,256,256]{2,1,0:T(8,128)(2,1)S(1)} %copy-done.3), custom_call_target="tpu_custom_call" | custom-call | tf_op jit(solution)/shard_map/pallas_call | solution.py:102
  37.5 2.7 %collective-permute-start.13 = (f32[14,16,128]{2,1,0:T(8,128)S(1)}, f32[14,16,128]{2,1,0:T(8,128)S(1)}, u32[]{:S(2)}, u32[]{:S(2)}) collective-permute-start(f32[14,16,128]{2,1,0:T(8,128)S(1)} %get-tuple-element.84), channel_id=1, source_target_pairs={{32,0},{64,32},{96,64},{0,96},{33,1},{65,33},{97,65},{1,97},{34,2}... | collective-permute-start | bytes 344072 | tf_op jit(solution)/shard_map/ppermute | solution.py:819
  40.1 3.5 %collective-permute-done.12 = f32[14,16,128]{2,1,0:T(8,128)S(1)} collective-permute-done((f32[14,16,128]{2,1,0:T(8,128)S(1)}, f32[14,16,128]{2,1,0:T(8,128)S(1)}, u32[]{:S(2)}, u32[]{:S(2)}) %collective-permute-start.12) | collective-permute-done | bytes 114720 | tf_op jit(solution)/shard_map/ppermute | solution.py:819
  47.1 2.9 %collective-permute-done.17.refs_4_ = f32[64,512]{1,0:T(8,128)S(1)} collective-permute-done((f32[64,512]{1,0:T(8,128)S(1)}, f32[64,512]{1,0:T(8,128)S(1)}, u32[]{:S(2)}, u32[]{:S(2)}) %collective-permute-start.17) | collective-permute-done | bytes 131104 | tf_op jit(solution)/shard_map/ppermute | solution.py:819
  50.0 3.2 %collective-permute-done.15 = f32[44,16,128]{2,1,0:T(8,128)S(1)} collective-permute-done((f32[44,16,128]{2,1,0:T(8,128)S(1)}, f32[44,16,128]{2,1,0:T(8,128)S(1)}, u32[]{:S(2)}, u32[]{:S(2)}) %collective-permute-start.15) | collective-permute-done | bytes 360480 | tf_op jit(solution)/shard_map/ppermute | solution.py:819
  57.2 3.4 %collective-permute-done.18.refs_1_ = f32[11,2,24,128]{3,2,1,0:T(8,128)S(1)} collective-permute-done((f32[11,2,24,128]{3,2,1,0:T(8,128)S(1)}, f32[11,2,24,128]{3,2,1,0:T(8,128)S(1)}, u32[]{:S(2)}, u32[]{:S(2)}) %collective-permute-start.18) | collective-permute-done | bytes 270368 | tf_op jit(solution)/shard_map/ppermute | solution.py:819
  60.6 2.8 %collective-permute-done.19.refs_2_ = f32[11,2,24,128]{3,2,1,0:T(8,128)S(1)} collective-permute-done((f32[11,2,24,128]{3,2,1,0:T(8,128)S(1)}, f32[11,2,24,128]{3,2,1,0:T(8,128)S(1)}, u32[]{:S(2)}, u32[]{:S(2)}) %collective-permute-start.19) | collective-permute-done | bytes 270368 | tf_op jit(solution)/shard_map/ppermute | solution.py:819
  63.4 4.5 %shard_map.81 = f32[512,128]{1,0:T(8,128)} custom-call(f32[44,2,24,128]{3,2,1,0:T(8,128)S(1)} %get-tuple-element.58.refs_0_, f32[11,2,24,128]{3,2,1,0:T(8,128)S(1)} %collective-permute-done.18.refs_1_, f32[11,2,24,128]{3,2,1,0:T(8,128)S(1)} %collective-permute-done.19.refs_2_, bf16[4,384,256]{2,1,0:T(8,128)(2,1)S(1)} %copy-done), custom_call_target="tpu_custom_call" | custom-call | tf_op jit(solution)/shard_map/pallas_call | solution.py:102
  67.8 6.6 %all-to-all-start = ((f32[128,4,128]{2,1,0:T(4,128)}), f32[128,4,128]{2,1,0:T(4,128)S(1)}, u32[]{:S(2)}, u32[]{:S(2)}) async-start(f32[128,4,128]{2,1,0:T(4,128)} %bitcast), calls=%async_computation | async-start | bytes 524288 | tf_op jit(solution)/shard_map/all_to_all | solution.py:889
  74.5 6.3 %shard_map.82.refs_5_.refs_4_.refs_6_ = f32[60,44,2,24,128]{4,3,2,1,0:T(8,128)} custom-call(f32[44,2,24,128]{3,2,1,0:T(8,128)S(1)} %get-tuple-element.58.refs_0_, f32[11,2,24,128]{3,2,1,0:T(8,128)S(1)} %collective-permute-done.18.refs_1_, f32[11,2,24,128]{3,2,1,0:T(8,128)S(1)} %collective-permute-done.19.refs_2_, bf16[4,384,256]{2,1,0:T(8,128)(2,1)S(1)} %copy-done), custom_call_target="tpu_custom_call" | custom-call | tf_op jit(solution)/shard_map/pallas_call | solution.py:102
  80.8 4.5 %all-to-all-done = f32[128,4,128]{2,1,0:T(4,128)S(1)} async-done(((f32[128,4,128]{2,1,0:T(4,128)}), f32[128,4,128]{2,1,0:T(4,128)S(1)}, u32[]{:S(2)}, u32[]{:S(2)}) %all-to-all-start) | async-done | bytes 262176 | tf_op jit(solution)/shard_map/all_to_all | solution.py:889
  85.3 10.7 %shard_map.83 = (f32[16,16,128]{2,1,0:T(8,128)S(1)}, f32[8,8,128]{2,1,0:T(8,128)S(1)}, f32[48,2,24,128]{3,2,1,0:T(8,128)S(1)}, f32[8,16,128]{2,1,0:T(8,128)S(1)}, f32[8,128]{1,0:T(8,128)S(1)}) custom-call(f32[512,128]{1,0:T(8,128)S(1)} %bitcast.10, s32[3]{0:T(128)S(1)} %pad_add_fusion.refs_1_, f32[64,512]{1,0:T(8,128)S(1)} %concatenate.29.refs_2_, ...), custom_call_target="tpu_custom_call" | custom-call | tf_op jit(solution)/shard_map/pallas_call | solution.py:102
  102.0 3.1 %collective-permute-done.23 = f32[24,16,128]{2,1,0:T(8,128)S(1)} collective-permute-done((f32[24,16,128]{2,1,0:T(8,128)S(1)}, f32[24,16,128]{2,1,0:T(8,128)S(1)}, u32[]{:S(2)}, u32[]{:S(2)}) %collective-permute-start.23) | collective-permute-done | bytes 196640 | tf_op jit(solution)/shard_map/ppermute | solution.py:819
  107.8 3.5 %collective-permute-start.24 = (f32[6,2,24,128]{3,2,1,0:T(8,128)S(1)}, f32[6,2,24,128]{3,2,1,0:T(8,128)S(1)}, u32[]{:S(2)}, u32[]{:S(2)}) collective-permute-start(f32[6,2,24,128]{3,2,1,0:T(8,128)S(1)} %get-tuple-element.66), channel_id=1, source_target_pairs={{0,1},{1,2},{2,3},{3,4},{4,5},{5,6},{6,7},{7,0},{8,9},{9,10},{10,1... | collective-permute-start | bytes 442376 | tf_op jit(solution)/shard_map/ppermute | solution.py:819
  113.4 2.8 %collective-permute-done.25.refs_2_ = f32[6,2,24,128]{3,2,1,0:T(8,128)S(1)} collective-permute-done((f32[6,2,24,128]{3,2,1,0:T(8,128)S(1)}, f32[6,2,24,128]{3,2,1,0:T(8,128)S(1)}, u32[]{:S(2)}, u32[]{:S(2)}) %collective-permute-start.25) | collective-permute-done | bytes 147488 | tf_op jit(solution)/shard_map/ppermute | solution.py:819
  116.2 5.0 %shard_map.85 = (f32[44,2,24,128]{3,2,1,0:T(8,128)S(1)}, f32[44,24,128]{2,1,0:T(8,128)S(1)}, f32[20,24,128]{2,1,0:T(8,128)S(1)}, f32[20,24,128]{2,1,0:T(8,128)S(1)}, f32[256,128]{1,0:T(8,128)S(1)}) custom-call(f32[24,2,24,128]{3,2,1,0:T(8,128)S(1)} %get-tuple-element.65.refs_0_, f32[6,2,24,128]{3,2,1,0:T(8,128)S(1)} %collective-permute-done.24.refs_1_, ...), custom_call_target="tpu_custom_call" | custom-call | tf_op jit(solution)/shard_map/pallas_call | solution.py:102
  121.2 16.8 %all_to_all.31 = f32[128,2,128]{2,1,0:T(2,128)S(1)} all-to-all(f32[128,2,128]{2,1,0:T(2,128)S(1)} %bitcast.12), channel_id=1, replica_groups=mesh['gx'=4,'gy'=4,'gz'=8] {'gx','gy','gz'}, dimensions={0} | all-to-all | bytes 262144 | tf_op jit(solution)/shard_map/all_to_all | solution.py:923
  138.0 8.9 %shard_map.86 = (f32[128,128]{1,0:T(8,128)}, f32[48,2,24,128]{3,2,1,0:T(8,128)S(1)}, f32[48,2,24,128]{3,2,1,0:T(8,128)S(1)}) custom-call(f32[256,128]{1,0:T(8,128)S(1)} %bitcast.11, s32[3]{0:T(128)S(1)} %pad_add_fusion.refs_1_, f32[64,512]{1,0:T(8,128)S(1)} %concatenate.29.refs_2_, f32[64,512]{1,0:T(8,128)S(1)} %collective-permute-done.16.refs_3_, ...), custom_call_target="tpu_custom_call" | custom-call | tf_op jit(solution)/shard_map/pallas_call | solution.py:102
  146.9 4.4 %all-to-all-start.2 = ((f32[128,1,128]{2,1,0:T(1,128)}), f32[128,1,128]{2,1,0:T(1,128)S(1)}, u32[]{:S(2)}, u32[]{:S(2)}) async-start(f32[128,1,128]{2,1,0:T(1,128)} %bitcast.8), calls=%async_computation.2 | async-start | bytes 131072 | tf_op jit(solution)/shard_map/all_to_all | solution.py:930
  151.3 2.7 %shard_map.87 = f32[32,32,128]{2,1,0:T(8,128)} custom-call(f32[48,2,24,128]{3,2,1,0:T(8,128)S(1)} %get-tuple-element.77.refs_0_, f32[48,2,24,128]{3,2,1,0:T(8,128)S(1)} %get-tuple-element.78.refs_1_, bf16[256,128]{1,0:T(8,128)(2,1)S(1)} %copy-done.4), custom_call_target="tpu_custom_call" | custom-call | tf_op jit(solution)/shard_map/pallas_call | solution.py:102
  154.0 6.9 %all-to-all-done.2 = f32[128,1,128]{2,1,0:T(1,128)S(1)} async-done(((f32[128,1,128]{2,1,0:T(1,128)}), f32[128,1,128]{2,1,0:T(1,128)S(1)}, u32[]{:S(2)}, u32[]{:S(2)}) %all-to-all-start.2) | async-done | bytes 65568 | tf_op jit(solution)/shard_map/all_to_all | solution.py:930
  (75 shorter events, 40.2 us)
Async XLA Ops:
  1.9 9.5 %collective-permute-start = (f32[16,32,128]{2,1,0:T(8,128)S(1)}, f32[16,32,128]{2,1,0:T(8,128)S(1)}, u32[]{:S(2)}, u32[]{:S(2)}) collective-permute-start(f32[16,32,128]{2,1,0:T(8,128)S(1)} %pad_maximum_fusion.2), channel_id=1, source_target_pairs={{0,32},{32,64},{64,96},{96,0},{1,33},{33,65},{65,97},{97,1},{2,34}... | collective-permute-start | bytes 786440 | tf_op jit(solution)/shard_map/ppermute | solution.py:819
  4.1 7.3 %collective-permute-start.1 = (f32[16,32,128]{2,1,0:T(8,128)S(1)}, f32[16,32,128]{2,1,0:T(8,128)S(1)}, u32[]{:S(2)}, u32[]{:S(2)}) collective-permute-start(f32[16,32,128]{2,1,0:T(8,128)S(1)} %pad_maximum_fusion.3), channel_id=1, source_target_pairs={{32,0},{64,32},{96,64},{0,96},{33,1},{65,33},{97,65},{1,97},{34,2}... | collective-permute-start | bytes 786440 | tf_op jit(solution)/shard_map/ppermute | solution.py:819
  5.7 5.9 %collective-permute-start.4 = (f32[4,512]{1,0:T(4,128)S(1)}, f32[4,512]{1,0:T(4,128)S(1)}, u32[]{:S(2)}, u32[]{:S(2)}) collective-permute-start(f32[4,512]{1,0:T(4,128)S(1)} %copy-done.5), channel_id=1, source_target_pairs={{0,24},{8,0},{16,8},{24,16},{1,25},{9,1},{17,9},{25,17},{2,26},{10... | collective-permute-start | bytes 24584 | tf_op jit(solution)/shard_map/ppermute | solution.py:825
  12.4 9.3 %collective-permute-start.5 = (f32[80,8,128]{2,1,0:T(8,128)S(1)}, f32[80,8,128]{2,1,0:T(8,128)S(1)}, u32[]{:S(2)}, u32[]{:S(2)}) collective-permute-start(f32[80,8,128]{2,1,0:T(8,128)S(1)} %get-tuple-element.43), channel_id=1, source_target_pairs={{0,8},{8,16},{16,24},{24,0},{1,9},{9,17},{17,25},{25,1},{2,10},{10... | collective-permute-start | bytes 983048 | tf_op jit(solution)/shard_map/ppermute | solution.py:819
  12.7 9.0 %collective-permute-start.6 = (f32[80,8,128]{2,1,0:T(8,128)S(1)}, f32[80,8,128]{2,1,0:T(8,128)S(1)}, u32[]{:S(2)}, u32[]{:S(2)}) collective-permute-start(f32[80,8,128]{2,1,0:T(8,128)S(1)} %get-tuple-element.44), channel_id=1, source_target_pairs={{8,0},{16,8},{24,16},{0,24},{9,1},{17,9},{25,17},{1,25},{10,2},{18... | collective-permute-start | bytes 983048 | tf_op jit(solution)/shard_map/ppermute | solution.py:819
  16.9 4.4 %collective-permute-start.8 = (f32[16,512]{1,0:T(8,128)S(1)}, f32[16,512]{1,0:T(8,128)S(1)}, u32[]{:S(2)}, u32[]{:S(2)}) collective-permute-start(f32[16,512]{1,0:T(8,128)S(1)} %pad_maximum_fusion.4), channel_id=1, source_target_pairs={{0,64},{32,96},{64,0},{96,32},{1,65},{33,97},{65,1},{97,33},{2,66}... | collective-permute-start | bytes 98312 | tf_op jit(solution)/shard_map/ppermute | solution.py:825
  17.1 4.6 %collective-permute-start.7 = (f32[16,512]{1,0:T(8,128)S(1)}, f32[16,512]{1,0:T(8,128)S(1)}, u32[]{:S(2)}, u32[]{:S(2)}) collective-permute-start(f32[16,512]{1,0:T(8,128)S(1)} %pad_maximum_fusion.4), channel_id=1, source_target_pairs={{0,32},{32,64},{64,96},{96,0},{1,33},{33,65},{65,97},{97,1},{2,34}... | collective-permute-start | bytes 98312 | tf_op jit(solution)/shard_map/ppermute | solution.py:825
  22.9 8.1 %collective-permute-start.10 = (f32[6,48,128]{2,1,0:T(8,128)S(1)}, f32[6,48,128]{2,1,0:T(8,128)S(1)}, u32[]{:S(2)}, u32[]{:S(2)}) collective-permute-start(f32[6,48,128]{2,1,0:T(8,128)S(1)} %get-tuple-element.51), channel_id=1, source_target_pairs={{0,1},{1,2},{2,3},{3,4},{4,5},{5,6},{6,7},{7,0},{8,9},{9,10},{10,1... | collective-permute-start | bytes 442376 | tf_op jit(solution)/shard_map/ppermute | solution.py:819
  28.8 4.6 %collective-permute-start.11 = (f32[6,48,128]{2,1,0:T(8,128)S(1)}, f32[6,48,128]{2,1,0:T(8,128)S(1)}, u32[]{:S(2)}, u32[]{:S(2)}) collective-permute-start(f32[6,48,128]{2,1,0:T(8,128)S(1)} %get-tuple-element.52), channel_id=1, source_target_pairs={{1,0},{2,1},{3,2},{4,3},{5,4},{6,5},{7,6},{0,7},{9,8},{10,9},{11,1... | collective-permute-start | bytes 442376 | tf_op jit(solution)/shard_map/ppermute | solution.py:819
  37.4 6.3 %collective-permute-start.12 = (f32[14,16,128]{2,1,0:T(8,128)S(1)}, f32[14,16,128]{2,1,0:T(8,128)S(1)}, u32[]{:S(2)}, u32[]{:S(2)}) collective-permute-start(f32[14,16,128]{2,1,0:T(8,128)S(1)} %get-tuple-element.85), channel_id=1, source_target_pairs={{0,32},{32,64},{64,96},{96,0},{1,33},{33,65},{65,97},{97,1},{2,34}... | collective-permute-start | bytes 344072 | tf_op jit(solution)/shard_map/ppermute | solution.py:819
  37.5 6.2 %collective-permute-start.13 = (f32[14,16,128]{2,1,0:T(8,128)S(1)}, f32[14,16,128]{2,1,0:T(8,128)S(1)}, u32[]{:S(2)}, u32[]{:S(2)}) collective-permute-start(f32[14,16,128]{2,1,0:T(8,128)S(1)} %get-tuple-element.84), channel_id=1, source_target_pairs={{32,0},{64,32},{96,64},{0,96},{33,1},{65,33},{97,65},{1,97},{34,2}... | collective-permute-start | bytes 344072 | tf_op jit(solution)/shard_map/ppermute | solution.py:819
  43.7 9.5 %collective-permute-start.15 = (f32[44,16,128]{2,1,0:T(8,128)S(1)}, f32[44,16,128]{2,1,0:T(8,128)S(1)}, u32[]{:S(2)}, u32[]{:S(2)}) collective-permute-start(f32[44,16,128]{2,1,0:T(8,128)S(1)} %constant_dynamic-update-slice_fusion.refs_0_), channel_id=1, source_target_pairs={{8,0},{16,8},{24,16},{0,24},{9,1},{17,9},{25,17},{1,25},{10,2},{18... | collective-permute-start | bytes 1081352 | tf_op jit(solution)/shard_map/ppermute | solution.py:819
  44.1 10.3 %collective-permute-start.14 = (f32[44,16,128]{2,1,0:T(8,128)S(1)}, f32[44,16,128]{2,1,0:T(8,128)S(1)}, u32[]{:S(2)}, u32[]{:S(2)}) collective-permute-start(f32[44,16,128]{2,1,0:T(8,128)S(1)} %constant_dynamic-update-slice_fusion.refs_0_), channel_id=1, source_target_pairs={{0,8},{8,16},{16,24},{24,0},{1,9},{9,17},{17,25},{25,1},{2,10},{10... | collective-permute-start | bytes 1081352 | tf_op jit(solution)/shard_map/ppermute | solution.py:819
  45.3 4.7 %collective-permute-start.17 = (f32[64,512]{1,0:T(8,128)S(1)}, f32[64,512]{1,0:T(8,128)S(1)}, u32[]{:S(2)}, u32[]{:S(2)}) collective-permute-start(f32[64,512]{1,0:T(8,128)S(1)} %concatenate.29.refs_2_), channel_id=1, source_target_pairs={{1,0},{2,1},{3,2},{4,3},{5,4},{6,5},{7,6},{0,7},{9,8},{10,9},{11,1... | collective-permute-start | bytes 393224 | tf_op jit(solution)/shard_map/ppermute | solution.py:819
  55.1 5.5 %collective-permute-start.18 = (f32[11,2,24,128]{3,2,1,0:T(8,128)S(1)}, f32[11,2,24,128]{3,2,1,0:T(8,128)S(1)}, u32[]{:S(2)}, u32[]{:S(2)}) collective-permute-start(f32[11,2,24,128]{3,2,1,0:T(8,128)S(1)} %get-tuple-element.59), channel_id=1, source_target_pairs={{0,1},{1,2},{2,3},{3,4},{4,5},{5,6},{6,7},{7,0},{8,9},{9,10},{10,1... | collective-permute-start | bytes 811016 | tf_op jit(solution)/shard_map/ppermute | solution.py:819
  57.2 6.2 %collective-permute-start.19 = (f32[11,2,24,128]{3,2,1,0:T(8,128)S(1)}, f32[11,2,24,128]{3,2,1,0:T(8,128)S(1)}, u32[]{:S(2)}, u32[]{:S(2)}) collective-permute-start(f32[11,2,24,128]{3,2,1,0:T(8,128)S(1)} %get-tuple-element.60), channel_id=1, source_target_pairs={{1,0},{2,1},{3,2},{4,3},{5,4},{6,5},{7,6},{0,7},{9,8},{10,9},{11,1... | collective-permute-start | bytes 811016 | tf_op jit(solution)/shard_map/ppermute | solution.py:819
  67.8 17.4 %all-to-all-start = ((f32[128,4,128]{2,1,0:T(4,128)}), f32[128,4,128]{2,1,0:T(4,128)S(1)}, u32[]{:S(2)}, u32[]{:S(2)}) async-start(f32[128,4,128]{2,1,0:T(4,128)} %bitcast), calls=%async_computation | async-start | bytes 524288 | tf_op jit(solution)/shard_map/all_to_all | solution.py:889
  96.0 4.4 %collective-permute-start.20 = (f32[8,16,128]{2,1,0:T(8,128)S(1)}, f32[8,16,128]{2,1,0:T(8,128)S(1)}, u32[]{:S(2)}, u32[]{:S(2)}) collective-permute-start(f32[8,16,128]{2,1,0:T(8,128)S(1)} %get-tuple-element.64), channel_id=1, source_target_pairs={{0,32},{32,64},{64,96},{96,0},{1,33},{33,65},{65,97},{97,1},{2,34}... | collective-permute-start | bytes 196616 | tf_op jit(solution)/shard_map/ppermute | solution.py:819
  96.4 4.0 %collective-permute-start.21 = (f32[8,16,128]{2,1,0:T(8,128)S(1)}, f32[8,16,128]{2,1,0:T(8,128)S(1)}, u32[]{:S(2)}, u32[]{:S(2)}) collective-permute-start(f32[8,16,128]{2,1,0:T(8,128)S(1)} %get-tuple-element.64), channel_id=1, source_target_pairs={{32,0},{64,32},{96,64},{0,96},{33,1},{65,33},{97,65},{1,97},{34,2}... | collective-permute-start | bytes 196616 | tf_op jit(solution)/shard_map/ppermute | solution.py:819
  100.4 4.6 %collective-permute-start.23 = (f32[24,16,128]{2,1,0:T(8,128)S(1)}, f32[24,16,128]{2,1,0:T(8,128)S(1)}, u32[]{:S(2)}, u32[]{:S(2)}) collective-permute-start(f32[24,16,128]{2,1,0:T(8,128)S(1)} %constant_dynamic-update-slice_fusion.3.refs_0_), channel_id=1, source_target_pairs={{8,0},{16,8},{24,16},{0,24},{9,1},{17,9},{25,17},{1,25},{10,2},{18... | collective-permute-start | bytes 589832 | tf_op jit(solution)/shard_map/ppermute | solution.py:819
  101.7 5.7 %collective-permute-start.22 = (f32[24,16,128]{2,1,0:T(8,128)S(1)}, f32[24,16,128]{2,1,0:T(8,128)S(1)}, u32[]{:S(2)}, u32[]{:S(2)}) collective-permute-start(f32[24,16,128]{2,1,0:T(8,128)S(1)} %constant_dynamic-update-slice_fusion.3.refs_0_), channel_id=1, source_target_pairs={{0,8},{8,16},{16,24},{24,0},{1,9},{9,17},{17,25},{25,1},{2,10},{10... | collective-permute-start | bytes 589832 | tf_op jit(solution)/shard_map/ppermute | solution.py:819
  107.8 5.6 %collective-permute-start.24 = (f32[6,2,24,128]{3,2,1,0:T(8,128)S(1)}, f32[6,2,24,128]{3,2,1,0:T(8,128)S(1)}, u32[]{:S(2)}, u32[]{:S(2)}) collective-permute-start(f32[6,2,24,128]{3,2,1,0:T(8,128)S(1)} %get-tuple-element.66), channel_id=1, source_target_pairs={{0,1},{1,2},{2,3},{3,4},{4,5},{5,6},{6,7},{7,0},{8,9},{9,10},{10,1... | collective-permute-start | bytes 442376 | tf_op jit(solution)/shard_map/ppermute | solution.py:819
  111.3 4.9 %collective-permute-start.25 = (f32[6,2,24,128]{3,2,1,0:T(8,128)S(1)}, f32[6,2,24,128]{3,2,1,0:T(8,128)S(1)}, u32[]{:S(2)}, u32[]{:S(2)}) collective-permute-start(f32[6,2,24,128]{3,2,1,0:T(8,128)S(1)} %get-tuple-element.67), channel_id=1, source_target_pairs={{1,0},{2,1},{3,2},{4,3},{5,4},{6,5},{7,6},{0,7},{9,8},{10,9},{11,1... | collective-permute-start | bytes 442376 | tf_op jit(solution)/shard_map/ppermute | solution.py:819
  146.9 13.9 %all-to-all-start.2 = ((f32[128,1,128]{2,1,0:T(1,128)}), f32[128,1,128]{2,1,0:T(1,128)S(1)}, u32[]{:S(2)}, u32[]{:S(2)}) async-start(f32[128,1,128]{2,1,0:T(1,128)} %bitcast.8), calls=%async_computation.2 | async-start | bytes 131072 | tf_op jit(solution)/shard_map/all_to_all | solution.py:930
  (10 other events, 94.0 us)
